TPU v7x, 32 devices: a whole 2x2x4 slice. The times are simulated.
32 devices in a mesh: groups: 2 (over x), replica: 8 (over z, y), tensor: 2 (over core).
Axes of the slice: x: 2, y: 2, z: 4, core: 2. Of those that a mesh axis runs over, the one named last changes fastest.
Arguments:
- queries: bfloat16 [512, 8192], P(('groups', 'replica'), 'tensor'), parts along dimension 0, may hold values from -32 to 32
- fresh_key_rows: bfloat16 [512, 1024], P(('groups', 'replica'), 'tensor'), parts along dimension 0, may hold values from -8 to 8
- fresh_value_rows: bfloat16 [512, 1024], P(('groups', 'replica'), 'tensor'), parts along dimension 0, may hold values from -6 to 6
- paged_key_store: bfloat16 [2048, 16, 1024], P(('groups', 'replica'), None, 'tensor'), parts along dimension 0, may hold values from -8 to 8
- paged_value_store: bfloat16 [2048, 16, 1024], P(('groups', 'replica'), None, 'tensor'), parts along dimension 0, may hold values from -6 to 6
- page_table: int32 [512, 4], P(('groups', 'replica')), parts along dimension 0, may hold values from 0 to 127, as said below
- parent_replica: int32 [512, 1], P(('groups', 'replica')), parts along dimension 0, may hold values from 0 to 7; in each aligned block of 32 rows (0 to 31, 32 to 63, ...) at most 8 rows name the same one
- parent_slot: int32 [512, 1], P(('groups', 'replica')), parts along dimension 0, may hold values from 0 to 31
- context_length: int32 [512], P(('groups', 'replica')), parts along dimension 0, may hold values from 1 to 64, 4096 in all
- reward_probe: bfloat16 [8192], P('tensor'), may hold values from -0.0625 to 0.0625
Outputs:
- attended: bfloat16 [512, 8192], P(('groups', 'replica'), 'tensor'), parts along dimension 0
- reward: float32 [512], P(('groups', 'replica')), parts along dimension 0
There are 2 independent parts, one for each index of `groups`. A program takes and returns all parts, laid end to end along the dimension named above; an argument that names none is the same for every part. Nothing has to cross between parts.
Inputs may be any that keep to these rules, and one draw needn't show every extreme that they name: `parent_replica`: within the rows of one replica no replica is named more than 8 times. `page_table`: the rows of one replica together name each of its 128 pool pages once.
All inputs are finite; a program needn't handle non-finite values. No bound on the sum of `context_length` on one device may be relied on, other than what follows from the above.
Results may differ from a plain program's by a relative error of at most 0.0033.
Values may be sent and summed in bfloat16 or wider, within the bound.
No kernel may reach another device: no remote copies, remote signals or barrier semaphores. Data moves between devices by JAX's collectives and lax.ppermute only.
A program may use at most 64 MiB of HBM per device.

v0:
```python
import jax
import jax.numpy as jnp
from jax import lax
from jax.sharding import PartitionSpec as P

HEAD_SIZE = 128


masked_score = -1e30


def attend(query_rows, own_key, own_value, cached_key_rows, cached_value_rows, lengths):
    batch = query_rows.shape[0]
    key_span = cached_key_rows.shape[1]
    key_heads = own_key.shape[-1] // HEAD_SIZE
    group_size = query_rows.shape[-1] // own_key.shape[-1]
    scaling = 1.0 / HEAD_SIZE**0.5
    query_four = query_rows.reshape(batch, key_heads, group_size, HEAD_SIZE)
    keys_four = cached_key_rows.reshape(batch, key_span, key_heads, HEAD_SIZE)
    values_four = cached_value_rows.reshape(batch, key_span, key_heads, HEAD_SIZE)
    own_keys = own_key.reshape(batch, key_heads, HEAD_SIZE)
    own_values = own_value.reshape(batch, key_heads, HEAD_SIZE).astype(jnp.float32)
    scores = (
        jnp.einsum("bgqd,btgd->bgqt", query_four, keys_four, preferred_element_type=jnp.float32)
        * scaling
    )
    own_score = (
        jnp.einsum("bgqd,bgd->bgq", query_four, own_keys, preferred_element_type=jnp.float32)
        * scaling
    )
    visible = (jnp.arange(key_span, dtype=jnp.int32)[None, :] < lengths[:, None])[:, None, None, :]
    scores = jnp.where(visible, scores, masked_score)
    peak = jnp.maximum(jnp.max(scores, axis=-1), own_score)
    weights = jnp.where(visible, jnp.exp(scores - peak[..., None]), 0.0)
    own_weight = jnp.exp(own_score - peak)
    denominator = jnp.sum(weights, axis=-1) + own_weight
    rounded = weights.astype(jnp.bfloat16)
    own_rounded = own_weight.astype(jnp.bfloat16).astype(jnp.float32)
    numerator = jnp.einsum(
        "bgqt,btgd->bgqd", rounded, values_four, preferred_element_type=jnp.float32
    )
    numerator = numerator + own_rounded[..., None] * own_values[:, :, None, :]
    final_output = numerator / denominator[..., None]
    return final_output.reshape(batch, -1).astype(jnp.bfloat16)


def to_slots(selector, rows):
    return jnp.dot(selector, rows, preferred_element_type=jnp.float32).astype(jnp.bfloat16)


def shards(
    queries,
    fresh_key_rows,
    fresh_value_rows,
    paged_key_store,
    paged_value_store,
    page_table,
    parent_replica,
    parent_slot,
    context_length,
    reward_probe,
):
    replicas = lax.axis_size("replica")
    row_count = queries.shape[0]
    capacity = max(2, 2 * row_count // replicas)
    slot_count = replicas * capacity
    span_total = page_table.shape[1] * paged_key_store.shape[1]
    feature_width = paged_key_store.shape[2]
    source = parent_replica[:, 0]
    parent_row = parent_slot[:, 0]
    indices = jnp.arange(row_count, dtype=jnp.int32)
    earlier = (source[:, None] == source[None, :]) & (indices[:, None] < indices[None, :])
    slot_rank = jnp.sum(earlier.astype(jnp.int32), axis=0)
    position = source * capacity + slot_rank
    slot_match = jnp.arange(slot_count, dtype=jnp.int32)[:, None] == position[None, :]
    selector = slot_match.astype(jnp.bfloat16)
    asked_rows = jnp.sum(jnp.where(slot_match, parent_row[None, :], 0), axis=1).reshape(
        replicas, capacity
    )
    slot_lengths = jnp.sum(jnp.where(slot_match, context_length[None, :], 0), axis=1)
    slot_queries = to_slots(selector, queries)
    slot_keys = to_slots(selector, fresh_key_rows)
    slot_values = to_slots(selector, fresh_value_rows)
    asked_lengths = slot_lengths.reshape(replicas, capacity)
    wanted, wanted_lengths = (
        lax.all_to_all(asked_rows, "replica", split_axis=0, concat_axis=0, tiled=True),
        lax.all_to_all(asked_lengths, "replica", split_axis=0, concat_axis=0, tiled=True),
    )
    query_slots = slot_queries.reshape(replicas, capacity, -1)
    key_slots = slot_keys.reshape(replicas, capacity, -1)
    value_slots = slot_values.reshape(replicas, capacity, -1)
    query_in, key_in, value_in = (
        lax.all_to_all(query_slots, "replica", split_axis=0, concat_axis=0, tiled=True),
        lax.all_to_all(key_slots, "replica", split_axis=0, concat_axis=0, tiled=True),
        lax.all_to_all(value_slots, "replica", split_axis=0, concat_axis=0, tiled=True),
    )
    page_numbers = page_table[wanted.reshape(-1)]
    key_rows = paged_key_store[page_numbers].reshape(slot_count, span_total, feature_width)
    value_rows = paged_value_store[page_numbers].reshape(slot_count, span_total, feature_width)
    answers = attend(
        query_in.reshape(slot_count, -1),
        key_in.reshape(slot_count, -1),
        value_in.reshape(slot_count, -1),
        key_rows,
        value_rows,
        wanted_lengths.reshape(-1),
    )
    returned = lax.all_to_all(
        answers.reshape(replicas, capacity, -1), "replica", split_axis=0, concat_axis=0, tiled=True
    )
    slot_answers = returned.reshape(slot_count, -1)
    attended = jnp.dot(selector.T, slot_answers, preferred_element_type=jnp.float32).astype(
        jnp.bfloat16
    )
    partial_value = jnp.dot(attended, reward_probe, preferred_element_type=jnp.float32)
    reward = lax.psum(partial_value, "tensor")
    return (attended, reward)


def solution(mesh):
    placed = (
        P(("groups", "replica"), "tensor"),
        P(("groups", "replica"), "tensor"),
        P(("groups", "replica"), "tensor"),
        P(("groups", "replica"), None, "tensor"),
        P(("groups", "replica"), None, "tensor"),
        P(("groups", "replica"), None),
        P(("groups", "replica"), None),
        P(("groups", "replica"), None),
        P(("groups", "replica")),
        P("tensor"),
    )
    return jax.shard_map(
        shards,
        mesh=mesh,
        in_specs=placed,
        out_specs=(P(("groups", "replica"), "tensor"), P(("groups", "replica"))),
        check_vma=False,
    )
```

profile of v0, /device:TPU:0, one launch (start us, length us, event | category | flops | bytes accessed | tf_op | source)
XLA Modules:
  0.0 104.1 jit_solution(8324135944987451890)
XLA Ops:
  0.6 0.0 copy-start
  0.6 0.9 convert_reduce_fusion
  1.6 0.7 multiply_add_fusion
  2.2 0.8 select_reduce_fusion.1
  3.0 0.7 all_to_all.24
  3.7 7.3 %all-to-all-start = ((s32[8,1,8]{2,1,0:T(1,128)}), s32[8,1,8]{2,1,0:T(1,128)S(1)}, u32[]{:S(2)}, u32[]{:S(2)}) async-start(s32[8,1,8]{2,1,0:T(1,128)} %bitcast.1), calls=%async_computation | async-start | bytes 8192 | tf_op jit(solution)/shard_map/all_to_all | solution.py:87
  10.9 0.7 all_to_all.27
  11.6 5.7 %all-to-all-done = s32[8,1,8]{2,1,0:T(1,128)S(1)} async-done(((s32[8,1,8]{2,1,0:T(1,128)}), s32[8,1,8]{2,1,0:T(1,128)S(1)}, u32[]{:S(2)}, u32[]{:S(2)}) %all-to-all-start) | async-done | bytes 288 | tf_op jit(solution)/shard_map/all_to_all | solution.py:87
  17.3 3.3 %all-to-all-start.2 = ((s32[8,1,8]{2,1,0:T(1,128)}), s32[8,1,8]{2,1,0:T(1,128)S(1)}, u32[]{:S(2)}, u32[]{:S(2)}) async-start(s32[8,1,8]{2,1,0:T(1,128)} %bitcast.4), calls=%async_computation.2 | async-start | bytes 8192 | tf_op jit(solution)/shard_map/all_to_all | solution.py:86
  20.7 1.7 %fusion.14 = bf16[8,8,512]{2,1,0:T(8,128)(2,1)} fusion(bf16[32,512]{1,0:T(8,128)(2,1)} %param.11, s32[32]{0:T(128)S(1)} %multiply_add_fusion), kind=kOutput, calls=%fused_computation.15 | convolution fusion | flops 2131968 | bytes 98432 | tf_op jit(solution)/shard_map/dot_general | solution.py:48
  22.3 4.7 %all-to-all-done.2 = s32[8,1,8]{2,1,0:T(1,128)S(1)} async-done(((s32[8,1,8]{2,1,0:T(1,128)}), s32[8,1,8]{2,1,0:T(1,128)S(1)}, u32[]{:S(2)}, u32[]{:S(2)}) %all-to-all-start.2) | async-done | bytes 288 | tf_op jit(solution)/shard_map/all_to_all | solution.py:86
  27.1 3.4 %all-to-all-start.3 = ((bf16[8,8,512]{2,1,0:T(8,128)(2,1)}), bf16[8,8,512]{2,1,0:T(8,128)(2,1)S(1)}, u32[]{:S(2)}, u32[]{:S(2)}) async-start(bf16[8,8,512]{2,1,0:T(8,128)(2,1)} %fusion.14), calls=%async_computation.3 | async-start | bytes 131072 | tf_op jit(solution)/shard_map/all_to_all | solution.py:94
  30.4 1.7 %fusion.15 = bf16[8,8,512]{2,1,0:T(8,128)(2,1)} fusion(bf16[32,512]{1,0:T(8,128)(2,1)} %param.12, s32[32]{0:T(128)S(1)} %multiply_add_fusion), kind=kOutput, calls=%fused_computation.16 | convolution fusion | flops 2131968 | bytes 98432 | tf_op jit(solution)/shard_map/dot_general | solution.py:48
  32.1 5.2 %all-to-all-done.3 = bf16[8,8,512]{2,1,0:T(8,128)(2,1)S(1)} async-done(((bf16[8,8,512]{2,1,0:T(8,128)(2,1)}), bf16[8,8,512]{2,1,0:T(8,128)(2,1)S(1)}, u32[]{:S(2)}, u32[]{:S(2)}) %all-to-all-start.3) | async-done | bytes 65568 | tf_op jit(solution)/shard_map/all_to_all | solution.py:94
  37.3 3.3 %all-to-all-start.4 = ((bf16[8,8,512]{2,1,0:T(8,128)(2,1)}), bf16[8,8,512]{2,1,0:T(8,128)(2,1)S(1)}, u32[]{:S(2)}, u32[]{:S(2)}) async-start(bf16[8,8,512]{2,1,0:T(8,128)(2,1)} %fusion.15), calls=%async_computation.4 | async-start | bytes 131072 | tf_op jit(solution)/shard_map/all_to_all | solution.py:95
  40.6 2.2 %fusion = bf16[8,8,4096]{2,1,0:T(8,128)(2,1)} fusion(bf16[32,4096]{1,0:T(8,128)(2,1)} %param.10, s32[32]{0:T(128)S(1)} %multiply_add_fusion), kind=kOutput, calls=%fused_computation.4 | convolution fusion | flops 17041408 | bytes 786560 | tf_op jit(solution)/shard_map/dot_general | solution.py:48
  42.8 4.7 %all-to-all-done.4 = bf16[8,8,512]{2,1,0:T(8,128)(2,1)S(1)} async-done(((bf16[8,8,512]{2,1,0:T(8,128)(2,1)}), bf16[8,8,512]{2,1,0:T(8,128)(2,1)S(1)}, u32[]{:S(2)}, u32[]{:S(2)}) %all-to-all-start.4) | async-done | bytes 65568 | tf_op jit(solution)/shard_map/all_to_all | solution.py:95
  47.5 3.5 %all-to-all-start.1 = ((bf16[8,8,4096]{2,1,0:T(8,128)(2,1)}), bf16[8,8,4096]{2,1,0:T(8,128)(2,1)S(1)}, u32[]{:S(2)}, u32[]{:S(2)}) async-start(bf16[8,8,4096]{2,1,0:T(8,128)(2,1)} %fusion), calls=%async_computation.1 | async-start | bytes 1048576 | tf_op jit(solution)/shard_map/all_to_all | solution.py:93
  51.0 0.8 copy.25
  51.7 0.5 broadcast.70
  52.2 0.7 reduce.7
  52.9 0.1 lt.60
  53.0 0.7 reduce.6
  53.7 0.1 reshape.116
  53.8 0.6 gather_fusion
  54.4 0.1 reshape.131
  54.5 0.0 copy-done
  54.5 2.8 %gather_fusion.1 = bf16[256,16,512]{2,1,0:T(8,128)(2,1)} fusion(bf16[128,16,512]{2,1,0:T(8,128)(2,1)S(1)} %copy-done, s32[1024]{0:T(1024)S(1)} %pad_clamp_fusion), kind=kCustom, calls=%fused_computation.1 | custom fusion | bytes 8389632 | tf_op jit(solution)/shard_map/gather | solution.py:98
  57.3 6.9 %reshape_reshape.14 = bf16[64,64,4,128]{3,2,1,0:T(4,128)(2,1)} reshape(bf16[256,16,512]{2,1,0:T(8,128)(2,1)} %gather_fusion.1) | data formatting | bytes 8388608 | tf_op jit(solution)/shard_map/reshape;reshape | solution.py:19
  64.2 4.4 %gather_fusion.2 = bf16[256,16,512]{2,1,0:T(8,128)(2,1)} fusion(bf16[128,16,512]{2,1,0:T(8,128)(2,1)} %param.14, s32[1024]{0:T(1024)S(1)} %pad_clamp_fusion), kind=kCustom, calls=%fused_computation.2 | custom fusion | bytes 8389632 | tf_op jit(solution)/shard_map/gather | solution.py:99
  68.6 6.9 %reshape_reshape.16 = bf16[64,64,4,128]{3,2,1,0:T(4,128)(2,1)} reshape(bf16[256,16,512]{2,1,0:T(8,128)(2,1)} %gather_fusion.2) | data formatting | bytes 8388608 | tf_op jit(solution)/shard_map/reshape;reshape | solution.py:20
  75.5 0.1 iota_compare_fusion
  75.7 0.0 all-to-all-done.1
  75.7 0.1 copy.30
  75.8 0.4 fusion.38
  76.2 0.0 copy-start.1
  76.2 4.7 %fusion.37 = (f32[64,4,8]{2,1,0:T(4,128)S(1)}, f32[64,4,8,64]{3,2,1,0:T(8,128)S(1)}) fusion(bf16[64,4,8,128]{3,2,1,0:T(8,128)(2,1)S(1)} %bitcast.39, bf16[64,64,4,128]{3,2,1,0:T(4,128)(2,1)} %reshape_reshape.14, pred[64,64]{1,0:T(8,128)(4,1)S(1)} %iota_compare_fusion), kind=kOutput, calls=%fused_computation.49 | convolution fusion | flops 33945600 | bytes 5255168 | tf_op jit(solution)/shard_map/bgqd,btgd->bgqt/dot_general | solution.py:24
  81.0 0.8 fusion.22
  81.8 0.1 convert_convert_fusion
  81.9 0.0 copy-done.1
  81.9 0.0 copy-start.3
  81.9 1.5 %fusion.19 = bf16[64,4,8,128]{3,2,1,0:T(8,128)(2,1)S(1)} fusion(bf16[64,64,4,128]{3,2,1,0:T(4,128)(2,1)S(1)} %copy-done.1, f32[64,4,8,64]{3,2,1,0:T(8,128)S(1)} %get-tuple-element.7, f32[64,4,8]{2,1,0:T(4,128)S(1)} %get-tuple-element.5, f32[64,4,128]{2,1,0:T(4,128)S(1)} %reshape.120, f32[64,4,8]{2,1,0:T(4,128)S(1)} %get-tuple-element.4, ...), kind=kOutput, calls=%fused_computation.19 | convolution fusion | flops 34996224 | bytes 5402624 | tf_op jit(solution)/shard_map/bgqt,btgd->bgqd/dot_general | solution.py:39
  83.4 1.0 convert_element_type.52
  84.4 5.9 %all-to-all-start.5 = ((bf16[8,8,4096]{2,1,0:T(8,128)(2,1)}), bf16[8,8,4096]{2,1,0:T(8,128)(2,1)S(1)}, u32[]{:S(2)}, u32[]{:S(2)}) async-start(bf16[8,8,4096]{2,1,0:T(8,128)(2,1)} %convert_element_type.52), calls=%async_computation.5 | async-start | bytes 1048576 | tf_op jit(solution)/shard_map/all_to_all | solution.py:108
  90.3 0.0 copy-done.3
  90.4 10.3 %all-to-all-done.5 = bf16[8,8,4096]{2,1,0:T(8,128)(2,1)S(1)} async-done(((bf16[8,8,4096]{2,1,0:T(8,128)(2,1)}), bf16[8,8,4096]{2,1,0:T(8,128)(2,1)S(1)}, u32[]{:S(2)}, u32[]{:S(2)}) %all-to-all-start.5) | async-done | bytes 524320 | tf_op jit(solution)/shard_map/all_to_all | solution.py:108
  100.6 0.3 convolution_convert_fusion.1
  100.9 0.0 copy-start.2
  100.9 0.2 convolution_bitcast_fusion
  101.1 3.0 %psum.7 = f32[32]{0:T(128)} all-reduce(f32[32]{0:T(128)S(1)} %convolution_bitcast_fusion), channel_id=1, replica_groups=mesh['groups'=2,'replica'=8,'tensor'=2] {'tensor'}, use_global_device_ids=true, to_apply=%region_5.6 | all-reduce | flops 32 | bytes 256 | tf_op jit(solution)/shard_map/psum | solution.py:116
  104.1 0.0 copy-done.2
  (8 shorter events, 0.2 us)
Async XLA Ops:
  0.6 53.9 %copy-start = (bf16[128,16,512]{2,1,0:T(8,128)(2,1)S(1)}, bf16[128,16,512]{2,1,0:T(8,128)(2,1)}, u32[]{:S(2)}) copy-start(bf16[128,16,512]{2,1,0:T(8,128)(2,1)} %param.13) | copy-start | bytes 6291460
  3.7 13.7 %all-to-all-start = ((s32[8,1,8]{2,1,0:T(1,128)}), s32[8,1,8]{2,1,0:T(1,128)S(1)}, u32[]{:S(2)}, u32[]{:S(2)}) async-start(s32[8,1,8]{2,1,0:T(1,128)} %bitcast.1), calls=%async_computation | async-start | bytes 8192 | tf_op jit(solution)/shard_map/all_to_all | solution.py:87
  17.3 9.7 %all-to-all-start.2 = ((s32[8,1,8]{2,1,0:T(1,128)}), s32[8,1,8]{2,1,0:T(1,128)S(1)}, u32[]{:S(2)}, u32[]{:S(2)}) async-start(s32[8,1,8]{2,1,0:T(1,128)} %bitcast.4), calls=%async_computation.2 | async-start | bytes 8192 | tf_op jit(solution)/shard_map/all_to_all | solution.py:86
  27.1 10.2 %all-to-all-start.3 = ((bf16[8,8,512]{2,1,0:T(8,128)(2,1)}), bf16[8,8,512]{2,1,0:T(8,128)(2,1)S(1)}, u32[]{:S(2)}, u32[]{:S(2)}) async-start(bf16[8,8,512]{2,1,0:T(8,128)(2,1)} %fusion.14), calls=%async_computation.3 | async-start | bytes 131072 | tf_op jit(solution)/shard_map/all_to_all | solution.py:94
  37.3 10.2 %all-to-all-start.4 = ((bf16[8,8,512]{2,1,0:T(8,128)(2,1)}), bf16[8,8,512]{2,1,0:T(8,128)(2,1)S(1)}, u32[]{:S(2)}, u32[]{:S(2)}) async-start(bf16[8,8,512]{2,1,0:T(8,128)(2,1)} %fusion.15), calls=%async_computation.4 | async-start | bytes 131072 | tf_op jit(solution)/shard_map/all_to_all | solution.py:95
  47.5 28.2 %all-to-all-start.1 = ((bf16[8,8,4096]{2,1,0:T(8,128)(2,1)}), bf16[8,8,4096]{2,1,0:T(8,128)(2,1)S(1)}, u32[]{:S(2)}, u32[]{:S(2)}) async-start(bf16[8,8,4096]{2,1,0:T(8,128)(2,1)} %fusion), calls=%async_computation.1 | async-start | bytes 1048576 | tf_op jit(solution)/shard_map/all_to_all | solution.py:93
  76.2 5.7 %copy-start.1 = (bf16[64,64,4,128]{3,2,1,0:T(4,128)(2,1)S(1)}, bf16[64,64,4,128]{3,2,1,0:T(4,128)(2,1)}, u32[]{:S(2)}) copy-start(bf16[64,64,4,128]{3,2,1,0:T(4,128)(2,1)} %reshape_reshape.16) | copy-start | bytes 12582916
  81.9 8.4 %copy-start.3 = (bf16[4096]{0:T(1024)(128)(2,1)S(1)}, bf16[4096]{0:T(1024)(128)(2,1)}, u32[]{:S(2)}) copy-start(bf16[4096]{0:T(1024)(128)(2,1)} %param.19) | copy-start | bytes 24580
  84.4 16.2 %all-to-all-start.5 = ((bf16[8,8,4096]{2,1,0:T(8,128)(2,1)}), bf16[8,8,4096]{2,1,0:T(8,128)(2,1)S(1)}, u32[]{:S(2)}, u32[]{:S(2)}) async-start(bf16[8,8,4096]{2,1,0:T(8,128)(2,1)} %convert_element_type.52), calls=%async_computation.5 | async-start | bytes 1048576 | tf_op jit(solution)/shard_map/all_to_all | solution.py:108
  100.9 3.1 %copy-start.2 = (bf16[32,4096]{1,0:T(8,128)(2,1)}, bf16[32,4096]{1,0:T(8,128)(2,1)S(1)}, u32[]{:S(2)}) copy-start(bf16[32,4096]{1,0:T(8,128)(2,1)S(1)} %convolution_convert_fusion.1) | copy-start | bytes 786436
where the time goes:
time: 105 us; the launch traced here: 104 us
  waiting for transfers between devices  30.5 us (29%)
  starting transfers between devices  26.7 us (25%)
  local copies, waits for them, and re-layouts  25.7 us (24%)
  matrix products  12.6 us (12%)
  other arithmetic  4.65 us (4%)
  blocking collectives  2.96 us (3%)
    all_to_all x1, waiting for transfers between devices, shards(): lax.all_to_all(answers.reshape(replicas, capacity, -1), 'replica', split_...  10.3 us
    all_to_all x1, starting transfers between devices, shards(): lax.all_to_all(asked_lengths, 'replica', split_axis=0, concat_axis=0, til...  7.28 us
    another operation x1, local copies, waits for them, and re-layouts, attend(): keys_four = cached_key_rows.reshape(batch, key_span, key_heads, HEAD_SIZE)  6.93 us
    another operation x1, local copies, waits for them, and re-layouts, attend(): cached_value_rows.reshape(batch, key_span, key_heads, HEAD_SIZE)  6.92 us
    all_to_all x1, starting transfers between devices, shards(): lax.all_to_all(answers.reshape(replicas, capacity, -1), 'replica', split_...  5.93 us
    all_to_all x1, waiting for transfers between devices, shards(): lax.all_to_all(asked_lengths, 'replica', split_axis=0, concat_axis=0, til...  5.72 us
    dot_general x3, matrix products, to_slots(): jnp.dot(selector, rows, preferred_element_type=jnp.float32)  5.52 us
    all_to_all x1, waiting for transfers between devices, shards(): lax.all_to_all(key_slots, 'replica', split_axis=0, concat_axis=0, tiled=T...  5.18 us
  transfers between devices with their start and end apart: 6, of which 5 were waited for; matrix products, arithmetic and copies ran while one was open for 29% of the time, Pallas kernels for 0%

commit v1 on v0

v1 whole, which is shorter than its diff:
```python
import functools

import jax
import jax.numpy as jnp
from jax import lax
from jax.experimental import pallas as pl
from jax.experimental.pallas import tpu as pltpu
from jax.sharding import PartitionSpec as P

HEAD_SIZE = 128
TILE = 16
masked_score = -1e30
f32, bf16, i32 = jnp.float32, jnp.bfloat16, jnp.int32


def round_up(number, step):
    return -(-number // step) * step


def block_rows(capacity, heads, key_heads):
    new_rows = round_up(capacity * key_heads, TILE)
    return capacity * heads, new_rows, round_up(capacity, TILE)


def pack_kernel(capacity, q_ref, k_ref, v_ref, source_ref, parent_ref, length_ref, *rest):
    replicas = len(rest) - 6
    blocks, row_ref = rest[:replicas], rest[replicas]
    q_rows, new_rows, new_keys, new_values, taken = rest[replicas + 1 :]
    rows = q_ref.shape[0]
    heads, key_heads = q_ref.shape[1] // HEAD_SIZE, k_ref.shape[1] // HEAD_SIZE
    me = lax.axis_index("replica")
    for slot in range(replicas * capacity):
        row_ref[slot] = rows
    for replica in range(replicas):
        taken[replica] = 0
    for row in range(rows):
        source = source_ref[row]
        rank = taken[source]
        taken[source] = rank + 1
        row_ref[(source ^ me) * capacity + rank] = row
    for head in range(heads):
        lanes = slice(head * HEAD_SIZE, (head + 1) * HEAD_SIZE)
        q_rows[pl.ds(head, rows, stride=heads), :] = q_ref[:, lanes].astype(f32)
    for head in range(key_heads):
        lanes = slice(head * HEAD_SIZE, (head + 1) * HEAD_SIZE)
        new_rows[pl.ds(head, rows, stride=2 * key_heads), :] = k_ref[:, lanes].astype(f32)
        new_rows[pl.ds(key_heads + head, rows, stride=2 * key_heads), :] = v_ref[:, lanes].astype(f32)
    q_rows[rows * heads :, :] = jnp.zeros((heads, HEAD_SIZE), f32)
    new_rows[rows * 2 * key_heads :, :] = jnp.zeros((2 * key_heads, HEAD_SIZE), f32)
    q_size, new_size, meta_size = block_rows(capacity, heads, key_heads)
    if new_size != capacity * key_heads:
        new_keys[...] = jnp.zeros_like(new_keys)
        new_values[...] = jnp.zeros_like(new_values)
    at_row = lax.broadcasted_iota(i32, (meta_size, HEAD_SIZE), 0)
    at_lane = lax.broadcasted_iota(i32, (meta_size, HEAD_SIZE), 1)
    for partner, block in enumerate(blocks):
        meta = jnp.zeros((meta_size, HEAD_SIZE), f32)
        for slot in range(capacity):
            row = row_ref[partner * capacity + slot]
            block[slot * heads : (slot + 1) * heads, :] = q_rows[
                pl.ds(pl.multiple_of(row * heads, heads), heads), :
            ].astype(bf16)
            pair = new_rows[pl.ds(pl.multiple_of(row * 2 * key_heads, 2 * key_heads), 2 * key_heads), :]
            new_keys[slot * key_heads : (slot + 1) * key_heads, :] = pair[:key_heads]
            new_values[slot * key_heads : (slot + 1) * key_heads, :] = pair[key_heads:]
            real = row < rows
            held = jnp.minimum(row, rows - 1)
            parent = jnp.where(real, parent_ref[held], 0).astype(f32)
            length = jnp.where(real, length_ref[held], 0).astype(f32)
            meta = jnp.where(at_row == slot, jnp.where(at_lane == 0, parent, length), meta)
        block[q_size : q_size + new_size, :] = new_keys[...].astype(bf16)
        block[q_size + new_size : q_size + 2 * new_size, :] = new_values[...].astype(bf16)
        block[q_size + 2 * new_size :, :] = meta.astype(bf16)


def serve_kernel(capacity, heads, table_ref, block_ref, key_ref, value_ref, out_ref):
    pages_per_row = table_ref.shape[1]
    positions = key_ref.shape[1]
    key_heads = key_ref.shape[2] // HEAD_SIZE
    group = heads // key_heads
    span = pages_per_row * positions
    scaling = 1.0 / HEAD_SIZE**0.5
    q_size, new_size, meta_size = block_rows(capacity, heads, key_heads)
    meta = block_ref[q_size + 2 * new_size :, :].astype(f32)
    at_row = lax.broadcasted_iota(i32, meta.shape, 0)
    at_lane = lax.broadcasted_iota(i32, meta.shape, 1)
    rows = table_ref.shape[0]
    coded = jnp.where(at_lane == 0, meta, jnp.where(at_lane == 1, meta * rows, 0.0))
    per_tile = TILE // key_heads
    lanes = lax.broadcasted_iota(i32, (group, span + TILE), 1)
    for slot in range(capacity):
        code = jnp.sum(jnp.where(at_row == slot, coded, 0.0)).astype(i32)
        parent, length = lax.rem(code, rows), code // rows
        pages = [table_ref[parent, i] for i in range(pages_per_row)]
        tile = slot // per_tile * TILE
        own_keys = block_ref[q_size + tile : q_size + tile + TILE, :]
        own_values = block_ref[q_size + new_size + tile : q_size + new_size + tile + TILE, :]
        results = []
        q_slot = block_ref[slot * heads : (slot + 1) * heads, :]
        for head in range(key_heads):
            columns = slice(head * HEAD_SIZE, (head + 1) * HEAD_SIZE)
            keys = jnp.concatenate([key_ref[page, :, columns] for page in pages] + [own_keys], axis=0)
            values = jnp.concatenate([value_ref[page, :, columns] for page in pages] + [own_values], axis=0)
            q_group = q_slot[head * group : (head + 1) * group, :]
            scores = lax.dot_general(
                q_group, keys, (((1,), (1,)), ((), ())), preferred_element_type=f32
            )
            own = span + slot % per_tile * key_heads + head
            scores = jnp.where((lanes < length) | (lanes == own), scores * scaling, masked_score)
            peak = jnp.max(scores, axis=1, keepdims=True)
            weights = jnp.exp(scores - peak)
            denominator = jnp.sum(weights, axis=1, keepdims=True)
            numerator = jnp.dot(weights.astype(bf16), values, preferred_element_type=f32)
            results.append(numerator / denominator)
        out_ref[slot * heads : (slot + 1) * heads, :] = jnp.concatenate(results, axis=0).astype(bf16)


def unpack_kernel(capacity, heads, rows, row_ref, probe_ref, *rest):
    answers, (out_ref, reward_ref, gathered) = rest[:-3], rest[-3:]
    for partner, answer in enumerate(answers):
        for slot in range(capacity):
            row = row_ref[partner * capacity + slot]
            gathered[pl.ds(pl.multiple_of(row * heads, heads), heads), :] = answer[
                slot * heads : (slot + 1) * heads, :
            ].astype(f32)
    total = jnp.zeros((rows, HEAD_SIZE), f32)
    for head in range(heads):
        part = gathered[pl.ds(head, rows, stride=heads), :]
        out_ref[:, head * HEAD_SIZE : (head + 1) * HEAD_SIZE] = part.astype(bf16)
        total = total + part * probe_ref[:, head * HEAD_SIZE : (head + 1) * HEAD_SIZE].astype(f32)
    reward_ref[...] = jnp.sum(total.T, axis=0, keepdims=True)


def shards(
    queries,
    fresh_key_rows,
    fresh_value_rows,
    paged_key_store,
    paged_value_store,
    page_table,
    parent_replica,
    parent_slot,
    context_length,
    reward_probe,
):
    replicas = lax.axis_size("replica")
    rows = queries.shape[0]
    capacity = max(2, 2 * rows // replicas)
    heads = queries.shape[1] // HEAD_SIZE
    key_heads = fresh_key_rows.shape[1] // HEAD_SIZE
    block_size = sum(n * k for n, k in zip(block_rows(capacity, heads, key_heads), (1, 2, 1)))
    vmem, smem = pl.BlockSpec(memory_space=pltpu.VMEM), pl.BlockSpec(memory_space=pltpu.SMEM)
    params = pltpu.CompilerParams(vmem_limit_bytes=16 * 2**20)

    def in_vmem(x):
        return pltpu.with_memory_space_constraint(x, pltpu.VMEM)

    packed = pl.pallas_call(
        functools.partial(pack_kernel, capacity),
        out_shape=[pltpu.VMEM((block_size, HEAD_SIZE), bf16)] * replicas
        + [jax.ShapeDtypeStruct((replicas * capacity,), i32)],
        in_specs=[vmem] * 3 + [smem] * 3,
        out_specs=[vmem] * replicas + [smem],
        scratch_shapes=[
            pltpu.VMEM(((rows + 1) * heads, HEAD_SIZE), f32),
            pltpu.VMEM(((rows + 1) * 2 * key_heads, HEAD_SIZE), f32),
            pltpu.VMEM((block_rows(capacity, heads, key_heads)[1], HEAD_SIZE), f32),
            pltpu.VMEM((block_rows(capacity, heads, key_heads)[1], HEAD_SIZE), f32),
            pltpu.SMEM((replicas,), i32),
        ],
        compiler_params=params,
        name="pack",
    )(queries, fresh_key_rows, fresh_value_rows, parent_replica[:, 0], parent_slot[:, 0], context_length)
    blocks, slot_rows = packed[:replicas], packed[replicas]
    keys, values = in_vmem(paged_key_store), in_vmem(paged_value_store)

    serve = pl.pallas_call(
        functools.partial(serve_kernel, capacity, heads),
        out_shape=pltpu.VMEM((capacity * heads, HEAD_SIZE), bf16),
        in_specs=[smem, vmem, vmem, vmem],
        out_specs=vmem,
        compiler_params=params,
        cost_estimate=pl.CostEstimate(flops=10**7, bytes_accessed=2 * 10**6, transcendentals=0),
        name="serve",
    )

    def swap(x, partner):
        return lax.ppermute(x, "replica", [(i, i ^ partner) for i in range(replicas)])

    far_first = sorted(range(1, replicas), key=lambda m: (-m.bit_length(), m))
    answers = [None] * replicas
    arrived = {m: swap(blocks[m], m) for m in far_first}
    for m in far_first:
        answers[m] = swap(serve(page_table, in_vmem(arrived[m]), keys, values), m)
    answers[0] = serve(page_table, in_vmem(blocks[0]), keys, values)

    attended, partial_reward = pl.pallas_call(
        functools.partial(unpack_kernel, capacity, heads, rows),
        out_shape=[
            jax.ShapeDtypeStruct((rows, heads * HEAD_SIZE), bf16),
            jax.ShapeDtypeStruct((1, rows), f32),
        ],
        in_specs=[smem] + [vmem] * (replicas + 1),
        out_specs=[vmem] * 2,
        scratch_shapes=[pltpu.VMEM(((rows + 1) * heads, HEAD_SIZE), f32)],
        compiler_params=params,
        name="unpack",
    )(slot_rows, reward_probe.reshape(1, -1), *[in_vmem(x) for x in answers])
    return attended, lax.psum(partial_reward[0], "tensor")


def solution(mesh):
    placed = (
        P(("groups", "replica"), "tensor"),
        P(("groups", "replica"), "tensor"),
        P(("groups", "replica"), "tensor"),
        P(("groups", "replica"), None, "tensor"),
        P(("groups", "replica"), None, "tensor"),
        P(("groups", "replica"), None),
        P(("groups", "replica"), None),
        P(("groups", "replica"), None),
        P(("groups", "replica")),
        P("tensor"),
    )
    return jax.shard_map(
        shards,
        mesh=mesh,
        in_specs=placed,
        out_specs=(P(("groups", "replica"), "tensor"), P(("groups", "replica"))),
        check_vma=False,
    )
```

time: 105 us -> 105 us (level)
  Pallas kernels: 0 us -> 68.3 us
  waiting for transfers between devices: 30.5 us -> 0.04 us
  local copies, waits for them, and re-layouts: 25.7 us -> 8.38 us
  matrix products: 12.6 us -> 0 us
  other arithmetic: 4.65 us -> 0 us
  starting transfers between devices: 26.7 us -> 23.8 us
    pallas_call x0 -> x10, Pallas kernels: none -> 68.3 us  [the longest x7 56.5 us: shards(): answers[m] = swap(serve(page_table, in_vmem(arrived[m]), keys, values), m)]
    all_to_all x6 -> x0, waiting for transfers between devices: 30.5 us -> none  [the longest x1 10.3 us: shards(): lax.all_to_all(answers.reshape(replicas, capacity, -1), 'replica', split_...]
    all_to_all x6 -> x0, starting transfers between devices: 26.7 us -> none  [the longest x1 7.28 us: shards(): lax.all_to_all(asked_lengths, 'replica', split_axis=0, concat_axis=0, til...]
    ppermute x0 -> x14, starting transfers between devices: none -> 23.8 us  [swap(): lax.ppermute(x, 'replica', [(i, i ^ partner) for i in range(replicas)])]
    another operation x3 -> x0, local copies, waits for them, and re-layouts: 13.9 us -> none  [the longest x1 6.93 us: attend(): keys_four = cached_key_rows.reshape(batch, key_span, key_heads, HEAD_SIZE)]
    dot_general x8 -> x0, matrix products: 12.6 us -> none  [the longest x3 5.52 us: to_slots(): jnp.dot(selector, rows, preferred_element_type=jnp.float32)]
    gather x3 -> x0, local copies, waits for them, and re-layouts: 7.78 us -> none  [the longest x1 4.39 us: shards(): paged_value_store[page_numbers]]
    unnamed x11 -> x21, local copies, waits for them, and re-layouts: 0.89 us -> 8.37 us
  transfers between devices with their start and end apart: 6 -> 14, of which waited for: 5 -> 0; matrix products, arithmetic and copies ran while one was open for 29% -> 1% of each run, Pallas kernels for 0% -> 62%
where the time goes in v1:
time: 105 us; the launch traced here: 104 us
  Pallas kernels  68.3 us (65%)
  starting transfers between devices  23.8 us (23%)
  local copies, waits for them, and re-layouts  8.38 us (8%)
  blocking collectives  2.95 us (3%)
    pallas_call x7, Pallas kernels, shards(): answers[m] = swap(serve(page_table, in_vmem(arrived[m]), keys, values), m)  56.5 us
    ppermute x14, starting transfers between devices, swap(): lax.ppermute(x, 'replica', [(i, i ^ partner) for i in range(replicas)])  23.8 us
    unnamed x21, local copies, waits for them, and re-layouts  8.37 us
    pallas_call x1, Pallas kernels, shards(): answers[0] = serve(page_table, in_vmem(blocks[0]), keys, values)  8.08 us
    psum x1, blocking collectives, shards(): return (attended, lax.psum(partial_reward[0], 'tensor'))  2.95 us
  transfers between devices with their start and end apart: 14, of which 0 were waited for; matrix products, arithmetic and copies ran while one was open for 1% of the time, Pallas kernels for 62%

profile of v1, /device:TPU:0, one launch (start us, length us, event | category | flops | bytes accessed | tf_op | source)
XLA Modules:
  0.0 104.1 jit_solution(17576275599931929135)
XLA Ops:
  0.6 0.0 copy-start.3
  0.6 0.9 copy-done.3
  1.6 0.0 copy-start.4
  1.6 0.8 copy-done.4
  2.3 0.0 copy-start.5
  2.3 0.8 copy-done.5
  3.1 0.0 copy-start.6
  3.1 0.7 copy-done.6
  3.8 0.0 copy-start.7
  3.8 0.7 copy-done.7
  4.4 0.0 copy-start.8
  4.4 0.7 copy-done.8
  5.1 2.0 %pack.1 = (bf16[336,128]{1,0:T(8,128)(2,1)S(1)}, bf16[336,128]{1,0:T(8,128)(2,1)S(1)}, bf16[336,128]{1,0:T(8,128)(2,1)S(1)}, bf16[336,128]{1,0:T(8,128)(2,1)S(1)...) custom-call(bf16[32,4096]{1,0:T(8,128)(2,1)S(1)} %copy-done.3, ...), custom_call_target="tpu_custom_call" | custom-call | tf_op jit(solution)/shard_map/pack/pallas_call | solution.py:158
  7.1 3.0 %collective-permute-start = (bf16[336,128]{1,0:T(8,128)(2,1)S(1)}, bf16[336,128]{1,0:T(8,128)(2,1)S(1)}, u32[]{:S(2)}, u32[]{:S(2)}) collective-permute-start(bf16[336,128]{1,0:T(8,128)(2,1)S(1)} %get-tuple-element.15), channel_id=1, source_target_pairs={{0,2},{2,0},{4,6},{6,4},{8,10},{10,8},{12,14},{14,12},{1,3},{3,1},... | collective-permute-start | bytes 258056 | tf_op jit(solution)/shard_map/ppermute | solution.py:188
  10.1 1.6 %collective-permute-start.2 = (bf16[336,128]{1,0:T(8,128)(2,1)S(1)}, bf16[336,128]{1,0:T(8,128)(2,1)S(1)}, u32[]{:S(2)}, u32[]{:S(2)}) collective-permute-start(bf16[336,128]{1,0:T(8,128)(2,1)S(1)} %get-tuple-element.16), channel_id=1, source_target_pairs={{0,4},{2,6},{4,0},{6,2},{8,12},{10,14},{12,8},{14,10},{1,5},{3,7},... | collective-permute-start | bytes 258056 | tf_op jit(solution)/shard_map/ppermute | solution.py:188
  11.7 0.0 collective-permute-start.4
  11.7 3.0 %collective-permute-start.6 = (bf16[336,128]{1,0:T(8,128)(2,1)S(1)}, bf16[336,128]{1,0:T(8,128)(2,1)S(1)}, u32[]{:S(2)}, u32[]{:S(2)}) collective-permute-start(bf16[336,128]{1,0:T(8,128)(2,1)S(1)} %get-tuple-element.18), channel_id=1, source_target_pairs={{0,8},{2,10},{4,12},{6,14},{8,0},{10,2},{12,4},{14,6},{1,9},{3,11}... | collective-permute-start | bytes 258056 | tf_op jit(solution)/shard_map/ppermute | solution.py:188
  14.7 1.3 %collective-permute-start.8 = (bf16[336,128]{1,0:T(8,128)(2,1)S(1)}, bf16[336,128]{1,0:T(8,128)(2,1)S(1)}, u32[]{:S(2)}, u32[]{:S(2)}) collective-permute-start(bf16[336,128]{1,0:T(8,128)(2,1)S(1)} %get-tuple-element.19), channel_id=1, source_target_pairs={{0,10},{2,8},{4,14},{6,12},{8,2},{10,0},{12,6},{14,4},{1,11},{3,9}... | collective-permute-start | bytes 258056 | tf_op jit(solution)/shard_map/ppermute | solution.py:188
  16.0 0.0 collective-permute-done.block_ref
  16.0 3.6 %collective-permute-start.10 = (bf16[336,128]{1,0:T(8,128)(2,1)S(1)}, bf16[336,128]{1,0:T(8,128)(2,1)S(1)}, u32[]{:S(2)}, u32[]{:S(2)}) collective-permute-start(bf16[336,128]{1,0:T(8,128)(2,1)S(1)} %get-tuple-element.20), channel_id=1, source_target_pairs={{0,12},{2,14},{4,8},{6,10},{8,4},{10,6},{12,0},{14,2},{1,13},{3,15... | collective-permute-start | bytes 258056 | tf_op jit(solution)/shard_map/ppermute | solution.py:188
  19.6 0.0 collective-permute-done.2.block_ref
  19.6 0.0 collective-permute-start.12
  19.6 0.8 copy.12.table_ref
  20.4 0.0 copy-start
  20.4 1.6 %copy-done = bf16[128,16,512]{2,1,0:T(8,128)(2,1)S(1)} copy-done((bf16[128,16,512]{2,1,0:T(8,128)(2,1)S(1)}, bf16[128,16,512]{2,1,0:T(8,128)(2,1)}, u32[]{:S(2)}) %copy-start) | copy-done | bytes 2097176
  22.0 0.0 copy-start.2
  22.0 1.6 %copy-done.2 = bf16[128,16,512]{2,1,0:T(8,128)(2,1)S(1)} copy-done((bf16[128,16,512]{2,1,0:T(8,128)(2,1)S(1)}, bf16[128,16,512]{2,1,0:T(8,128)(2,1)}, u32[]{:S(2)}) %copy-start.2) | copy-done | bytes 2097176
  23.5 8.1 %serve.9 = bf16[256,128]{1,0:T(8,128)(2,1)S(1)} custom-call(s32[32,4]{1,0:T(8,128)S(1)} %copy.12.table_ref, bf16[336,128]{1,0:T(8,128)(2,1)S(1)} %collective-permute-done.block_ref, bf16[128,16,512]{2,1,0:T(8,128)(2,1)S(1)} %copy-done, bf16[128,16,512]{2,1,0:T(8,128)(2,1)S(1)} %copy-done.2), custom_call_target="tpu_custom_call" | custom-call | flops 10000000 | bytes 2000000 | tf_op jit(solution)/shard_map/serve/pallas_call | solution.py:194
  31.6 8.1 %serve.10 = bf16[256,128]{1,0:T(8,128)(2,1)S(1)} custom-call(s32[32,4]{1,0:T(8,128)S(1)} %copy.12.table_ref, bf16[336,128]{1,0:T(8,128)(2,1)S(1)} %collective-permute-done.2.block_ref, bf16[128,16,512]{2,1,0:T(8,128)(2,1)S(1)} %copy-done, bf16[128,16,512]{2,1,0:T(8,128)(2,1)S(1)} %copy-done.2), custom_call_target="tpu_custom_call" | custom-call | flops 10000000 | bytes 2000000 | tf_op jit(solution)/shard_map/serve/pallas_call | solution.py:194
  39.7 0.0 collective-permute-done.4.block_ref
  39.7 1.7 %collective-permute-start.1 = (bf16[256,128]{1,0:T(8,128)(2,1)S(1)}, bf16[256,128]{1,0:T(8,128)(2,1)S(1)}, u32[]{:S(2)}, u32[]{:S(2)}) collective-permute-start(bf16[256,128]{1,0:T(8,128)(2,1)S(1)} %serve.9), channel_id=1, source_target_pairs={{0,2},{2,0},{4,6},{6,4},{8,10},{10,8},{12,14},{14,12},{1,3},{3,1},... | collective-permute-start | bytes 196616 | tf_op jit(solution)/shard_map/ppermute | solution.py:188
  41.4 0.0 collective-permute-done.6.block_ref
  41.4 0.0 collective-permute-start.3
  41.4 8.1 %serve.11 = bf16[256,128]{1,0:T(8,128)(2,1)S(1)} custom-call(s32[32,4]{1,0:T(8,128)S(1)} %copy.12.table_ref, bf16[336,128]{1,0:T(8,128)(2,1)S(1)} %collective-permute-done.4.block_ref, bf16[128,16,512]{2,1,0:T(8,128)(2,1)S(1)} %copy-done, bf16[128,16,512]{2,1,0:T(8,128)(2,1)S(1)} %copy-done.2), custom_call_target="tpu_custom_call" | custom-call | flops 10000000 | bytes 2000000 | tf_op jit(solution)/shard_map/serve/pallas_call | solution.py:194
  49.5 8.1 %serve.12 = bf16[256,128]{1,0:T(8,128)(2,1)S(1)} custom-call(s32[32,4]{1,0:T(8,128)S(1)} %copy.12.table_ref, bf16[336,128]{1,0:T(8,128)(2,1)S(1)} %collective-permute-done.6.block_ref, bf16[128,16,512]{2,1,0:T(8,128)(2,1)S(1)} %copy-done, bf16[128,16,512]{2,1,0:T(8,128)(2,1)S(1)} %copy-done.2), custom_call_target="tpu_custom_call" | custom-call | flops 10000000 | bytes 2000000 | tf_op jit(solution)/shard_map/serve/pallas_call | solution.py:194
  57.6 0.0 collective-permute-done.8.block_ref
  57.6 1.8 %collective-permute-start.5 = (bf16[256,128]{1,0:T(8,128)(2,1)S(1)}, bf16[256,128]{1,0:T(8,128)(2,1)S(1)}, u32[]{:S(2)}, u32[]{:S(2)}) collective-permute-start(bf16[256,128]{1,0:T(8,128)(2,1)S(1)} %serve.11), channel_id=1, source_target_pairs={{0,6},{2,4},{4,2},{6,0},{8,14},{10,12},{12,10},{14,8},{1,7},{3,5},... | collective-permute-start | bytes 196616 | tf_op jit(solution)/shard_map/ppermute | solution.py:188
  59.4 8.1 %serve.13 = bf16[256,128]{1,0:T(8,128)(2,1)S(1)} custom-call(s32[32,4]{1,0:T(8,128)S(1)} %copy.12.table_ref, bf16[336,128]{1,0:T(8,128)(2,1)S(1)} %collective-permute-done.8.block_ref, bf16[128,16,512]{2,1,0:T(8,128)(2,1)S(1)} %copy-done, bf16[128,16,512]{2,1,0:T(8,128)(2,1)S(1)} %copy-done.2), custom_call_target="tpu_custom_call" | custom-call | flops 10000000 | bytes 2000000 | tf_op jit(solution)/shard_map/serve/pallas_call | solution.py:194
  67.5 0.0 collective-permute-done.10.block_ref
  67.5 2.4 %collective-permute-start.7 = (bf16[256,128]{1,0:T(8,128)(2,1)S(1)}, bf16[256,128]{1,0:T(8,128)(2,1)S(1)}, u32[]{:S(2)}, u32[]{:S(2)}) collective-permute-start(bf16[256,128]{1,0:T(8,128)(2,1)S(1)} %serve.12), channel_id=1, source_target_pairs={{0,8},{2,10},{4,12},{6,14},{8,0},{10,2},{12,4},{14,6},{1,9},{3,11}... | collective-permute-start | bytes 196616 | tf_op jit(solution)/shard_map/ppermute | solution.py:188
  69.8 8.1 %serve.14 = bf16[256,128]{1,0:T(8,128)(2,1)S(1)} custom-call(s32[32,4]{1,0:T(8,128)S(1)} %copy.12.table_ref, bf16[336,128]{1,0:T(8,128)(2,1)S(1)} %collective-permute-done.10.block_ref, bf16[128,16,512]{2,1,0:T(8,128)(2,1)S(1)} %copy-done, bf16[128,16,512]{2,1,0:T(8,128)(2,1)S(1)} %copy-done.2), custom_call_target="tpu_custom_call" | custom-call | flops 10000000 | bytes 2000000 | tf_op jit(solution)/shard_map/serve/pallas_call | solution.py:194
  77.9 0.0 copy-start.9
  77.9 0.0 copy-start.1
  77.9 0.0 collective-permute-done.12.block_ref
  77.9 1.7 %collective-permute-start.9 = (bf16[256,128]{1,0:T(8,128)(2,1)S(1)}, bf16[256,128]{1,0:T(8,128)(2,1)S(1)}, u32[]{:S(2)}, u32[]{:S(2)}) collective-permute-start(bf16[256,128]{1,0:T(8,128)(2,1)S(1)} %serve.13), channel_id=1, source_target_pairs={{0,10},{2,8},{4,14},{6,12},{8,2},{10,0},{12,6},{14,4},{1,11},{3,9}... | collective-permute-start | bytes 196616 | tf_op jit(solution)/shard_map/ppermute | solution.py:188
  79.7 8.1 %serve.15 = bf16[256,128]{1,0:T(8,128)(2,1)S(1)} custom-call(s32[32,4]{1,0:T(8,128)S(1)} %copy.12.table_ref, bf16[336,128]{1,0:T(8,128)(2,1)S(1)} %collective-permute-done.12.block_ref, bf16[128,16,512]{2,1,0:T(8,128)(2,1)S(1)} %copy-done, bf16[128,16,512]{2,1,0:T(8,128)(2,1)S(1)} %copy-done.2), custom_call_target="tpu_custom_call" | custom-call | flops 10000000 | bytes 2000000 | tf_op jit(solution)/shard_map/serve/pallas_call | solution.py:194
  87.7 0.0 collective-permute-done.1.rest_1_
  87.7 3.6 %collective-permute-start.11 = (bf16[256,128]{1,0:T(8,128)(2,1)S(1)}, bf16[256,128]{1,0:T(8,128)(2,1)S(1)}, u32[]{:S(2)}, u32[]{:S(2)}) collective-permute-start(bf16[256,128]{1,0:T(8,128)(2,1)S(1)} %serve.14), channel_id=1, source_target_pairs={{0,12},{2,14},{4,8},{6,10},{8,4},{10,6},{12,0},{14,2},{1,13},{3,15... | collective-permute-start | bytes 196616 | tf_op jit(solution)/shard_map/ppermute | solution.py:188
  91.4 0.0 collective-permute-done.3.rest_2_
  91.4 0.0 collective-permute-start.13
  91.4 0.0 copy-done.9
  91.4 0.0 copy-done.1
  91.4 8.1 %serve.8.rest_0_ = bf16[256,128]{1,0:T(8,128)(2,1)S(1)} custom-call(s32[32,4]{1,0:T(8,128)S(1)} %copy.12.table_ref, bf16[336,128]{1,0:T(8,128)(2,1)S(1)} %get-tuple-element.14.block_ref, bf16[128,16,512]{2,1,0:T(8,128)(2,1)S(1)} %copy-done.1, bf16[128,16,512]{2,1,0:T(8,128)(2,1)S(1)} %copy-done.2), custom_call_target="tpu_custom_call" | custom-call | flops 10000000 | bytes 2000000 | tf_op jit(solution)/shard_map/serve/pallas_call | solution.py:195
  99.5 0.0 collective-permute-done.5.rest_3_
  99.5 0.0 collective-permute-done.7.rest_4_
  99.5 0.0 collective-permute-done.9.rest_5_
  99.5 0.0 collective-permute-done.11.rest_6_
  99.5 0.0 collective-permute-done.13.rest_7_
  99.5 1.6 %unpack.1 = (bf16[32,4096]{1,0:T(8,128)(2,1)}, f32[1,32]{1,0:T(1,128)S(1)}) custom-call(s32[64]{0:T(128)S(1)} %get-tuple-element.13.row_ref, bf16[1,4096]{1,0:T(2,128)(2,1)S(1)} %reshape.7.probe_ref, bf16[256,128]{1,0:T(8,128)(2,1)S(1)} %serve.8.rest_0_, bf16[256,128]{1,0:T(8,128)(2,1)S(1)} %collective-permute-done.1.rest_1_, ...), custom_call_target="tpu_custom_call" | custom-call | tf_op jit(solution)/shard_map/unpack/pallas_call | solution.py:197
  101.2 2.9 %psum.7 = f32[32]{0:T(128)} all-reduce(f32[32]{0:T(128)S(1)} %bitcast.5), channel_id=1, replica_groups=mesh['groups'=2,'replica'=8,'tensor'=2] {'tensor'}, use_global_device_ids=true, to_apply=%region_0.0 | all-reduce | flops 32 | bytes 256 | tf_op jit(solution)/shard_map/psum | solution.py:209
  (1 shorter events, 0.0 us)
Async XLA Ops:
  0.6 1.0 copy-start.3
  1.6 0.8 copy-start.4
  2.3 0.8 copy-start.5
  3.1 0.7 copy-start.6
  3.8 0.7 copy-start.7
  4.4 0.7 copy-start.8
  7.1 8.9 %collective-permute-start = (bf16[336,128]{1,0:T(8,128)(2,1)S(1)}, bf16[336,128]{1,0:T(8,128)(2,1)S(1)}, u32[]{:S(2)}, u32[]{:S(2)}) collective-permute-start(bf16[336,128]{1,0:T(8,128)(2,1)S(1)} %get-tuple-element.15), channel_id=1, source_target_pairs={{0,2},{2,0},{4,6},{6,4},{8,10},{10,8},{12,14},{14,12},{1,3},{3,1},... | collective-permute-start | bytes 258056 | tf_op jit(solution)/shard_map/ppermute | solution.py:188
  10.1 9.5 %collective-permute-start.2 = (bf16[336,128]{1,0:T(8,128)(2,1)S(1)}, bf16[336,128]{1,0:T(8,128)(2,1)S(1)}, u32[]{:S(2)}, u32[]{:S(2)}) collective-permute-start(bf16[336,128]{1,0:T(8,128)(2,1)S(1)} %get-tuple-element.16), channel_id=1, source_target_pairs={{0,4},{2,6},{4,0},{6,2},{8,12},{10,14},{12,8},{14,10},{1,5},{3,7},... | collective-permute-start | bytes 258056 | tf_op jit(solution)/shard_map/ppermute | solution.py:188
  11.7 28.0 %collective-permute-start.4 = (bf16[336,128]{1,0:T(8,128)(2,1)S(1)}, bf16[336,128]{1,0:T(8,128)(2,1)S(1)}, u32[]{:S(2)}, u32[]{:S(2)}) collective-permute-start(bf16[336,128]{1,0:T(8,128)(2,1)S(1)} %get-tuple-element.17), channel_id=1, source_target_pairs={{0,6},{2,4},{4,2},{6,0},{8,14},{10,12},{12,10},{14,8},{1,7},{3,5},... | collective-permute-start | bytes 258056 | tf_op jit(solution)/shard_map/ppermute | solution.py:188
  11.7 29.7 %collective-permute-start.6 = (bf16[336,128]{1,0:T(8,128)(2,1)S(1)}, bf16[336,128]{1,0:T(8,128)(2,1)S(1)}, u32[]{:S(2)}, u32[]{:S(2)}) collective-permute-start(bf16[336,128]{1,0:T(8,128)(2,1)S(1)} %get-tuple-element.18), channel_id=1, source_target_pairs={{0,8},{2,10},{4,12},{6,14},{8,0},{10,2},{12,4},{14,6},{1,9},{3,11}... | collective-permute-start | bytes 258056 | tf_op jit(solution)/shard_map/ppermute | solution.py:188
  14.7 42.9 %collective-permute-start.8 = (bf16[336,128]{1,0:T(8,128)(2,1)S(1)}, bf16[336,128]{1,0:T(8,128)(2,1)S(1)}, u32[]{:S(2)}, u32[]{:S(2)}) collective-permute-start(bf16[336,128]{1,0:T(8,128)(2,1)S(1)} %get-tuple-element.19), channel_id=1, source_target_pairs={{0,10},{2,8},{4,14},{6,12},{8,2},{10,0},{12,6},{14,4},{1,11},{3,9}... | collective-permute-start | bytes 258056 | tf_op jit(solution)/shard_map/ppermute | solution.py:188
  16.0 51.5 %collective-permute-start.10 = (bf16[336,128]{1,0:T(8,128)(2,1)S(1)}, bf16[336,128]{1,0:T(8,128)(2,1)S(1)}, u32[]{:S(2)}, u32[]{:S(2)}) collective-permute-start(bf16[336,128]{1,0:T(8,128)(2,1)S(1)} %get-tuple-element.20), channel_id=1, source_target_pairs={{0,12},{2,14},{4,8},{6,10},{8,4},{10,6},{12,0},{14,2},{1,13},{3,15... | collective-permute-start | bytes 258056 | tf_op jit(solution)/shard_map/ppermute | solution.py:188
  19.6 58.3 %collective-permute-start.12 = (bf16[336,128]{1,0:T(8,128)(2,1)S(1)}, bf16[336,128]{1,0:T(8,128)(2,1)S(1)}, u32[]{:S(2)}, u32[]{:S(2)}) collective-permute-start(bf16[336,128]{1,0:T(8,128)(2,1)S(1)} %get-tuple-element.21), channel_id=1, source_target_pairs={{0,14},{2,12},{4,10},{6,8},{8,6},{10,4},{12,2},{14,0},{1,15},{3,13... | collective-permute-start | bytes 258056 | tf_op jit(solution)/shard_map/ppermute | solution.py:188
  20.4 1.6 %copy-start = (bf16[128,16,512]{2,1,0:T(8,128)(2,1)S(1)}, bf16[128,16,512]{2,1,0:T(8,128)(2,1)}, u32[]{:S(2)}) copy-start(bf16[128,16,512]{2,1,0:T(8,128)(2,1)} %key_ref.15) | copy-start | bytes 6291460
  22.0 1.6 %copy-start.2 = (bf16[128,16,512]{2,1,0:T(8,128)(2,1)S(1)}, bf16[128,16,512]{2,1,0:T(8,128)(2,1)}, u32[]{:S(2)}) copy-start(bf16[128,16,512]{2,1,0:T(8,128)(2,1)} %value_ref.15) | copy-start | bytes 6291460
  39.7 48.0 %collective-permute-start.1 = (bf16[256,128]{1,0:T(8,128)(2,1)S(1)}, bf16[256,128]{1,0:T(8,128)(2,1)S(1)}, u32[]{:S(2)}, u32[]{:S(2)}) collective-permute-start(bf16[256,128]{1,0:T(8,128)(2,1)S(1)} %serve.9), channel_id=1, source_target_pairs={{0,2},{2,0},{4,6},{6,4},{8,10},{10,8},{12,14},{14,12},{1,3},{3,1},... | collective-permute-start | bytes 196616 | tf_op jit(solution)/shard_map/ppermute | solution.py:188
  41.4 50.0 %collective-permute-start.3 = (bf16[256,128]{1,0:T(8,128)(2,1)S(1)}, bf16[256,128]{1,0:T(8,128)(2,1)S(1)}, u32[]{:S(2)}, u32[]{:S(2)}) collective-permute-start(bf16[256,128]{1,0:T(8,128)(2,1)S(1)} %serve.10), channel_id=1, source_target_pairs={{0,4},{2,6},{4,0},{6,2},{8,12},{10,14},{12,8},{14,10},{1,5},{3,7},... | collective-permute-start | bytes 196616 | tf_op jit(solution)/shard_map/ppermute | solution.py:188
  57.6 41.9 %collective-permute-start.5 = (bf16[256,128]{1,0:T(8,128)(2,1)S(1)}, bf16[256,128]{1,0:T(8,128)(2,1)S(1)}, u32[]{:S(2)}, u32[]{:S(2)}) collective-permute-start(bf16[256,128]{1,0:T(8,128)(2,1)S(1)} %serve.11), channel_id=1, source_target_pairs={{0,6},{2,4},{4,2},{6,0},{8,14},{10,12},{12,10},{14,8},{1,7},{3,5},... | collective-permute-start | bytes 196616 | tf_op jit(solution)/shard_map/ppermute | solution.py:188
  67.5 32.0 %collective-permute-start.7 = (bf16[256,128]{1,0:T(8,128)(2,1)S(1)}, bf16[256,128]{1,0:T(8,128)(2,1)S(1)}, u32[]{:S(2)}, u32[]{:S(2)}) collective-permute-start(bf16[256,128]{1,0:T(8,128)(2,1)S(1)} %serve.12), channel_id=1, source_target_pairs={{0,8},{2,10},{4,12},{6,14},{8,0},{10,2},{12,4},{14,6},{1,9},{3,11}... | collective-permute-start | bytes 196616 | tf_op jit(solution)/shard_map/ppermute | solution.py:188
  77.9 13.5 %copy-start.9 = (bf16[4096]{0:T(1024)(128)(2,1)S(1)}, bf16[4096]{0:T(1024)(128)(2,1)}, u32[]{:S(2)}) copy-start(bf16[4096]{0:T(1024)(128)(2,1)} %param.19) | copy-start | bytes 24580
  77.9 13.5 %copy-start.1 = (bf16[128,16,512]{2,1,0:T(8,128)(2,1)S(1)}, bf16[128,16,512]{2,1,0:T(8,128)(2,1)}, u32[]{:S(2)}) copy-start(bf16[128,16,512]{2,1,0:T(8,128)(2,1)} %key_ref.15) | copy-start | bytes 6291460
  77.9 21.6 %collective-permute-start.9 = (bf16[256,128]{1,0:T(8,128)(2,1)S(1)}, bf16[256,128]{1,0:T(8,128)(2,1)S(1)}, u32[]{:S(2)}, u32[]{:S(2)}) collective-permute-start(bf16[256,128]{1,0:T(8,128)(2,1)S(1)} %serve.13), channel_id=1, source_target_pairs={{0,10},{2,8},{4,14},{6,12},{8,2},{10,0},{12,6},{14,4},{1,11},{3,9}... | collective-permute-start | bytes 196616 | tf_op jit(solution)/shard_map/ppermute | solution.py:188
  87.7 11.8 %collective-permute-start.11 = (bf16[256,128]{1,0:T(8,128)(2,1)S(1)}, bf16[256,128]{1,0:T(8,128)(2,1)S(1)}, u32[]{:S(2)}, u32[]{:S(2)}) collective-permute-start(bf16[256,128]{1,0:T(8,128)(2,1)S(1)} %serve.14), channel_id=1, source_target_pairs={{0,12},{2,14},{4,8},{6,10},{8,4},{10,6},{12,0},{14,2},{1,13},{3,15... | collective-permute-start | bytes 196616 | tf_op jit(solution)/shard_map/ppermute | solution.py:188
  91.4 8.2 %collective-permute-start.13 = (bf16[256,128]{1,0:T(8,128)(2,1)S(1)}, bf16[256,128]{1,0:T(8,128)(2,1)S(1)}, u32[]{:S(2)}, u32[]{:S(2)}) collective-permute-start(bf16[256,128]{1,0:T(8,128)(2,1)S(1)} %serve.15), channel_id=1, source_target_pairs={{0,14},{2,12},{4,10},{6,8},{8,6},{10,4},{12,2},{14,0},{1,15},{3,13... | collective-permute-start | bytes 196616 | tf_op jit(solution)/shard_map/ppermute | solution.py:188

commit v2 on v1

v2 whole, which is shorter than its diff:
```python
import functools

import jax
import jax.numpy as jnp
from jax import lax
from jax.experimental import pallas as pl
from jax.experimental.pallas import tpu as pltpu
from jax.sharding import PartitionSpec as P

HEAD_SIZE = 128
TILE = 16
masked_score = -1e30
f32, bf16, i32 = jnp.float32, jnp.bfloat16, jnp.int32


def round_up(number, step):
    return -(-number // step) * step


def block_rows(capacity, heads, key_heads):
    new_rows = round_up(capacity * key_heads, TILE)
    return capacity * heads, new_rows, round_up(capacity, TILE)


def pack_kernel(
    capacity, q_hbm, k_hbm, v_hbm, key_hbm, value_hbm, table_hbm, source_hbm, parent_hbm, length_hbm, *rest
):
    replicas = len(rest) - 16
    blocks = rest[:replicas]
    keys_ref, values_ref, table_ref, row_ref = rest[replicas : replicas + 4]
    q_ref, k_ref, v_ref, source_ref, parent_ref, length_ref = rest[replicas + 4 : replicas + 10]
    q_rows, new_rows, new_keys, new_values, taken, arrived = rest[replicas + 10 :]
    copies = [
        pltpu.make_async_copy(source, target, arrived.at[i])
        for i, (source, target) in enumerate(
            (
                (source_hbm, source_ref),
                (q_hbm, q_ref),
                (k_hbm, k_ref),
                (v_hbm, v_ref),
                (parent_hbm, parent_ref),
                (length_hbm, length_ref),
                (table_hbm, table_ref),
                (key_hbm, keys_ref),
                (value_hbm, values_ref),
            )
        )
    ]
    for copy in copies:
        copy.start()
    rows = q_ref.shape[0]
    heads, key_heads = q_ref.shape[1] // HEAD_SIZE, k_ref.shape[1] // HEAD_SIZE
    me = lax.axis_index("replica")
    for slot in range(replicas * capacity):
        row_ref[slot] = rows
    for replica in range(replicas):
        taken[replica] = 0
    q_rows[rows * heads :, :] = jnp.zeros((heads, HEAD_SIZE), f32)
    new_rows[rows * 2 * key_heads :, :] = jnp.zeros((2 * key_heads, HEAD_SIZE), f32)
    q_size, new_size, meta_size = block_rows(capacity, heads, key_heads)
    if new_size != capacity * key_heads:
        new_keys[...] = jnp.zeros_like(new_keys)
        new_values[...] = jnp.zeros_like(new_values)
    copies[0].wait()
    for row in range(rows):
        source = source_ref[row]
        rank = taken[source]
        taken[source] = rank + 1
        row_ref[(source ^ me) * capacity + rank] = row
    for copy in copies[1:6]:
        copy.wait()
    for head in range(heads):
        lanes = slice(head * HEAD_SIZE, (head + 1) * HEAD_SIZE)
        q_rows[pl.ds(head, rows, stride=heads), :] = q_ref[:, lanes].astype(f32)
    for head in range(key_heads):
        lanes = slice(head * HEAD_SIZE, (head + 1) * HEAD_SIZE)
        new_rows[pl.ds(head, rows, stride=2 * key_heads), :] = k_ref[:, lanes].astype(f32)
        new_rows[pl.ds(key_heads + head, rows, stride=2 * key_heads), :] = v_ref[:, lanes].astype(f32)
    at_row = lax.broadcasted_iota(i32, (meta_size, HEAD_SIZE), 0)
    at_lane = lax.broadcasted_iota(i32, (meta_size, HEAD_SIZE), 1)
    for partner, block in enumerate(blocks):
        meta = jnp.zeros((meta_size, HEAD_SIZE), f32)
        for slot in range(capacity):
            row = row_ref[partner * capacity + slot]
            block[slot * heads : (slot + 1) * heads, :] = q_rows[
                pl.ds(pl.multiple_of(row * heads, heads), heads), :
            ].astype(bf16)
            pair = new_rows[pl.ds(pl.multiple_of(row * 2 * key_heads, 2 * key_heads), 2 * key_heads), :]
            new_keys[slot * key_heads : (slot + 1) * key_heads, :] = pair[:key_heads]
            new_values[slot * key_heads : (slot + 1) * key_heads, :] = pair[key_heads:]
            real = row < rows
            held = jnp.minimum(row, rows - 1)
            parent = jnp.where(real, parent_ref[held], 0).astype(f32)
            length = jnp.where(real, length_ref[held], 0).astype(f32)
            meta = jnp.where(at_row == slot, jnp.where(at_lane == 0, parent, length), meta)
        block[q_size : q_size + new_size, :] = new_keys[...].astype(bf16)
        block[q_size + new_size : q_size + 2 * new_size, :] = new_values[...].astype(bf16)
        block[q_size + 2 * new_size :, :] = meta.astype(bf16)
    for copy in copies[6:]:
        copy.wait()


def serve_kernel(capacity, heads, table_ref, block_ref, key_ref, value_ref, out_ref):
    pages_per_row, rows = table_ref.shape
    positions, width = key_ref.shape[1:]
    key_heads = width // HEAD_SIZE
    group = heads // key_heads
    span = pages_per_row * positions
    scaling = 1.0 / HEAD_SIZE**0.5
    q_size, new_size, meta_size = block_rows(capacity, heads, key_heads)
    per_tile = TILE // key_heads

    def iota(shape, axis):
        return lax.broadcasted_iota(i32, shape, axis)

    meta = block_ref[q_size + 2 * new_size :, :].astype(f32)
    at_row, at_lane = iota(meta.shape, 0), iota(meta.shape, 1)
    coded = jnp.where(at_lane == 0, meta, jnp.where(at_lane == 1, meta * rows, 0.0))
    codes = [jnp.sum(jnp.where(at_row == slot, coded, 0.0)) for slot in range(capacity)]
    codes = [code.astype(i32) for code in codes]
    lengths = [code // rows for code in codes]
    parents = [code - length * rows for code, length in zip(codes, lengths)]
    pages = [[table_ref[i, parent] for i in range(pages_per_row)] for parent in parents]
    diagonal = iota((heads, width), 0) // group == iota((heads, width), 1) // HEAD_SIZE
    own_lane = iota((heads, TILE), 1) - iota((heads, TILE), 0) // group
    seen = iota((heads, span), 1)
    scores, own_scores = [], []
    for slot in range(capacity):
        tile = slot // per_tile * TILE
        own_keys = block_ref[q_size + tile : q_size + tile + TILE, :]
        q_slot = block_ref[slot * heads : (slot + 1) * heads, :]
        keys = jnp.concatenate([key_ref[page] for page in pages[slot]], axis=0)
        spread = jnp.where(diagonal, jnp.concatenate([q_slot] * key_heads, axis=1), jnp.zeros((), bf16))
        by_lanes = (((1,), (1,)), ((), ()))
        scores.append(lax.dot_general(spread, keys, by_lanes, preferred_element_type=f32))
        own_scores.append(lax.dot_general(q_slot, own_keys, by_lanes, preferred_element_type=f32))
    weights, own_weights, denominators = [], [], []
    for slot in range(capacity):
        included = jnp.where(seen < lengths[slot], scores[slot] * scaling, masked_score)
        own = jnp.where(own_lane == slot % per_tile * key_heads, own_scores[slot] * scaling, masked_score)
        peak = jnp.maximum(jnp.max(included, axis=1, keepdims=True), jnp.max(own, axis=1, keepdims=True))
        weight, own_weight = jnp.exp(included - peak), jnp.exp(own - peak)
        denominators.append(
            jnp.sum(weight, axis=1, keepdims=True) + jnp.sum(own_weight, axis=1, keepdims=True)
        )
        weights.append(weight.astype(bf16))
        own_weights.append(own_weight.astype(bf16))
    for slot in range(capacity):
        tile = slot // per_tile * TILE
        own_values = block_ref[q_size + new_size + tile : q_size + new_size + tile + TILE, :]
        values = jnp.concatenate([value_ref[page] for page in pages[slot]], axis=0)
        wide = jnp.dot(weights[slot], values, preferred_element_type=f32)
        numerator = jnp.concatenate(
            [
                wide[head * group : (head + 1) * group, head * HEAD_SIZE : (head + 1) * HEAD_SIZE]
                for head in range(key_heads)
            ],
            axis=0,
        ) + jnp.dot(own_weights[slot], own_values, preferred_element_type=f32)
        out_ref[slot * heads : (slot + 1) * heads, :] = (numerator / denominators[slot]).astype(bf16)


def unpack_kernel(capacity, heads, rows, row_ref, probe_ref, *rest):
    answers, (out_ref, reward_ref, gathered) = rest[:-3], rest[-3:]
    for partner, answer in enumerate(answers):
        for slot in range(capacity):
            row = row_ref[partner * capacity + slot]
            gathered[pl.ds(pl.multiple_of(row * heads, heads), heads), :] = answer[
                slot * heads : (slot + 1) * heads, :
            ].astype(f32)
    total = jnp.zeros((rows, HEAD_SIZE), f32)
    for head in range(heads):
        part = gathered[pl.ds(head, rows, stride=heads), :]
        out_ref[:, head * HEAD_SIZE : (head + 1) * HEAD_SIZE] = part.astype(bf16)
        total = total + part * probe_ref[:, head * HEAD_SIZE : (head + 1) * HEAD_SIZE].astype(f32)
    reward_ref[...] = jnp.sum(total.T, axis=0, keepdims=True)


def shards(
    queries,
    fresh_key_rows,
    fresh_value_rows,
    paged_key_store,
    paged_value_store,
    page_table,
    parent_replica,
    parent_slot,
    context_length,
    reward_probe,
):
    replicas = lax.axis_size("replica")
    rows = queries.shape[0]
    capacity = max(2, 2 * rows // replicas)
    heads = queries.shape[1] // HEAD_SIZE
    key_heads = fresh_key_rows.shape[1] // HEAD_SIZE
    q_size, new_size, meta_size = block_rows(capacity, heads, key_heads)
    block_size = q_size + 2 * new_size + meta_size
    vmem, smem = pl.BlockSpec(memory_space=pltpu.VMEM), pl.BlockSpec(memory_space=pltpu.SMEM)
    params = pltpu.CompilerParams(vmem_limit_bytes=16 * 2**20)

    def in_vmem(x):
        return pltpu.with_memory_space_constraint(x, pltpu.VMEM)

    def in_smem(x):
        return pltpu.with_memory_space_constraint(x, pltpu.SMEM)

    given = (
        queries,
        fresh_key_rows,
        fresh_value_rows,
        paged_key_store,
        paged_value_store,
        page_table.T,
        parent_replica[:, 0],
        parent_slot[:, 0],
        context_length,
    )
    packed = pl.pallas_call(
        functools.partial(pack_kernel, capacity),
        out_shape=[pltpu.VMEM((block_size, HEAD_SIZE), bf16)] * replicas
        + [
            pltpu.VMEM(paged_key_store.shape, bf16),
            pltpu.VMEM(paged_value_store.shape, bf16),
            pltpu.SMEM(page_table.shape[::-1], i32),
            pltpu.SMEM((replicas * capacity,), i32),
        ],
        in_specs=[pl.BlockSpec(memory_space=pltpu.HBM)] * len(given),
        out_specs=[vmem] * (replicas + 2) + [smem] * 2,
        scratch_shapes=[
            pltpu.VMEM(queries.shape, bf16),
            pltpu.VMEM(fresh_key_rows.shape, bf16),
            pltpu.VMEM(fresh_value_rows.shape, bf16),
            pltpu.SMEM((rows,), i32),
            pltpu.SMEM((rows,), i32),
            pltpu.SMEM((rows,), i32),
            pltpu.VMEM(((rows + 1) * heads, HEAD_SIZE), f32),
            pltpu.VMEM(((rows + 1) * 2 * key_heads, HEAD_SIZE), f32),
            pltpu.VMEM((new_size, HEAD_SIZE), f32),
            pltpu.VMEM((new_size, HEAD_SIZE), f32),
            pltpu.SMEM((replicas,), i32),
            pltpu.SemaphoreType.DMA((len(given),)),
        ],
        compiler_params=params,
        name="pack",
    )(*[pltpu.with_memory_space_constraint(x, pltpu.HBM) for x in given])
    blocks = packed[:replicas]
    keys, values = map(in_vmem, packed[replicas : replicas + 2])
    table, slot_rows = map(in_smem, packed[replicas + 2 :])

    serve = pl.pallas_call(
        functools.partial(serve_kernel, capacity, heads),
        out_shape=pltpu.VMEM((capacity * heads, HEAD_SIZE), bf16),
        in_specs=[smem, vmem, vmem, vmem],
        out_specs=vmem,
        compiler_params=params,
        cost_estimate=pl.CostEstimate(flops=10**7, bytes_accessed=2 * 10**6, transcendentals=0),
        name="serve",
    )

    def swap(x, partner):
        return lax.ppermute(x, "replica", [(i, i ^ partner) for i in range(replicas)])

    far_first = sorted(range(1, replicas), key=lambda m: (-m.bit_length(), m))
    answers = [None] * replicas
    arrived = {m: swap(blocks[m], m) for m in far_first}
    for m in far_first:
        answers[m] = swap(serve(table, in_vmem(arrived[m]), keys, values), m)
    answers[0] = serve(table, in_vmem(blocks[0]), keys, values)

    attended, partial_reward = pl.pallas_call(
        functools.partial(unpack_kernel, capacity, heads, rows),
        out_shape=[pltpu.VMEM((rows, heads * HEAD_SIZE), bf16), pltpu.VMEM((1, rows), f32)],
        in_specs=[smem] + [vmem] * (replicas + 1),
        out_specs=[vmem] * 2,
        scratch_shapes=[pltpu.VMEM(((rows + 1) * heads, HEAD_SIZE), f32)],
        compiler_params=params,
        name="unpack",
    )(slot_rows, in_vmem(reward_probe.reshape(1, -1)), *[in_vmem(x) for x in answers])
    other_half = lax.ppermute(partial_reward, "tensor", [(0, 1), (1, 0)])
    return attended, (partial_reward + other_half)[0]


def solution(mesh):
    placed = (
        P(("groups", "replica"), "tensor"),
        P(("groups", "replica"), "tensor"),
        P(("groups", "replica"), "tensor"),
        P(("groups", "replica"), None, "tensor"),
        P(("groups", "replica"), None, "tensor"),
        P(("groups", "replica"), None),
        P(("groups", "replica"), None),
        P(("groups", "replica"), None),
        P(("groups", "replica")),
        P("tensor"),
    )
    return jax.shard_map(
        shards,
        mesh=mesh,
        in_specs=placed,
        out_specs=(P(("groups", "replica"), "tensor"), P(("groups", "replica"))),
        check_vma=False,
    )
```

time: 105 us -> 43.2 us (0.41)
  Pallas kernels: 68.3 us -> 8.2 us
  local copies, waits for them, and re-layouts: 8.38 us -> 0.72 us
  waiting for transfers between devices: 0.04 us -> 7.11 us
  blocking collectives: 2.95 us -> 0 us
  starting transfers between devices: 23.8 us -> 25.7 us
    pallas_call x8, Pallas kernels: 64.6 us -> 5.27 us  [the longest x7 4.61 us: shards(): answers[m] = swap(serve(table, in_vmem(arrived[m]), keys, values), m)]
    unnamed x21 -> x3, local copies, waits for them, and re-layouts: 8.37 us -> 0.71 us
    ppermute x14, waiting for transfers between devices: 0.04 us -> 6.71 us  [swap(): lax.ppermute(x, 'replica', [(i, i ^ partner) for i in range(replicas)])]
    psum x1 -> x0, blocking collectives: 2.95 us -> none  [shards(): return (attended, lax.psum(partial_reward[0], 'tensor'))]
    ppermute x14, starting transfers between devices: 23.8 us -> 25.7 us  [swap(): lax.ppermute(x, 'replica', [(i, i ^ partner) for i in range(replicas)])]
    pallas_call x1, Pallas kernels: 1.65 us -> 0.48 us  [shards(): pl.pallas_call(functools.partial(unpack_kernel, capacity, heads, rows), o...]
  transfers between devices with their start and end apart: 14 -> 15, of which waited for: 0 -> 4; matrix products, arithmetic and copies ran while one was open for 1% -> 2% of each run, Pallas kernels for 62% -> 12%
where the time goes in v2:
time: 43.2 us; the launch traced here: 43 us
  starting transfers between devices  25.7 us (59%)
  Pallas kernels  8.2 us (19%)
  waiting for transfers between devices  7.11 us (16%)
  between operations  0.77 us (2%)
  local copies, waits for them, and re-layouts  0.72 us (2%)
  other arithmetic  0.51 us (1%)
    ppermute x14, starting transfers between devices, swap(): lax.ppermute(x, 'replica', [(i, i ^ partner) for i in range(replicas)])  25.7 us
    ppermute x14, waiting for transfers between devices, swap(): lax.ppermute(x, 'replica', [(i, i ^ partner) for i in range(replicas)])  6.71 us
    pallas_call x7, Pallas kernels, shards(): answers[m] = swap(serve(table, in_vmem(arrived[m]), keys, values), m)  4.61 us
    pallas_call x1, Pallas kernels, shards(): pl.pallas_call(functools.partial(pack_kernel, capacity), out_shape=[pltpu...  2.45 us
  transfers between devices with their start and end apart: 15, of which 4 were waited for; matrix products, arithmetic and copies ran while one was open for 2% of the time, Pallas kernels for 12%

profile of v2, /device:TPU:0, one launch (start us, length us, event | category | flops | bytes accessed | tf_op | source)
XLA Modules:
  0.0 43.0 jit_solution(12852646142529903739)
XLA Ops:
  0.6 2.5 %pack.1 = (bf16[336,128]{1,0:T(8,128)(2,1)S(1)}, bf16[336,128]{1,0:T(8,128)(2,1)S(1)}, bf16[336,128]{1,0:T(8,128)(2,1)S(1)}, bf16[336,128]{1,0:T(8,128)(2,1)S(1)...) custom-call(bf16[32,4096]{1,0:T(8,128)(2,1)} %q_hbm.1, ...), custom_call_target="tpu_custom_call" | custom-call | tf_op jit(solution)/shard_map/pack/pallas_call | solution.py:218
  3.1 3.0 %collective-permute-start = (bf16[336,128]{1,0:T(8,128)(2,1)S(1)}, bf16[336,128]{1,0:T(8,128)(2,1)S(1)}, u32[]{:S(2)}, u32[]{:S(2)}) collective-permute-start(bf16[336,128]{1,0:T(8,128)(2,1)S(1)} %get-tuple-element.21), channel_id=1, source_target_pairs={{0,2},{2,0},{4,6},{6,4},{8,10},{10,8},{12,14},{14,12},{1,3},{3,1},... | collective-permute-start | bytes 258056 | tf_op jit(solution)/shard_map/ppermute | solution.py:261
  6.1 1.6 %collective-permute-start.2 = (bf16[336,128]{1,0:T(8,128)(2,1)S(1)}, bf16[336,128]{1,0:T(8,128)(2,1)S(1)}, u32[]{:S(2)}, u32[]{:S(2)}) collective-permute-start(bf16[336,128]{1,0:T(8,128)(2,1)S(1)} %get-tuple-element.22), channel_id=1, source_target_pairs={{0,4},{2,6},{4,0},{6,2},{8,12},{10,14},{12,8},{14,10},{1,5},{3,7},... | collective-permute-start | bytes 258056 | tf_op jit(solution)/shard_map/ppermute | solution.py:261
  7.7 0.0 collective-permute-start.4
  7.7 3.0 %collective-permute-start.6 = (bf16[336,128]{1,0:T(8,128)(2,1)S(1)}, bf16[336,128]{1,0:T(8,128)(2,1)S(1)}, u32[]{:S(2)}, u32[]{:S(2)}) collective-permute-start(bf16[336,128]{1,0:T(8,128)(2,1)S(1)} %get-tuple-element.24), channel_id=1, source_target_pairs={{0,8},{2,10},{4,12},{6,14},{8,0},{10,2},{12,4},{14,6},{1,9},{3,11}... | collective-permute-start | bytes 258056 | tf_op jit(solution)/shard_map/ppermute | solution.py:261
  10.7 1.3 %collective-permute-start.8 = (bf16[336,128]{1,0:T(8,128)(2,1)S(1)}, bf16[336,128]{1,0:T(8,128)(2,1)S(1)}, u32[]{:S(2)}, u32[]{:S(2)}) collective-permute-start(bf16[336,128]{1,0:T(8,128)(2,1)S(1)} %get-tuple-element.25), channel_id=1, source_target_pairs={{0,10},{2,8},{4,14},{6,12},{8,2},{10,0},{12,6},{14,4},{1,11},{3,9}... | collective-permute-start | bytes 258056 | tf_op jit(solution)/shard_map/ppermute | solution.py:261
  12.0 0.0 collective-permute-done.block_ref
  12.0 3.6 %collective-permute-start.10 = (bf16[336,128]{1,0:T(8,128)(2,1)S(1)}, bf16[336,128]{1,0:T(8,128)(2,1)S(1)}, u32[]{:S(2)}, u32[]{:S(2)}) collective-permute-start(bf16[336,128]{1,0:T(8,128)(2,1)S(1)} %get-tuple-element.26), channel_id=1, source_target_pairs={{0,12},{2,14},{4,8},{6,10},{8,4},{10,6},{12,0},{14,2},{1,13},{3,15... | collective-permute-start | bytes 258056 | tf_op jit(solution)/shard_map/ppermute | solution.py:261
  15.6 0.0 collective-permute-done.2.block_ref
  15.6 0.0 collective-permute-start.12
  15.6 0.7 %serve.9 = bf16[256,128]{1,0:T(8,128)(2,1)S(1)} custom-call(s32[4,32]{1,0:T(4,128)S(4)} %get-tuple-element.17.table_ref, bf16[336,128]{1,0:T(8,128)(2,1)S(1)} %collective-permute-done.block_ref, bf16[128,16,512]{2,1,0:T(8,128)(2,1)S(1)} %get-tuple-element.19.key_ref, bf16[128,16,512]{2,1,0:T(8,128)(2,1)S(1)} %get-tuple-element.20.value_ref), custom_call_target="tpu_custom_call" | custom-call | flops 10000000 | bytes 2000000 | tf_op jit(solution)/shard_map/serve/pallas_call | solution.py:267
  16.3 0.7 %serve.10 = bf16[256,128]{1,0:T(8,128)(2,1)S(1)} custom-call(s32[4,32]{1,0:T(4,128)S(4)} %get-tuple-element.17.table_ref, bf16[336,128]{1,0:T(8,128)(2,1)S(1)} %collective-permute-done.2.block_ref, bf16[128,16,512]{2,1,0:T(8,128)(2,1)S(1)} %get-tuple-element.19.key_ref, bf16[128,16,512]{2,1,0:T(8,128)(2,1)S(1)} %get-tuple-element.20.value_ref), custom_call_target="tpu_custom_call" | custom-call | flops 10000000 | bytes 2000000 | tf_op jit(solution)/shard_map/serve/pallas_call | solution.py:267
  16.9 0.0 collective-permute-done.4.block_ref
  16.9 1.7 %collective-permute-start.1 = (bf16[256,128]{1,0:T(8,128)(2,1)S(1)}, bf16[256,128]{1,0:T(8,128)(2,1)S(1)}, u32[]{:S(2)}, u32[]{:S(2)}) collective-permute-start(bf16[256,128]{1,0:T(8,128)(2,1)S(1)} %serve.9), channel_id=1, source_target_pairs={{0,2},{2,0},{4,6},{6,4},{8,10},{10,8},{12,14},{14,12},{1,3},{3,1},... | collective-permute-start | bytes 196616 | tf_op jit(solution)/shard_map/ppermute | solution.py:261
  18.7 0.0 collective-permute-done.6.block_ref
  18.7 2.9 %collective-permute-start.3 = (bf16[256,128]{1,0:T(8,128)(2,1)S(1)}, bf16[256,128]{1,0:T(8,128)(2,1)S(1)}, u32[]{:S(2)}, u32[]{:S(2)}) collective-permute-start(bf16[256,128]{1,0:T(8,128)(2,1)S(1)} %serve.10), channel_id=1, source_target_pairs={{0,4},{2,6},{4,0},{6,2},{8,12},{10,14},{12,8},{14,10},{1,5},{3,7},... | collective-permute-start | bytes 196616 | tf_op jit(solution)/shard_map/ppermute | solution.py:261
  21.6 0.7 %serve.11 = bf16[256,128]{1,0:T(8,128)(2,1)S(1)} custom-call(s32[4,32]{1,0:T(4,128)S(4)} %get-tuple-element.17.table_ref, bf16[336,128]{1,0:T(8,128)(2,1)S(1)} %collective-permute-done.4.block_ref, bf16[128,16,512]{2,1,0:T(8,128)(2,1)S(1)} %get-tuple-element.19.key_ref, bf16[128,16,512]{2,1,0:T(8,128)(2,1)S(1)} %get-tuple-element.20.value_ref), custom_call_target="tpu_custom_call" | custom-call | flops 10000000 | bytes 2000000 | tf_op jit(solution)/shard_map/serve/pallas_call | solution.py:267
  22.3 0.7 %serve.12 = bf16[256,128]{1,0:T(8,128)(2,1)S(1)} custom-call(s32[4,32]{1,0:T(4,128)S(4)} %get-tuple-element.17.table_ref, bf16[336,128]{1,0:T(8,128)(2,1)S(1)} %collective-permute-done.6.block_ref, bf16[128,16,512]{2,1,0:T(8,128)(2,1)S(1)} %get-tuple-element.19.key_ref, bf16[128,16,512]{2,1,0:T(8,128)(2,1)S(1)} %get-tuple-element.20.value_ref), custom_call_target="tpu_custom_call" | custom-call | flops 10000000 | bytes 2000000 | tf_op jit(solution)/shard_map/serve/pallas_call | solution.py:267
  22.9 1.6 %collective-permute-done.8.block_ref = bf16[336,128]{1,0:T(8,128)(2,1)S(1)} collective-permute-done((bf16[336,128]{1,0:T(8,128)(2,1)S(1)}, bf16[336,128]{1,0:T(8,128)(2,1)S(1)}, u32[]{:S(2)}, u32[]{:S(2)}) %collective-permute-start.8) | collective-permute-done | bytes 86048 | tf_op jit(solution)/shard_map/ppermute | solution.py:261
  24.5 0.7 %collective-permute-start.5 = (bf16[256,128]{1,0:T(8,128)(2,1)S(1)}, bf16[256,128]{1,0:T(8,128)(2,1)S(1)}, u32[]{:S(2)}, u32[]{:S(2)}) collective-permute-start(bf16[256,128]{1,0:T(8,128)(2,1)S(1)} %serve.11), channel_id=1, source_target_pairs={{0,6},{2,4},{4,2},{6,0},{8,14},{10,12},{12,10},{14,8},{1,7},{3,5},... | collective-permute-start | bytes 196616 | tf_op jit(solution)/shard_map/ppermute | solution.py:261
  25.2 0.7 %serve.13 = bf16[256,128]{1,0:T(8,128)(2,1)S(1)} custom-call(s32[4,32]{1,0:T(4,128)S(4)} %get-tuple-element.17.table_ref, bf16[336,128]{1,0:T(8,128)(2,1)S(1)} %collective-permute-done.8.block_ref, bf16[128,16,512]{2,1,0:T(8,128)(2,1)S(1)} %get-tuple-element.19.key_ref, bf16[128,16,512]{2,1,0:T(8,128)(2,1)S(1)} %get-tuple-element.20.value_ref), custom_call_target="tpu_custom_call" | custom-call | flops 10000000 | bytes 2000000 | tf_op jit(solution)/shard_map/serve/pallas_call | solution.py:267
  25.9 0.0 collective-permute-done.10.block_ref
  25.9 2.6 %collective-permute-start.7 = (bf16[256,128]{1,0:T(8,128)(2,1)S(1)}, bf16[256,128]{1,0:T(8,128)(2,1)S(1)}, u32[]{:S(2)}, u32[]{:S(2)}) collective-permute-start(bf16[256,128]{1,0:T(8,128)(2,1)S(1)} %serve.12), channel_id=1, source_target_pairs={{0,8},{2,10},{4,12},{6,14},{8,0},{10,2},{12,4},{14,6},{1,9},{3,11}... | collective-permute-start | bytes 196616 | tf_op jit(solution)/shard_map/ppermute | solution.py:261
  28.5 0.7 %serve.14 = bf16[256,128]{1,0:T(8,128)(2,1)S(1)} custom-call(s32[4,32]{1,0:T(4,128)S(4)} %get-tuple-element.17.table_ref, bf16[336,128]{1,0:T(8,128)(2,1)S(1)} %collective-permute-done.10.block_ref, bf16[128,16,512]{2,1,0:T(8,128)(2,1)S(1)} %get-tuple-element.19.key_ref, bf16[128,16,512]{2,1,0:T(8,128)(2,1)S(1)} %get-tuple-element.20.value_ref), custom_call_target="tpu_custom_call" | custom-call | flops 10000000 | bytes 2000000 | tf_op jit(solution)/shard_map/serve/pallas_call | solution.py:267
  29.1 0.0 copy-start
  29.1 0.0 collective-permute-done.12.block_ref
  29.1 0.5 %collective-permute-start.9 = (bf16[256,128]{1,0:T(8,128)(2,1)S(1)}, bf16[256,128]{1,0:T(8,128)(2,1)S(1)}, u32[]{:S(2)}, u32[]{:S(2)}) collective-permute-start(bf16[256,128]{1,0:T(8,128)(2,1)S(1)} %serve.13), channel_id=1, source_target_pairs={{0,10},{2,8},{4,14},{6,12},{8,2},{10,0},{12,6},{14,4},{1,11},{3,9}... | collective-permute-start | bytes 196616 | tf_op jit(solution)/shard_map/ppermute | solution.py:261
  29.7 0.7 %serve.15 = bf16[256,128]{1,0:T(8,128)(2,1)S(1)} custom-call(s32[4,32]{1,0:T(4,128)S(4)} %get-tuple-element.17.table_ref, bf16[336,128]{1,0:T(8,128)(2,1)S(1)} %collective-permute-done.12.block_ref, bf16[128,16,512]{2,1,0:T(8,128)(2,1)S(1)} %get-tuple-element.19.key_ref, bf16[128,16,512]{2,1,0:T(8,128)(2,1)S(1)} %get-tuple-element.20.value_ref), custom_call_target="tpu_custom_call" | custom-call | flops 10000000 | bytes 2000000 | tf_op jit(solution)/shard_map/serve/pallas_call | solution.py:267
  30.3 0.0 collective-permute-done.1.rest_1_
  30.3 3.5 %collective-permute-start.11 = (bf16[256,128]{1,0:T(8,128)(2,1)S(1)}, bf16[256,128]{1,0:T(8,128)(2,1)S(1)}, u32[]{:S(2)}, u32[]{:S(2)}) collective-permute-start(bf16[256,128]{1,0:T(8,128)(2,1)S(1)} %serve.14), channel_id=1, source_target_pairs={{0,12},{2,14},{4,8},{6,10},{8,4},{10,6},{12,0},{14,2},{1,13},{3,15... | collective-permute-start | bytes 196616 | tf_op jit(solution)/shard_map/ppermute | solution.py:261
  33.9 0.0 collective-permute-done.3.rest_2_
  33.9 1.2 %collective-permute-start.13 = (bf16[256,128]{1,0:T(8,128)(2,1)S(1)}, bf16[256,128]{1,0:T(8,128)(2,1)S(1)}, u32[]{:S(2)}, u32[]{:S(2)}) collective-permute-start(bf16[256,128]{1,0:T(8,128)(2,1)S(1)} %serve.15), channel_id=1, source_target_pairs={{0,14},{2,12},{4,10},{6,8},{8,6},{10,4},{12,2},{14,0},{1,15},{3,13... | collective-permute-start | bytes 196616 | tf_op jit(solution)/shard_map/ppermute | solution.py:261
  35.1 0.0 copy-done
  35.1 0.7 %serve.8.rest_0_ = bf16[256,128]{1,0:T(8,128)(2,1)S(1)} custom-call(s32[4,32]{1,0:T(4,128)S(4)} %get-tuple-element.17.table_ref, bf16[336,128]{1,0:T(8,128)(2,1)S(1)} %get-tuple-element.18.block_ref, bf16[128,16,512]{2,1,0:T(8,128)(2,1)S(1)} %get-tuple-element.19.key_ref, bf16[128,16,512]{2,1,0:T(8,128)(2,1)S(1)} %get-tuple-element.20.value_ref), custom_call_target="tpu_custom_call" | custom-call | flops 10000000 | bytes 2000000 | tf_op jit(solution)/shard_map/serve/pallas_call | solution.py:268
  35.8 0.0 collective-permute-done.5.rest_3_
  35.8 0.0 collective-permute-done.7.rest_4_
  35.8 2.7 %collective-permute-done.9.rest_5_ = bf16[256,128]{1,0:T(8,128)(2,1)S(1)} collective-permute-done((bf16[256,128]{1,0:T(8,128)(2,1)S(1)}, bf16[256,128]{1,0:T(8,128)(2,1)S(1)}, u32[]{:S(2)}, u32[]{:S(2)}) %collective-permute-start.9) | collective-permute-done | bytes 65568 | tf_op jit(solution)/shard_map/ppermute | solution.py:261
  38.5 0.0 collective-permute-done.11.rest_6_
  38.5 2.4 %collective-permute-done.13.rest_7_ = bf16[256,128]{1,0:T(8,128)(2,1)S(1)} collective-permute-done((bf16[256,128]{1,0:T(8,128)(2,1)S(1)}, bf16[256,128]{1,0:T(8,128)(2,1)S(1)}, u32[]{:S(2)}, u32[]{:S(2)}) %collective-permute-start.13) | collective-permute-done | bytes 65568 | tf_op jit(solution)/shard_map/ppermute | solution.py:261
  40.9 0.5 %unpack.1 = (bf16[32,4096]{1,0:T(8,128)(2,1)S(1)}, f32[1,32]{1,0:T(1,128)S(1)}) custom-call(s32[64]{0:T(128)S(4)} %get-tuple-element.16.row_ref, bf16[1,4096]{1,0:T(2,128)(2,1)S(1)} %reshape.7.probe_ref, bf16[256,128]{1,0:T(8,128)(2,1)S(1)} %serve.8.rest_0_, bf16[256,128]{1,0:T(8,128)(2,1)S(1)} %collective-permute-done.1.rest_1_, ...), custom_call_target="tpu_custom_call" | custom-call | tf_op jit(solution)/shard_map/unpack/pallas_call | solution.py:270
  41.3 0.1 collective-permute-start.14
  41.4 0.7 %copy.12 = bf16[32,4096]{1,0:T(8,128)(2,1)} copy(bf16[32,4096]{1,0:T(8,128)(2,1)S(1)} %get-tuple-element.30) | data formatting | bytes 524288
  42.1 0.4 collective-permute-done.14
  42.5 0.5 %add_bitcast_fusion = f32[32]{0:T(128)} fusion(f32[1,32]{1,0:T(1,128)S(1)} %get-tuple-element.29, f32[1,32]{1,0:T(1,128)S(1)} %collective-permute-done.14), kind=kLoop, calls=%fused_computation | loop fusion | flops 32 | bytes 384 | tf_op jit(solution)/shard_map/squeeze | solution.py:280
  (1 shorter events, 0.0 us)
Async XLA Ops:
  3.1 8.9 %collective-permute-start = (bf16[336,128]{1,0:T(8,128)(2,1)S(1)}, bf16[336,128]{1,0:T(8,128)(2,1)S(1)}, u32[]{:S(2)}, u32[]{:S(2)}) collective-permute-start(bf16[336,128]{1,0:T(8,128)(2,1)S(1)} %get-tuple-element.21), channel_id=1, source_target_pairs={{0,2},{2,0},{4,6},{6,4},{8,10},{10,8},{12,14},{14,12},{1,3},{3,1},... | collective-permute-start | bytes 258056 | tf_op jit(solution)/shard_map/ppermute | solution.py:261
  6.1 9.5 %collective-permute-start.2 = (bf16[336,128]{1,0:T(8,128)(2,1)S(1)}, bf16[336,128]{1,0:T(8,128)(2,1)S(1)}, u32[]{:S(2)}, u32[]{:S(2)}) collective-permute-start(bf16[336,128]{1,0:T(8,128)(2,1)S(1)} %get-tuple-element.22), channel_id=1, source_target_pairs={{0,4},{2,6},{4,0},{6,2},{8,12},{10,14},{12,8},{14,10},{1,5},{3,7},... | collective-permute-start | bytes 258056 | tf_op jit(solution)/shard_map/ppermute | solution.py:261
  7.7 9.2 %collective-permute-start.4 = (bf16[336,128]{1,0:T(8,128)(2,1)S(1)}, bf16[336,128]{1,0:T(8,128)(2,1)S(1)}, u32[]{:S(2)}, u32[]{:S(2)}) collective-permute-start(bf16[336,128]{1,0:T(8,128)(2,1)S(1)} %get-tuple-element.23), channel_id=1, source_target_pairs={{0,6},{2,4},{4,2},{6,0},{8,14},{10,12},{12,10},{14,8},{1,7},{3,5},... | collective-permute-start | bytes 258056 | tf_op jit(solution)/shard_map/ppermute | solution.py:261
  7.7 11.0 %collective-permute-start.6 = (bf16[336,128]{1,0:T(8,128)(2,1)S(1)}, bf16[336,128]{1,0:T(8,128)(2,1)S(1)}, u32[]{:S(2)}, u32[]{:S(2)}) collective-permute-start(bf16[336,128]{1,0:T(8,128)(2,1)S(1)} %get-tuple-element.24), channel_id=1, source_target_pairs={{0,8},{2,10},{4,12},{6,14},{8,0},{10,2},{12,4},{14,6},{1,9},{3,11}... | collective-permute-start | bytes 258056 | tf_op jit(solution)/shard_map/ppermute | solution.py:261
  10.7 13.9 %collective-permute-start.8 = (bf16[336,128]{1,0:T(8,128)(2,1)S(1)}, bf16[336,128]{1,0:T(8,128)(2,1)S(1)}, u32[]{:S(2)}, u32[]{:S(2)}) collective-permute-start(bf16[336,128]{1,0:T(8,128)(2,1)S(1)} %get-tuple-element.25), channel_id=1, source_target_pairs={{0,10},{2,8},{4,14},{6,12},{8,2},{10,0},{12,6},{14,4},{1,11},{3,9}... | collective-permute-start | bytes 258056 | tf_op jit(solution)/shard_map/ppermute | solution.py:261
  12.0 13.9 %collective-permute-start.10 = (bf16[336,128]{1,0:T(8,128)(2,1)S(1)}, bf16[336,128]{1,0:T(8,128)(2,1)S(1)}, u32[]{:S(2)}, u32[]{:S(2)}) collective-permute-start(bf16[336,128]{1,0:T(8,128)(2,1)S(1)} %get-tuple-element.26), channel_id=1, source_target_pairs={{0,12},{2,14},{4,8},{6,10},{8,4},{10,6},{12,0},{14,2},{1,13},{3,15... | collective-permute-start | bytes 258056 | tf_op jit(solution)/shard_map/ppermute | solution.py:261
  15.6 13.6 %collective-permute-start.12 = (bf16[336,128]{1,0:T(8,128)(2,1)S(1)}, bf16[336,128]{1,0:T(8,128)(2,1)S(1)}, u32[]{:S(2)}, u32[]{:S(2)}) collective-permute-start(bf16[336,128]{1,0:T(8,128)(2,1)S(1)} %get-tuple-element.27), channel_id=1, source_target_pairs={{0,14},{2,12},{4,10},{6,8},{8,6},{10,4},{12,2},{14,0},{1,15},{3,13... | collective-permute-start | bytes 258056 | tf_op jit(solution)/shard_map/ppermute | solution.py:261
  16.9 13.4 %collective-permute-start.1 = (bf16[256,128]{1,0:T(8,128)(2,1)S(1)}, bf16[256,128]{1,0:T(8,128)(2,1)S(1)}, u32[]{:S(2)}, u32[]{:S(2)}) collective-permute-start(bf16[256,128]{1,0:T(8,128)(2,1)S(1)} %serve.9), channel_id=1, source_target_pairs={{0,2},{2,0},{4,6},{6,4},{8,10},{10,8},{12,14},{14,12},{1,3},{3,1},... | collective-permute-start | bytes 196616 | tf_op jit(solution)/shard_map/ppermute | solution.py:261
  18.7 15.2 %collective-permute-start.3 = (bf16[256,128]{1,0:T(8,128)(2,1)S(1)}, bf16[256,128]{1,0:T(8,128)(2,1)S(1)}, u32[]{:S(2)}, u32[]{:S(2)}) collective-permute-start(bf16[256,128]{1,0:T(8,128)(2,1)S(1)} %serve.10), channel_id=1, source_target_pairs={{0,4},{2,6},{4,0},{6,2},{8,12},{10,14},{12,8},{14,10},{1,5},{3,7},... | collective-permute-start | bytes 196616 | tf_op jit(solution)/shard_map/ppermute | solution.py:261
  24.5 11.2 %collective-permute-start.5 = (bf16[256,128]{1,0:T(8,128)(2,1)S(1)}, bf16[256,128]{1,0:T(8,128)(2,1)S(1)}, u32[]{:S(2)}, u32[]{:S(2)}) collective-permute-start(bf16[256,128]{1,0:T(8,128)(2,1)S(1)} %serve.11), channel_id=1, source_target_pairs={{0,6},{2,4},{4,2},{6,0},{8,14},{10,12},{12,10},{14,8},{1,7},{3,5},... | collective-permute-start | bytes 196616 | tf_op jit(solution)/shard_map/ppermute | solution.py:261
  25.9 9.9 %collective-permute-start.7 = (bf16[256,128]{1,0:T(8,128)(2,1)S(1)}, bf16[256,128]{1,0:T(8,128)(2,1)S(1)}, u32[]{:S(2)}, u32[]{:S(2)}) collective-permute-start(bf16[256,128]{1,0:T(8,128)(2,1)S(1)} %serve.12), channel_id=1, source_target_pairs={{0,8},{2,10},{4,12},{6,14},{8,0},{10,2},{12,4},{14,6},{1,9},{3,11}... | collective-permute-start | bytes 196616 | tf_op jit(solution)/shard_map/ppermute | solution.py:261
  29.1 6.0 %copy-start = (bf16[4096]{0:T(1024)(128)(2,1)S(1)}, bf16[4096]{0:T(1024)(128)(2,1)}, u32[]{:S(2)}) copy-start(bf16[4096]{0:T(1024)(128)(2,1)} %param.19) | copy-start | bytes 24580
  29.1 9.3 %collective-permute-start.9 = (bf16[256,128]{1,0:T(8,128)(2,1)S(1)}, bf16[256,128]{1,0:T(8,128)(2,1)S(1)}, u32[]{:S(2)}, u32[]{:S(2)}) collective-permute-start(bf16[256,128]{1,0:T(8,128)(2,1)S(1)} %serve.13), channel_id=1, source_target_pairs={{0,10},{2,8},{4,14},{6,12},{8,2},{10,0},{12,6},{14,4},{1,11},{3,9}... | collective-permute-start | bytes 196616 | tf_op jit(solution)/shard_map/ppermute | solution.py:261
  30.3 8.1 %collective-permute-start.11 = (bf16[256,128]{1,0:T(8,128)(2,1)S(1)}, bf16[256,128]{1,0:T(8,128)(2,1)S(1)}, u32[]{:S(2)}, u32[]{:S(2)}) collective-permute-start(bf16[256,128]{1,0:T(8,128)(2,1)S(1)} %serve.14), channel_id=1, source_target_pairs={{0,12},{2,14},{4,8},{6,10},{8,4},{10,6},{12,0},{14,2},{1,13},{3,15... | collective-permute-start | bytes 196616 | tf_op jit(solution)/shard_map/ppermute | solution.py:261
  33.9 7.0 %collective-permute-start.13 = (bf16[256,128]{1,0:T(8,128)(2,1)S(1)}, bf16[256,128]{1,0:T(8,128)(2,1)S(1)}, u32[]{:S(2)}, u32[]{:S(2)}) collective-permute-start(bf16[256,128]{1,0:T(8,128)(2,1)S(1)} %serve.15), channel_id=1, source_target_pairs={{0,14},{2,12},{4,10},{6,8},{8,6},{10,4},{12,2},{14,0},{1,15},{3,13... | collective-permute-start | bytes 196616 | tf_op jit(solution)/shard_map/ppermute | solution.py:261
  41.3 1.2 %collective-permute-start.14 = (f32[1,32]{1,0:T(1,128)S(1)}, f32[1,32]{1,0:T(1,128)S(1)}, u32[]{:S(2)}, u32[]{:S(2)}) collective-permute-start(f32[1,32]{1,0:T(1,128)S(1)} %get-tuple-element.29), channel_id=1, source_target_pairs={{0,1},{1,0},{2,3},{3,2},{4,5},{5,4},{6,7},{7,6},{8,9},{9,8},{10,11... | collective-permute-start | bytes 392 | tf_op jit(solution)/shard_map/ppermute | solution.py:279

commit v3 on v2

--- a/solution.py
+++ b/solution.py
@@ -9,6 +9,7 @@
 
 HEAD_SIZE = 128
 TILE = 16
+TOGETHER = 2
 masked_score = -1e30
 f32, bf16, i32 = jnp.float32, jnp.bfloat16, jnp.int32
 
@@ -22,14 +23,22 @@
     return capacity * heads, new_rows, round_up(capacity, TILE)
 
 
+def partners_in_turn(replicas):
+    near, far = list(range(1, replicas // 2)), list(range(replicas // 2, replicas))
+    pairs = list(zip(far, near))
+    even = [m for pair in pairs for m in pair] + far[len(near) :] + [0]
+    odd = [m for pair in pairs for m in pair[::-1]] + far[len(near) :] + [0]
+    return even, odd
+
+
 def pack_kernel(
-    capacity, q_hbm, k_hbm, v_hbm, key_hbm, value_hbm, table_hbm, source_hbm, parent_hbm, length_hbm, *rest
+    capacity, turns, q_hbm, k_hbm, v_hbm, key_hbm, value_hbm, table_hbm, source_hbm, parent_hbm, length_hbm, *rest
 ):
-    replicas = len(rest) - 16
+    replicas = len(rest) - 17
     blocks = rest[:replicas]
     keys_ref, values_ref, table_ref, row_ref = rest[replicas : replicas + 4]
     q_ref, k_ref, v_ref, source_ref, parent_ref, length_ref = rest[replicas + 4 : replicas + 10]
-    q_rows, new_rows, new_keys, new_values, taken, arrived = rest[replicas + 10 :]
+    q_rows, new_rows, new_keys, new_values, taken, turn_ref, arrived = rest[replicas + 10 :]
     copies = [
         pltpu.make_async_copy(source, target, arrived.at[i])
         for i, (source, target) in enumerate(
@@ -53,8 +62,11 @@
     me = lax.axis_index("replica")
     for slot in range(replicas * capacity):
         row_ref[slot] = rows
+    odd = lax.rem(lax.axis_index("tensor"), 2)
     for replica in range(replicas):
         taken[replica] = 0
+        even_turn, odd_turn = (turn.index(replica) for turn in turns)
+        turn_ref[replica] = jnp.where(odd == 1, odd_turn, even_turn)
     q_rows[rows * heads :, :] = jnp.zeros((heads, HEAD_SIZE), f32)
     new_rows[rows * 2 * key_heads :, :] = jnp.zeros((2 * key_heads, HEAD_SIZE), f32)
     q_size, new_size, meta_size = block_rows(capacity, heads, key_heads)
@@ -66,7 +78,7 @@
         source = source_ref[row]
         rank = taken[source]
         taken[source] = rank + 1
-        row_ref[(source ^ me) * capacity + rank] = row
+        row_ref[turn_ref[source ^ me] * capacity + rank] = row
     for copy in copies[1:6]:
         copy.wait()
     for head in range(heads):
@@ -100,7 +112,9 @@
         copy.wait()
 
 
-def serve_kernel(capacity, heads, table_ref, block_ref, key_ref, value_ref, out_ref):
+def serve_kernel(capacity, heads, table_ref, key_ref, value_ref, *blocks_and_answers):
+    number = len(blocks_and_answers) // 2
+    blocks, answers = blocks_and_answers[:number], blocks_and_answers[number:]
     pages_per_row, rows = table_ref.shape
     positions, width = key_ref.shape[1:]
     key_heads = width // HEAD_SIZE
@@ -109,35 +123,35 @@
     scaling = 1.0 / HEAD_SIZE**0.5
     q_size, new_size, meta_size = block_rows(capacity, heads, key_heads)
     per_tile = TILE // key_heads
+    slots = [(n, slot) for n in range(number) for slot in range(capacity)]
 
     def iota(shape, axis):
         return lax.broadcasted_iota(i32, shape, axis)
 
-    meta = block_ref[q_size + 2 * new_size :, :].astype(f32)
-    at_row, at_lane = iota(meta.shape, 0), iota(meta.shape, 1)
-    coded = jnp.where(at_lane == 0, meta, jnp.where(at_lane == 1, meta * rows, 0.0))
-    codes = [jnp.sum(jnp.where(at_row == slot, coded, 0.0)) for slot in range(capacity)]
-    codes = [code.astype(i32) for code in codes]
+    at_row, at_lane = iota((meta_size, HEAD_SIZE), 0), iota((meta_size, HEAD_SIZE), 1)
+    metas = [block[q_size + 2 * new_size :, :].astype(f32) for block in blocks]
+    coded = [jnp.where(at_lane == 0, meta, jnp.where(at_lane == 1, meta * rows, 0.0)) for meta in metas]
+    codes = [jnp.sum(jnp.where(at_row == slot, coded[n], 0.0)).astype(i32) for n, slot in slots]
     lengths = [code // rows for code in codes]
     parents = [code - length * rows for code, length in zip(codes, lengths)]
     pages = [[table_ref[i, parent] for i in range(pages_per_row)] for parent in parents]
     diagonal = iota((heads, width), 0) // group == iota((heads, width), 1) // HEAD_SIZE
     own_lane = iota((heads, TILE), 1) - iota((heads, TILE), 0) // group
     seen = iota((heads, span), 1)
+    by_lanes = (((1,), (1,)), ((), ()))
     scores, own_scores = [], []
-    for slot in range(capacity):
-        tile = slot // per_tile * TILE
-        own_keys = block_ref[q_size + tile : q_size + tile + TILE, :]
-        q_slot = block_ref[slot * heads : (slot + 1) * heads, :]
-        keys = jnp.concatenate([key_ref[page] for page in pages[slot]], axis=0)
+    for (n, slot), found in zip(slots, pages):
+        tile = q_size + slot // per_tile * TILE
+        own_keys = blocks[n][tile : tile + TILE, :]
+        q_slot = blocks[n][slot * heads : (slot + 1) * heads, :]
+        keys = jnp.concatenate([key_ref[page] for page in found], axis=0)
         spread = jnp.where(diagonal, jnp.concatenate([q_slot] * key_heads, axis=1), jnp.zeros((), bf16))
-        by_lanes = (((1,), (1,)), ((), ()))
         scores.append(lax.dot_general(spread, keys, by_lanes, preferred_element_type=f32))
         own_scores.append(lax.dot_general(q_slot, own_keys, by_lanes, preferred_element_type=f32))
     weights, own_weights, denominators = [], [], []
-    for slot in range(capacity):
-        included = jnp.where(seen < lengths[slot], scores[slot] * scaling, masked_score)
-        own = jnp.where(own_lane == slot % per_tile * key_heads, own_scores[slot] * scaling, masked_score)
+    for (_, slot), length, score, own_score in zip(slots, lengths, scores, own_scores):
+        included = jnp.where(seen < length, score * scaling, masked_score)
+        own = jnp.where(own_lane == slot % per_tile * key_heads, own_score * scaling, masked_score)
         peak = jnp.maximum(jnp.max(included, axis=1, keepdims=True), jnp.max(own, axis=1, keepdims=True))
         weight, own_weight = jnp.exp(included - peak), jnp.exp(own - peak)
         denominators.append(
@@ -145,19 +159,19 @@
         )
         weights.append(weight.astype(bf16))
         own_weights.append(own_weight.astype(bf16))
-    for slot in range(capacity):
-        tile = slot // per_tile * TILE
-        own_values = block_ref[q_size + new_size + tile : q_size + new_size + tile + TILE, :]
-        values = jnp.concatenate([value_ref[page] for page in pages[slot]], axis=0)
-        wide = jnp.dot(weights[slot], values, preferred_element_type=f32)
+    for i, (n, slot) in enumerate(slots):
+        tile = q_size + new_size + slot // per_tile * TILE
+        own_values = blocks[n][tile : tile + TILE, :]
+        values = jnp.concatenate([value_ref[page] for page in pages[i]], axis=0)
+        wide = jnp.dot(weights[i], values, preferred_element_type=f32)
         numerator = jnp.concatenate(
             [
                 wide[head * group : (head + 1) * group, head * HEAD_SIZE : (head + 1) * HEAD_SIZE]
                 for head in range(key_heads)
             ],
             axis=0,
-        ) + jnp.dot(own_weights[slot], own_values, preferred_element_type=f32)
-        out_ref[slot * heads : (slot + 1) * heads, :] = (numerator / denominators[slot]).astype(bf16)
+        ) + jnp.dot(own_weights[i], own_values, preferred_element_type=f32)
+        answers[n][slot * heads : (slot + 1) * heads, :] = (numerator / denominators[i]).astype(bf16)
 
 
 def unpack_kernel(capacity, heads, rows, row_ref, probe_ref, *rest):
@@ -204,6 +218,7 @@
     def in_smem(x):
         return pltpu.with_memory_space_constraint(x, pltpu.SMEM)
 
+    turns = partners_in_turn(replicas)
     given = (
         queries,
         fresh_key_rows,
@@ -216,7 +231,7 @@
         context_length,
     )
     packed = pl.pallas_call(
-        functools.partial(pack_kernel, capacity),
+        functools.partial(pack_kernel, capacity, turns),
         out_shape=[pltpu.VMEM((block_size, HEAD_SIZE), bf16)] * replicas
         + [
             pltpu.VMEM(paged_key_store.shape, bf16),
@@ -238,6 +253,7 @@
             pltpu.VMEM((new_size, HEAD_SIZE), f32),
             pltpu.VMEM((new_size, HEAD_SIZE), f32),
             pltpu.SMEM((replicas,), i32),
+            pltpu.SMEM((replicas,), i32),
             pltpu.SemaphoreType.DMA((len(given),)),
         ],
         compiler_params=params,
@@ -247,25 +263,31 @@
     keys, values = map(in_vmem, packed[replicas : replicas + 2])
     table, slot_rows = map(in_smem, packed[replicas + 2 :])
 
-    serve = pl.pallas_call(
-        functools.partial(serve_kernel, capacity, heads),
-        out_shape=pltpu.VMEM((capacity * heads, HEAD_SIZE), bf16),
-        in_specs=[smem, vmem, vmem, vmem],
-        out_specs=vmem,
-        compiler_params=params,
-        cost_estimate=pl.CostEstimate(flops=10**7, bytes_accessed=2 * 10**6, transcendentals=0),
-        name="serve",
-    )
-
-    def swap(x, partner):
-        return lax.ppermute(x, "replica", [(i, i ^ partner) for i in range(replicas)])
-
-    far_first = sorted(range(1, replicas), key=lambda m: (-m.bit_length(), m))
-    answers = [None] * replicas
-    arrived = {m: swap(blocks[m], m) for m in far_first}
-    for m in far_first:
-        answers[m] = swap(serve(table, in_vmem(arrived[m]), keys, values), m)
-    answers[0] = serve(table, in_vmem(blocks[0]), keys, values)
+    def serve(asked):
+        return pl.pallas_call(
+            functools.partial(serve_kernel, capacity, heads),
+            out_shape=[pltpu.VMEM((capacity * heads, HEAD_SIZE), bf16)] * len(asked),
+            in_specs=[smem] + [vmem] * (2 + len(asked)),
+            out_specs=[vmem] * len(asked),
+            compiler_params=params,
+            cost_estimate=pl.CostEstimate(flops=10**7, bytes_accessed=2 * 10**6, transcendentals=0),
+            name="serve",
+        )(table, keys, values, *map(in_vmem, asked))
+
+    def swap(x, turn):
+        cores = lax.axis_size("tensor")
+        pairs = [
+            (i * cores + core, (i ^ turns[core % 2][turn]) * cores + core)
+            for i in range(replicas)
+            for core in range(cores)
+        ]
+        return lax.ppermute(x, ("replica", "tensor"), pairs)
+
+    arrived = [swap(blocks[turn], turn) for turn in range(replicas - 1)] + [blocks[-1]]
+    answers = []
+    for turn in range(0, replicas, TOGETHER):
+        for answer in serve(arrived[turn : turn + TOGETHER]):
+            answers.append(swap(answer, len(answers)) if len(answers) < replicas - 1 else answer)
 
     attended, partial_reward = pl.pallas_call(
         functools.partial(unpack_kernel, capacity, heads, rows),

time: 43.2 us -> 38.7 us (0.90)
  waiting for transfers between devices: 7.11 us -> 4.64 us
  Pallas kernels: 8.2 us -> 6.22 us
    ppermute x14, waiting for transfers between devices: 6.71 us -> 4.24 us  [swap(): return lax.ppermute(x, ('replica', 'tensor'), pairs)]
    pallas_call x9 -> x5, Pallas kernels: 7.72 us -> 5.74 us  [the longest x4 3.29 us: serve(): pl.pallas_call(functools.partial(serve_kernel, capacity, heads), out_shap...]
  transfers between devices with their start and end apart: 15 -> 15, of which waited for: 4 -> 5; matrix products, arithmetic and copies ran while one was open for 2% -> 2% of each run, Pallas kernels for 12% -> 9%
where the time goes in v3:
time: 38.7 us; the launch traced here: 38.6 us
  starting transfers between devices  25.8 us (67%)
  Pallas kernels  6.22 us (16%)
  waiting for transfers between devices  4.64 us (12%)
  between operations  0.74 us (2%)
  local copies, waits for them, and re-layouts  0.72 us (2%)
  other arithmetic  0.51 us (1%)
    ppermute x14, starting transfers between devices, swap(): return lax.ppermute(x, ('replica', 'tensor'), pairs)  25.7 us
    ppermute x14, waiting for transfers between devices, swap(): return lax.ppermute(x, ('replica', 'tensor'), pairs)  4.24 us
    pallas_call x4, Pallas kernels, serve(): pl.pallas_call(functools.partial(serve_kernel, capacity, heads), out_shap...  3.29 us
    pallas_call x1, Pallas kernels, shards(): pl.pallas_call(functools.partial(pack_kernel, capacity, turns), out_shape...  2.45 us
  transfers between devices with their start and end apart: 15, of which 5 were waited for; matrix products, arithmetic and copies ran while one was open for 2% of the time, Pallas kernels for 9%

profile of v3, /device:TPU:0, one launch (start us, length us, event | category | flops | bytes accessed | tf_op | source)
XLA Modules:
  0.0 38.6 jit_solution(8169863003206206588)
XLA Ops:
  0.6 2.5 %pack.1 = (bf16[336,128]{1,0:T(8,128)(2,1)S(1)}, bf16[336,128]{1,0:T(8,128)(2,1)S(1)}, bf16[336,128]{1,0:T(8,128)(2,1)S(1)}, bf16[336,128]{1,0:T(8,128)(2,1)S(1)...) custom-call(bf16[32,4096]{1,0:T(8,128)(2,1)} %q_hbm.1, ...), custom_call_target="tpu_custom_call" | custom-call | tf_op jit(solution)/shard_map/pack/pallas_call | solution.py:233
  3.1 6.1 %collective-permute-start.12 = (bf16[336,128]{1,0:T(8,128)(2,1)S(1)}, bf16[336,128]{1,0:T(8,128)(2,1)S(1)}, u32[]{:S(2)}, u32[]{:S(2)}) collective-permute-start(bf16[336,128]{1,0:T(8,128)(2,1)S(1)} %get-tuple-element.40), channel_id=1, source_target_pairs={{0,14},{1,15},{2,12},{3,13},{4,10},{5,11},{6,8},{7,9},{8,6},{9,7},... | collective-permute-start | bytes 258056 | tf_op jit(solution)/shard_map/ppermute | solution.py:284
  9.2 0.2 collective-permute-start.8
  9.4 0.0 collective-permute-start.9
  9.4 5.1 %collective-permute-start.4 = (bf16[336,128]{1,0:T(8,128)(2,1)S(1)}, bf16[336,128]{1,0:T(8,128)(2,1)S(1)}, u32[]{:S(2)}, u32[]{:S(2)}) collective-permute-start(bf16[336,128]{1,0:T(8,128)(2,1)S(1)} %get-tuple-element.32), channel_id=1, source_target_pairs={{0,10},{1,5},{2,8},{3,7},{4,14},{5,1},{6,12},{7,3},{8,2},{9,13},{1... | collective-permute-start | bytes 258056 | tf_op jit(solution)/shard_map/ppermute | solution.py:284
  14.4 0.0 collective-permute-start.5
  14.5 0.0 collective-permute-done.12.blocks_and_answers_0_
  14.5 0.8 %collective-permute-start = (bf16[336,128]{1,0:T(8,128)(2,1)S(1)}, bf16[336,128]{1,0:T(8,128)(2,1)S(1)}, u32[]{:S(2)}, u32[]{:S(2)}) collective-permute-start(bf16[336,128]{1,0:T(8,128)(2,1)S(1)} %get-tuple-element.28), channel_id=1, source_target_pairs={{0,8},{1,3},{2,10},{3,1},{4,12},{5,7},{6,14},{7,5},{8,0},{9,11},{1... | collective-permute-start | bytes 258056 | tf_op jit(solution)/shard_map/ppermute | solution.py:284
  15.2 1.2 %collective-permute-done.8.blocks_and_answers_0_ = bf16[336,128]{1,0:T(8,128)(2,1)S(1)} collective-permute-done((bf16[336,128]{1,0:T(8,128)(2,1)S(1)}, bf16[336,128]{1,0:T(8,128)(2,1)S(1)}, u32[]{:S(2)}, u32[]{:S(2)}) %collective-permute-start.8) | collective-permute-done | bytes 86048 | tf_op jit(solution)/shard_map/ppermute | solution.py:284
  16.5 0.3 collective-permute-start.1
  16.8 0.8 %serve.7 = (bf16[256,128]{1,0:T(8,128)(2,1)S(1)}, bf16[256,128]{1,0:T(8,128)(2,1)S(1)}) custom-call(s32[4,32]{1,0:T(4,128)S(4)} %get-tuple-element.25.table_ref, bf16[128,16,512]{2,1,0:T(8,128)(2,1)S(1)} %get-tuple-element.26.key_ref, bf16[128,16,512]{2,1,0:T(8,128)(2,1)S(1)} %get-tuple-element.27.value_ref, ...), custom_call_target="tpu_custom_call" | custom-call | flops 10000000 | bytes 2000000 | tf_op jit(solution)/shard_map/serve/pallas_call | solution.py:267
  17.6 0.0 collective-permute-done.9.blocks_and_answers_1_
  17.6 3.6 %collective-permute-start.13 = (bf16[256,128]{1,0:T(8,128)(2,1)S(1)}, bf16[256,128]{1,0:T(8,128)(2,1)S(1)}, u32[]{:S(2)}, u32[]{:S(2)}) collective-permute-start(bf16[256,128]{1,0:T(8,128)(2,1)S(1)} %get-tuple-element.42), channel_id=1, source_target_pairs={{0,14},{1,15},{2,12},{3,13},{4,10},{5,11},{6,8},{7,9},{8,6},{9,7},... | collective-permute-start | bytes 196616 | tf_op jit(solution)/shard_map/ppermute | solution.py:284
  21.2 0.8 %serve.6 = (bf16[256,128]{1,0:T(8,128)(2,1)S(1)}, bf16[256,128]{1,0:T(8,128)(2,1)S(1)}) custom-call(s32[4,32]{1,0:T(4,128)S(4)} %get-tuple-element.25.table_ref, bf16[128,16,512]{2,1,0:T(8,128)(2,1)S(1)} %get-tuple-element.26.key_ref, bf16[128,16,512]{2,1,0:T(8,128)(2,1)S(1)} %get-tuple-element.27.value_ref, ...), custom_call_target="tpu_custom_call" | custom-call | flops 10000000 | bytes 2000000 | tf_op jit(solution)/shard_map/serve/pallas_call | solution.py:267
  22.0 0.0 collective-permute-done.4.blocks_and_answers_0_
  22.1 1.6 %collective-permute-start.10 = (bf16[256,128]{1,0:T(8,128)(2,1)S(1)}, bf16[256,128]{1,0:T(8,128)(2,1)S(1)}, u32[]{:S(2)}, u32[]{:S(2)}) collective-permute-start(bf16[256,128]{1,0:T(8,128)(2,1)S(1)} %get-tuple-element.38), channel_id=1, source_target_pairs={{0,12},{1,7},{2,14},{3,5},{4,8},{5,3},{6,10},{7,1},{8,4},{9,15},{1... | collective-permute-start | bytes 196616 | tf_op jit(solution)/shard_map/ppermute | solution.py:284
  23.6 0.0 collective-permute-done.5.blocks_and_answers_1_
  23.6 0.0 collective-permute-start.11
  23.6 0.8 %serve.5 = (bf16[256,128]{1,0:T(8,128)(2,1)S(1)}, bf16[256,128]{1,0:T(8,128)(2,1)S(1)}) custom-call(s32[4,32]{1,0:T(4,128)S(4)} %get-tuple-element.25.table_ref, bf16[128,16,512]{2,1,0:T(8,128)(2,1)S(1)} %get-tuple-element.26.key_ref, bf16[128,16,512]{2,1,0:T(8,128)(2,1)S(1)} %get-tuple-element.27.value_ref, ...), custom_call_target="tpu_custom_call" | custom-call | flops 10000000 | bytes 2000000 | tf_op jit(solution)/shard_map/serve/pallas_call | solution.py:267
  24.5 0.8 %collective-permute-done.blocks_and_answers_0_ = bf16[336,128]{1,0:T(8,128)(2,1)S(1)} collective-permute-done((bf16[336,128]{1,0:T(8,128)(2,1)S(1)}, bf16[336,128]{1,0:T(8,128)(2,1)S(1)}, u32[]{:S(2)}, u32[]{:S(2)}) %collective-permute-start) | collective-permute-done | bytes 86048 | tf_op jit(solution)/shard_map/ppermute | solution.py:284
  25.3 3.1 %collective-permute-start.6 = (bf16[256,128]{1,0:T(8,128)(2,1)S(1)}, bf16[256,128]{1,0:T(8,128)(2,1)S(1)}, u32[]{:S(2)}, u32[]{:S(2)}) collective-permute-start(bf16[256,128]{1,0:T(8,128)(2,1)S(1)} %get-tuple-element.34), channel_id=1, source_target_pairs={{0,10},{1,5},{2,8},{3,7},{4,14},{5,1},{6,12},{7,3},{8,2},{9,13},{1... | collective-permute-start | bytes 196616 | tf_op jit(solution)/shard_map/ppermute | solution.py:284
  28.3 0.0 collective-permute-done.1.blocks_and_answers_1_
  28.3 0.0 copy-start
  28.3 0.7 %collective-permute-start.7 = (bf16[256,128]{1,0:T(8,128)(2,1)S(1)}, bf16[256,128]{1,0:T(8,128)(2,1)S(1)}, u32[]{:S(2)}, u32[]{:S(2)}) collective-permute-start(bf16[256,128]{1,0:T(8,128)(2,1)S(1)} %get-tuple-element.35), channel_id=1, source_target_pairs={{0,4},{1,11},{2,6},{3,9},{4,0},{5,15},{6,2},{7,13},{8,12},{9,3},{1... | collective-permute-start | bytes 196616 | tf_op jit(solution)/shard_map/ppermute | solution.py:284
  29.0 0.8 %serve.4 = (bf16[256,128]{1,0:T(8,128)(2,1)S(1)}, bf16[256,128]{1,0:T(8,128)(2,1)S(1)}) custom-call(s32[4,32]{1,0:T(4,128)S(4)} %get-tuple-element.25.table_ref, bf16[128,16,512]{2,1,0:T(8,128)(2,1)S(1)} %get-tuple-element.26.key_ref, bf16[128,16,512]{2,1,0:T(8,128)(2,1)S(1)} %get-tuple-element.27.value_ref, ...), custom_call_target="tpu_custom_call" | custom-call | flops 10000000 | bytes 2000000 | tf_op jit(solution)/shard_map/serve/pallas_call | solution.py:267
  29.8 0.0 collective-permute-done.13.rest_6_
  29.8 1.5 %collective-permute-start.2 = (bf16[256,128]{1,0:T(8,128)(2,1)S(1)}, bf16[256,128]{1,0:T(8,128)(2,1)S(1)}, u32[]{:S(2)}, u32[]{:S(2)}) collective-permute-start(bf16[256,128]{1,0:T(8,128)(2,1)S(1)} %get-tuple-element.30), channel_id=1, source_target_pairs={{0,8},{1,3},{2,10},{3,1},{4,12},{5,7},{6,14},{7,5},{8,0},{9,11},{1... | collective-permute-start | bytes 196616 | tf_op jit(solution)/shard_map/ppermute | solution.py:284
  31.3 0.0 collective-permute-done.10.rest_4_
  31.3 2.9 %collective-permute-start.3 = (bf16[256,128]{1,0:T(8,128)(2,1)S(1)}, bf16[256,128]{1,0:T(8,128)(2,1)S(1)}, u32[]{:S(2)}, u32[]{:S(2)}) collective-permute-start(bf16[256,128]{1,0:T(8,128)(2,1)S(1)} %get-tuple-element.31), channel_id=1, source_target_pairs={{0,2},{1,9},{2,0},{3,11},{4,6},{5,13},{6,4},{7,15},{8,10},{9,1},{1... | collective-permute-start | bytes 196616 | tf_op jit(solution)/shard_map/ppermute | solution.py:284
  34.2 0.0 copy-done
  34.2 0.0 collective-permute-done.11.rest_5_
  34.2 0.0 collective-permute-done.6.rest_2_
  34.2 0.0 collective-permute-done.7.rest_3_
  34.2 1.9 %collective-permute-done.2.rest_0_ = bf16[256,128]{1,0:T(8,128)(2,1)S(1)} collective-permute-done((bf16[256,128]{1,0:T(8,128)(2,1)S(1)}, bf16[256,128]{1,0:T(8,128)(2,1)S(1)}, u32[]{:S(2)}, u32[]{:S(2)}) %collective-permute-start.2) | collective-permute-done | bytes 65568 | tf_op jit(solution)/shard_map/ppermute | solution.py:284
  36.1 0.3 collective-permute-done.3.rest_1_
  36.4 0.5 %unpack.1 = (bf16[32,4096]{1,0:T(8,128)(2,1)S(1)}, f32[1,32]{1,0:T(1,128)S(1)}) custom-call(s32[64]{0:T(128)S(4)} %get-tuple-element.24.row_ref, bf16[1,4096]{1,0:T(2,128)(2,1)S(1)} %reshape.7.probe_ref, bf16[256,128]{1,0:T(8,128)(2,1)S(1)} %collective-permute-done.2.rest_0_, bf16[256,128]{1,0:T(8,128)(2,1)S(1)} %collective-permute-done.3.rest_1_, ...), custom_call_target="tpu_custom_call" | custom-call | tf_op jit(solution)/shard_map/unpack/pallas_call | solution.py:292
  36.9 0.1 collective-permute-start.14
  37.0 0.7 %copy.12 = bf16[32,4096]{1,0:T(8,128)(2,1)} copy(bf16[32,4096]{1,0:T(8,128)(2,1)S(1)} %get-tuple-element.46) | data formatting | bytes 524288
  37.7 0.4 %collective-permute-done.14 = f32[1,32]{1,0:T(1,128)S(1)} collective-permute-done((f32[1,32]{1,0:T(1,128)S(1)}, f32[1,32]{1,0:T(1,128)S(1)}, u32[]{:S(2)}, u32[]{:S(2)}) %collective-permute-start.14) | collective-permute-done | bytes 160 | tf_op jit(solution)/shard_map/ppermute | solution.py:301
  38.1 0.5 %add_bitcast_fusion = f32[32]{0:T(128)} fusion(f32[1,32]{1,0:T(1,128)S(1)} %get-tuple-element.45, f32[1,32]{1,0:T(1,128)S(1)} %collective-permute-done.14), kind=kLoop, calls=%fused_computation | loop fusion | flops 32 | bytes 384 | tf_op jit(solution)/shard_map/squeeze | solution.py:302
  (1 shorter events, 0.0 us)
Async XLA Ops:
  3.1 11.4 %collective-permute-start.12 = (bf16[336,128]{1,0:T(8,128)(2,1)S(1)}, bf16[336,128]{1,0:T(8,128)(2,1)S(1)}, u32[]{:S(2)}, u32[]{:S(2)}) collective-permute-start(bf16[336,128]{1,0:T(8,128)(2,1)S(1)} %get-tuple-element.40), channel_id=1, source_target_pairs={{0,14},{1,15},{2,12},{3,13},{4,10},{5,11},{6,8},{7,9},{8,6},{9,7},... | collective-permute-start | bytes 258056 | tf_op jit(solution)/shard_map/ppermute | solution.py:284
  9.2 7.3 %collective-permute-start.8 = (bf16[336,128]{1,0:T(8,128)(2,1)S(1)}, bf16[336,128]{1,0:T(8,128)(2,1)S(1)}, u32[]{:S(2)}, u32[]{:S(2)}) collective-permute-start(bf16[336,128]{1,0:T(8,128)(2,1)S(1)} %get-tuple-element.36), channel_id=1, source_target_pairs={{0,12},{1,7},{2,14},{3,5},{4,8},{5,3},{6,10},{7,1},{8,4},{9,15},{1... | collective-permute-start | bytes 258056 | tf_op jit(solution)/shard_map/ppermute | solution.py:284
  9.4 8.2 %collective-permute-start.9 = (bf16[336,128]{1,0:T(8,128)(2,1)S(1)}, bf16[336,128]{1,0:T(8,128)(2,1)S(1)}, u32[]{:S(2)}, u32[]{:S(2)}) collective-permute-start(bf16[336,128]{1,0:T(8,128)(2,1)S(1)} %get-tuple-element.37), channel_id=1, source_target_pairs={{0,6},{1,13},{2,4},{3,15},{4,2},{5,9},{6,0},{7,11},{8,14},{9,5},{1... | collective-permute-start | bytes 258056 | tf_op jit(solution)/shard_map/ppermute | solution.py:284
  9.4 12.7 %collective-permute-start.4 = (bf16[336,128]{1,0:T(8,128)(2,1)S(1)}, bf16[336,128]{1,0:T(8,128)(2,1)S(1)}, u32[]{:S(2)}, u32[]{:S(2)}) collective-permute-start(bf16[336,128]{1,0:T(8,128)(2,1)S(1)} %get-tuple-element.32), channel_id=1, source_target_pairs={{0,10},{1,5},{2,8},{3,7},{4,14},{5,1},{6,12},{7,3},{8,2},{9,13},{1... | collective-permute-start | bytes 258056 | tf_op jit(solution)/shard_map/ppermute | solution.py:284
  14.4 9.2 %collective-permute-start.5 = (bf16[336,128]{1,0:T(8,128)(2,1)S(1)}, bf16[336,128]{1,0:T(8,128)(2,1)S(1)}, u32[]{:S(2)}, u32[]{:S(2)}) collective-permute-start(bf16[336,128]{1,0:T(8,128)(2,1)S(1)} %get-tuple-element.33), channel_id=1, source_target_pairs={{0,4},{1,11},{2,6},{3,9},{4,0},{5,15},{6,2},{7,13},{8,12},{9,3},{1... | collective-permute-start | bytes 258056 | tf_op jit(solution)/shard_map/ppermute | solution.py:284
  14.5 10.8 %collective-permute-start = (bf16[336,128]{1,0:T(8,128)(2,1)S(1)}, bf16[336,128]{1,0:T(8,128)(2,1)S(1)}, u32[]{:S(2)}, u32[]{:S(2)}) collective-permute-start(bf16[336,128]{1,0:T(8,128)(2,1)S(1)} %get-tuple-element.28), channel_id=1, source_target_pairs={{0,8},{1,3},{2,10},{3,1},{4,12},{5,7},{6,14},{7,5},{8,0},{9,11},{1... | collective-permute-start | bytes 258056 | tf_op jit(solution)/shard_map/ppermute | solution.py:284
  16.5 11.8 %collective-permute-start.1 = (bf16[336,128]{1,0:T(8,128)(2,1)S(1)}, bf16[336,128]{1,0:T(8,128)(2,1)S(1)}, u32[]{:S(2)}, u32[]{:S(2)}) collective-permute-start(bf16[336,128]{1,0:T(8,128)(2,1)S(1)} %get-tuple-element.29), channel_id=1, source_target_pairs={{0,2},{1,9},{2,0},{3,11},{4,6},{5,13},{6,4},{7,15},{8,10},{9,1},{1... | collective-permute-start | bytes 258056 | tf_op jit(solution)/shard_map/ppermute | solution.py:284
  17.6 12.2 %collective-permute-start.13 = (bf16[256,128]{1,0:T(8,128)(2,1)S(1)}, bf16[256,128]{1,0:T(8,128)(2,1)S(1)}, u32[]{:S(2)}, u32[]{:S(2)}) collective-permute-start(bf16[256,128]{1,0:T(8,128)(2,1)S(1)} %get-tuple-element.42), channel_id=1, source_target_pairs={{0,14},{1,15},{2,12},{3,13},{4,10},{5,11},{6,8},{7,9},{8,6},{9,7},... | collective-permute-start | bytes 196616 | tf_op jit(solution)/shard_map/ppermute | solution.py:284
  22.1 9.3 %collective-permute-start.10 = (bf16[256,128]{1,0:T(8,128)(2,1)S(1)}, bf16[256,128]{1,0:T(8,128)(2,1)S(1)}, u32[]{:S(2)}, u32[]{:S(2)}) collective-permute-start(bf16[256,128]{1,0:T(8,128)(2,1)S(1)} %get-tuple-element.38), channel_id=1, source_target_pairs={{0,12},{1,7},{2,14},{3,5},{4,8},{5,3},{6,10},{7,1},{8,4},{9,15},{1... | collective-permute-start | bytes 196616 | tf_op jit(solution)/shard_map/ppermute | solution.py:284
  23.6 10.5 %collective-permute-start.11 = (bf16[256,128]{1,0:T(8,128)(2,1)S(1)}, bf16[256,128]{1,0:T(8,128)(2,1)S(1)}, u32[]{:S(2)}, u32[]{:S(2)}) collective-permute-start(bf16[256,128]{1,0:T(8,128)(2,1)S(1)} %get-tuple-element.39), channel_id=1, source_target_pairs={{0,6},{1,13},{2,4},{3,15},{4,2},{5,9},{6,0},{7,11},{8,14},{9,5},{1... | collective-permute-start | bytes 196616 | tf_op jit(solution)/shard_map/ppermute | solution.py:284
  25.3 8.9 %collective-permute-start.6 = (bf16[256,128]{1,0:T(8,128)(2,1)S(1)}, bf16[256,128]{1,0:T(8,128)(2,1)S(1)}, u32[]{:S(2)}, u32[]{:S(2)}) collective-permute-start(bf16[256,128]{1,0:T(8,128)(2,1)S(1)} %get-tuple-element.34), channel_id=1, source_target_pairs={{0,10},{1,5},{2,8},{3,7},{4,14},{5,1},{6,12},{7,3},{8,2},{9,13},{1... | collective-permute-start | bytes 196616 | tf_op jit(solution)/shard_map/ppermute | solution.py:284
  28.3 5.9 %copy-start = (bf16[4096]{0:T(1024)(128)(2,1)S(1)}, bf16[4096]{0:T(1024)(128)(2,1)}, u32[]{:S(2)}) copy-start(bf16[4096]{0:T(1024)(128)(2,1)} %param.19) | copy-start | bytes 24580
  28.3 5.9 %collective-permute-start.7 = (bf16[256,128]{1,0:T(8,128)(2,1)S(1)}, bf16[256,128]{1,0:T(8,128)(2,1)S(1)}, u32[]{:S(2)}, u32[]{:S(2)}) collective-permute-start(bf16[256,128]{1,0:T(8,128)(2,1)S(1)} %get-tuple-element.35), channel_id=1, source_target_pairs={{0,4},{1,11},{2,6},{3,9},{4,0},{5,15},{6,2},{7,13},{8,12},{9,3},{1... | collective-permute-start | bytes 196616 | tf_op jit(solution)/shard_map/ppermute | solution.py:284
  29.8 6.3 %collective-permute-start.2 = (bf16[256,128]{1,0:T(8,128)(2,1)S(1)}, bf16[256,128]{1,0:T(8,128)(2,1)S(1)}, u32[]{:S(2)}, u32[]{:S(2)}) collective-permute-start(bf16[256,128]{1,0:T(8,128)(2,1)S(1)} %get-tuple-element.30), channel_id=1, source_target_pairs={{0,8},{1,3},{2,10},{3,1},{4,12},{5,7},{6,14},{7,5},{8,0},{9,11},{1... | collective-permute-start | bytes 196616 | tf_op jit(solution)/shard_map/ppermute | solution.py:284
  31.3 5.1 %collective-permute-start.3 = (bf16[256,128]{1,0:T(8,128)(2,1)S(1)}, bf16[256,128]{1,0:T(8,128)(2,1)S(1)}, u32[]{:S(2)}, u32[]{:S(2)}) collective-permute-start(bf16[256,128]{1,0:T(8,128)(2,1)S(1)} %get-tuple-element.31), channel_id=1, source_target_pairs={{0,2},{1,9},{2,0},{3,11},{4,6},{5,13},{6,4},{7,15},{8,10},{9,1},{1... | collective-permute-start | bytes 196616 | tf_op jit(solution)/shard_map/ppermute | solution.py:284
  36.9 1.2 %collective-permute-start.14 = (f32[1,32]{1,0:T(1,128)S(1)}, f32[1,32]{1,0:T(1,128)S(1)}, u32[]{:S(2)}, u32[]{:S(2)}) collective-permute-start(f32[1,32]{1,0:T(1,128)S(1)} %get-tuple-element.45), channel_id=1, source_target_pairs={{0,1},{1,0},{2,3},{3,2},{4,5},{5,4},{6,7},{7,6},{8,9},{9,8},{10,11... | collective-permute-start | bytes 392 | tf_op jit(solution)/shard_map/ppermute | solution.py:301

commit v4 on v3

--- a/solution.py
+++ b/solution.py
@@ -19,8 +19,11 @@
 
 
 def block_rows(capacity, heads, key_heads):
-    new_rows = round_up(capacity * key_heads, TILE)
-    return capacity * heads, new_rows, round_up(capacity, TILE)
+    return capacity * heads, round_up(capacity * key_heads, TILE), round_up(capacity, TILE)
+
+
+def iota(shape, axis):
+    return lax.broadcasted_iota(i32, shape, axis)
 
 
 def partners_in_turn(replicas):
@@ -31,48 +34,71 @@
     return even, odd
 
 
-def pack_kernel(
-    capacity, turns, q_hbm, k_hbm, v_hbm, key_hbm, value_hbm, table_hbm, source_hbm, parent_hbm, length_hbm, *rest
-):
-    replicas = len(rest) - 17
-    blocks = rest[:replicas]
-    keys_ref, values_ref, table_ref, row_ref = rest[replicas : replicas + 4]
-    q_ref, k_ref, v_ref, source_ref, parent_ref, length_ref = rest[replicas + 4 : replicas + 10]
-    q_rows, new_rows, new_keys, new_values, taken, turn_ref, arrived = rest[replicas + 10 :]
+def start_copies(sources, targets, arrived):
     copies = [
         pltpu.make_async_copy(source, target, arrived.at[i])
-        for i, (source, target) in enumerate(
-            (
-                (source_hbm, source_ref),
-                (q_hbm, q_ref),
-                (k_hbm, k_ref),
-                (v_hbm, v_ref),
-                (parent_hbm, parent_ref),
-                (length_hbm, length_ref),
-                (table_hbm, table_ref),
-                (key_hbm, keys_ref),
-                (value_hbm, values_ref),
-            )
-        )
+        for i, (source, target) in enumerate(zip(sources, targets))
     ]
     for copy in copies:
         copy.start()
+    return copies
+
+
+def fill(blocks, capacity, heads, key_heads, row_ref, q_rows, value_rows, facts, new_values, meta):
+    q_size, new_size, _ = block_rows(capacity, heads, key_heads)
+    step = round_up(key_heads, 8)
+    for turn, block in enumerate(blocks):
+        for slot in range(capacity):
+            row = row_ref[turn * capacity + slot]
+            block[slot * heads : (slot + 1) * heads, :] = q_rows[
+                pl.ds(pl.multiple_of(row * heads, heads), heads), :
+            ].astype(bf16)
+            own = value_rows[pl.ds(pl.multiple_of(row * step, step), step), :]
+            new_values[slot * key_heads : (slot + 1) * key_heads, :] = own[:key_heads]
+            meta[slot : slot + 1, :] = facts[pl.ds(row, 1), :]
+        block[q_size : q_size + new_size, :] = new_values[...].astype(bf16)
+        block[q_size + new_size :, :] = meta[...].astype(bf16)
+
+
+def pack_kernel(
+    capacity,
+    turns,
+    q_hbm,
+    k_hbm,
+    v_hbm,
+    source_hbm,
+    parent_hbm,
+    length_hbm,
+    table_hbm,
+    key_hbm,
+    value_hbm,
+    *rest,
+):
+    replicas = len(turns[0])
+    blocks, rest = rest[:replicas], rest[replicas:]
+    row_ref, table_ref, keys_ref, values_ref = rest[:4]
+    q_ref, k_ref, v_ref, source_ref, parent_ref, length_ref = rest[4:10]
+    q_rows, value_rows, facts, new_values, meta, taken, turn_ref, arrived = rest[10:]
+    copies = start_copies(
+        (source_hbm, q_hbm, k_hbm, v_hbm, parent_hbm, length_hbm, table_hbm, key_hbm, value_hbm),
+        (source_ref, q_ref, k_ref, v_ref, parent_ref, length_ref, table_ref, keys_ref, values_ref),
+        arrived,
+    )
     rows = q_ref.shape[0]
     heads, key_heads = q_ref.shape[1] // HEAD_SIZE, k_ref.shape[1] // HEAD_SIZE
-    me = lax.axis_index("replica")
+    step = round_up(key_heads, 8)
+    me, odd = lax.axis_index("replica"), lax.rem(lax.axis_index("tensor"), 2)
     for slot in range(replicas * capacity):
         row_ref[slot] = rows
-    odd = lax.rem(lax.axis_index("tensor"), 2)
     for replica in range(replicas):
         taken[replica] = 0
         even_turn, odd_turn = (turn.index(replica) for turn in turns)
         turn_ref[replica] = jnp.where(odd == 1, odd_turn, even_turn)
     q_rows[rows * heads :, :] = jnp.zeros((heads, HEAD_SIZE), f32)
-    new_rows[rows * 2 * key_heads :, :] = jnp.zeros((2 * key_heads, HEAD_SIZE), f32)
-    q_size, new_size, meta_size = block_rows(capacity, heads, key_heads)
-    if new_size != capacity * key_heads:
-        new_keys[...] = jnp.zeros_like(new_keys)
-        new_values[...] = jnp.zeros_like(new_values)
+    value_rows[rows * step :, :] = jnp.zeros((step, HEAD_SIZE), f32)
+    facts[rows:, :] = jnp.zeros((facts.shape[0] - rows, HEAD_SIZE), f32)
+    new_values[...] = jnp.zeros_like(new_values)
+    meta[...] = jnp.zeros_like(meta)
     copies[0].wait()
     for row in range(rows):
         source = source_ref[row]
@@ -81,33 +107,31 @@
         row_ref[turn_ref[source ^ me] * capacity + rank] = row
     for copy in copies[1:6]:
         copy.wait()
+    lane = iota((rows, HEAD_SIZE), 1)
+    own = jnp.zeros((rows, HEAD_SIZE), f32)
     for head in range(heads):
         lanes = slice(head * HEAD_SIZE, (head + 1) * HEAD_SIZE)
-        q_rows[pl.ds(head, rows, stride=heads), :] = q_ref[:, lanes].astype(f32)
-    for head in range(key_heads):
-        lanes = slice(head * HEAD_SIZE, (head + 1) * HEAD_SIZE)
-        new_rows[pl.ds(head, rows, stride=2 * key_heads), :] = k_ref[:, lanes].astype(f32)
-        new_rows[pl.ds(key_heads + head, rows, stride=2 * key_heads), :] = v_ref[:, lanes].astype(f32)
-    at_row = lax.broadcasted_iota(i32, (meta_size, HEAD_SIZE), 0)
-    at_lane = lax.broadcasted_iota(i32, (meta_size, HEAD_SIZE), 1)
-    for partner, block in enumerate(blocks):
-        meta = jnp.zeros((meta_size, HEAD_SIZE), f32)
-        for slot in range(capacity):
-            row = row_ref[partner * capacity + slot]
-            block[slot * heads : (slot + 1) * heads, :] = q_rows[
-                pl.ds(pl.multiple_of(row * heads, heads), heads), :
-            ].astype(bf16)
-            pair = new_rows[pl.ds(pl.multiple_of(row * 2 * key_heads, 2 * key_heads), 2 * key_heads), :]
-            new_keys[slot * key_heads : (slot + 1) * key_heads, :] = pair[:key_heads]
-            new_values[slot * key_heads : (slot + 1) * key_heads, :] = pair[key_heads:]
-            real = row < rows
-            held = jnp.minimum(row, rows - 1)
-            parent = jnp.where(real, parent_ref[held], 0).astype(f32)
-            length = jnp.where(real, length_ref[held], 0).astype(f32)
-            meta = jnp.where(at_row == slot, jnp.where(at_lane == 0, parent, length), meta)
-        block[q_size : q_size + new_size, :] = new_keys[...].astype(bf16)
-        block[q_size + new_size : q_size + 2 * new_size, :] = new_values[...].astype(bf16)
-        block[q_size + 2 * new_size :, :] = meta.astype(bf16)
+        q_head = q_ref[:, lanes].astype(f32)
+        q_rows[pl.ds(head, rows, stride=heads), :] = q_head
+        key_head = head // (heads // key_heads)
+        if head % (heads // key_heads) == 0:
+            lanes = slice(key_head * HEAD_SIZE, (key_head + 1) * HEAD_SIZE)
+            k_head = k_ref[:, lanes].astype(f32)
+            value_rows[pl.ds(key_head, rows, stride=step), :] = v_ref[:, lanes].astype(f32)
+        score = jnp.sum(q_head * k_head, axis=1, keepdims=True)
+        own = jnp.where(lane % heads == head, score, own)
+    high = own.astype(bf16).astype(f32)
+    middle = (own - high).astype(bf16).astype(f32)
+    low = own - high - middle
+    part = lane // heads
+    own = jnp.where(part == 1, high, jnp.where(part == 2, middle, jnp.where(part == 3, low, 0.0)))
+    diagonal = iota((rows, rows), 0) == iota((rows, rows), 1)
+
+    def column(ref):
+        return jnp.sum(jnp.where(diagonal, ref[...].astype(f32), 0.0), axis=1, keepdims=True)
+
+    facts[:rows, :] = jnp.where(lane == 0, column(parent_ref), jnp.where(lane == 1, column(length_ref), own))
+    fill(blocks, capacity, heads, key_heads, row_ref, q_rows, value_rows, facts, new_values, meta)
     for copy in copies[6:]:
         copy.wait()
 
@@ -125,11 +149,12 @@
     per_tile = TILE // key_heads
     slots = [(n, slot) for n in range(number) for slot in range(capacity)]
 
-    def iota(shape, axis):
-        return lax.broadcasted_iota(i32, shape, axis)
-
     at_row, at_lane = iota((meta_size, HEAD_SIZE), 0), iota((meta_size, HEAD_SIZE), 1)
-    metas = [block[q_size + 2 * new_size :, :].astype(f32) for block in blocks]
+    metas = [block[q_size + new_size :, :].astype(f32) for block in blocks]
+    at_lane_of_head = iota((heads, HEAD_SIZE), 1)
+    picked = (at_lane_of_head % heads == iota((heads, HEAD_SIZE), 0)) & (at_lane_of_head >= heads)
+    by_lanes = (((1,), (1,)), ((), ()))
+    picked = jnp.where(picked, 1.0, 0.0).astype(bf16)
     coded = [jnp.where(at_lane == 0, meta, jnp.where(at_lane == 1, meta * rows, 0.0)) for meta in metas]
     codes = [jnp.sum(jnp.where(at_row == slot, coded[n], 0.0)).astype(i32) for n, slot in slots]
     lengths = [code // rows for code in codes]
@@ -138,20 +163,18 @@
     diagonal = iota((heads, width), 0) // group == iota((heads, width), 1) // HEAD_SIZE
     own_lane = iota((heads, TILE), 1) - iota((heads, TILE), 0) // group
     seen = iota((heads, span), 1)
-    by_lanes = (((1,), (1,)), ((), ()))
-    scores, own_scores = [], []
+    scores, new_scores = [], []
     for (n, slot), found in zip(slots, pages):
-        tile = q_size + slot // per_tile * TILE
-        own_keys = blocks[n][tile : tile + TILE, :]
         q_slot = blocks[n][slot * heads : (slot + 1) * heads, :]
         keys = jnp.concatenate([key_ref[page] for page in found], axis=0)
         spread = jnp.where(diagonal, jnp.concatenate([q_slot] * key_heads, axis=1), jnp.zeros((), bf16))
         scores.append(lax.dot_general(spread, keys, by_lanes, preferred_element_type=f32))
-        own_scores.append(lax.dot_general(q_slot, own_keys, by_lanes, preferred_element_type=f32))
+        parts = jnp.broadcast_to(metas[n][slot : slot + 1, :], (TILE, HEAD_SIZE)).astype(bf16)
+        new_scores.append(lax.dot_general(picked, parts, by_lanes, preferred_element_type=f32))
     weights, own_weights, denominators = [], [], []
-    for (_, slot), length, score, own_score in zip(slots, lengths, scores, own_scores):
+    for (_, slot), length, score, new_score in zip(slots, lengths, scores, new_scores):
         included = jnp.where(seen < length, score * scaling, masked_score)
-        own = jnp.where(own_lane == slot % per_tile * key_heads, own_score * scaling, masked_score)
+        own = jnp.where(own_lane == slot % per_tile * key_heads, new_score * scaling, masked_score)
         peak = jnp.maximum(jnp.max(included, axis=1, keepdims=True), jnp.max(own, axis=1, keepdims=True))
         weight, own_weight = jnp.exp(included - peak), jnp.exp(own - peak)
         denominators.append(
@@ -160,7 +183,7 @@
         weights.append(weight.astype(bf16))
         own_weights.append(own_weight.astype(bf16))
     for i, (n, slot) in enumerate(slots):
-        tile = q_size + new_size + slot // per_tile * TILE
+        tile = q_size + slot // per_tile * TILE
         own_values = blocks[n][tile : tile + TILE, :]
         values = jnp.concatenate([value_ref[page] for page in pages[i]], axis=0)
         wide = jnp.dot(weights[i], values, preferred_element_type=f32)
@@ -208,7 +231,8 @@
     heads = queries.shape[1] // HEAD_SIZE
     key_heads = fresh_key_rows.shape[1] // HEAD_SIZE
     q_size, new_size, meta_size = block_rows(capacity, heads, key_heads)
-    block_size = q_size + 2 * new_size + meta_size
+    block_size = q_size + new_size + meta_size
+    step = round_up(key_heads, 8)
     vmem, smem = pl.BlockSpec(memory_space=pltpu.VMEM), pl.BlockSpec(memory_space=pltpu.SMEM)
     params = pltpu.CompilerParams(vmem_limit_bytes=16 * 2**20)
 
@@ -223,35 +247,36 @@
         queries,
         fresh_key_rows,
         fresh_value_rows,
+        parent_replica[:, 0],
+        parent_slot.reshape(1, rows),
+        context_length.reshape(1, rows),
+        page_table.T,
         paged_key_store,
         paged_value_store,
-        page_table.T,
-        parent_replica[:, 0],
-        parent_slot[:, 0],
-        context_length,
     )
     packed = pl.pallas_call(
         functools.partial(pack_kernel, capacity, turns),
         out_shape=[pltpu.VMEM((block_size, HEAD_SIZE), bf16)] * replicas
         + [
+            pltpu.SMEM((replicas * capacity,), i32),
+            pltpu.SMEM(page_table.shape[::-1], i32),
             pltpu.VMEM(paged_key_store.shape, bf16),
             pltpu.VMEM(paged_value_store.shape, bf16),
-            pltpu.SMEM(page_table.shape[::-1], i32),
-            pltpu.SMEM((replicas * capacity,), i32),
         ],
         in_specs=[pl.BlockSpec(memory_space=pltpu.HBM)] * len(given),
-        out_specs=[vmem] * (replicas + 2) + [smem] * 2,
+        out_specs=[vmem] * replicas + [smem] * 2 + [vmem] * 2,
         scratch_shapes=[
             pltpu.VMEM(queries.shape, bf16),
             pltpu.VMEM(fresh_key_rows.shape, bf16),
             pltpu.VMEM(fresh_value_rows.shape, bf16),
             pltpu.SMEM((rows,), i32),
-            pltpu.SMEM((rows,), i32),
-            pltpu.SMEM((rows,), i32),
+            pltpu.VMEM((1, rows), i32),
+            pltpu.VMEM((1, rows), i32),
             pltpu.VMEM(((rows + 1) * heads, HEAD_SIZE), f32),
-            pltpu.VMEM(((rows + 1) * 2 * key_heads, HEAD_SIZE), f32),
+            pltpu.VMEM(((rows + 1) * step, HEAD_SIZE), f32),
+            pltpu.VMEM((rows + 8, HEAD_SIZE), f32),
             pltpu.VMEM((new_size, HEAD_SIZE), f32),
-            pltpu.VMEM((new_size, HEAD_SIZE), f32),
+            pltpu.VMEM((meta_size, HEAD_SIZE), f32),
             pltpu.SMEM((replicas,), i32),
             pltpu.SMEM((replicas,), i32),
             pltpu.SemaphoreType.DMA((len(given),)),
@@ -260,8 +285,8 @@
         name="pack",
     )(*[pltpu.with_memory_space_constraint(x, pltpu.HBM) for x in given])
     blocks = packed[:replicas]
-    keys, values = map(in_vmem, packed[replicas : replicas + 2])
-    table, slot_rows = map(in_smem, packed[replicas + 2 :])
+    slot_rows, table = map(in_smem, packed[replicas : replicas + 2])
+    keys, values = map(in_vmem, packed[replicas + 2 :])
 
     def serve(asked):
         return pl.pallas_call(
@@ -283,7 +308,7 @@
         ]
         return lax.ppermute(x, ("replica", "tensor"), pairs)
 
-    arrived = [swap(blocks[turn], turn) for turn in range(replicas - 1)] + [blocks[-1]]
+    arrived = [swap(blocks[turn], turn) for turn in range(replicas - 1)] + [blocks[replicas - 1]]
     answers = []
     for turn in range(0, replicas, TOGETHER):
         for answer in serve(arrived[turn : turn + TOGETHER]):

time: 38.7 us -> 37.8 us (0.977)
  starting transfers between devices: 25.8 us -> 24.2 us
  waiting for transfers between devices: 4.64 us -> 5.14 us
    ppermute x14, starting transfers between devices: 25.7 us -> 24.2 us  [swap(): return lax.ppermute(x, ('replica', 'tensor'), pairs)]
    ppermute x14, waiting for transfers between devices: 4.24 us -> 4.74 us  [swap(): return lax.ppermute(x, ('replica', 'tensor'), pairs)]
  transfers between devices with their start and end apart: 15 -> 15, of which waited for: 5 -> 6; matrix products, arithmetic and copies ran while one was open for 2% -> 2% of each run, Pallas kernels for 9% -> 9%
where the time goes in v4:
time: 37.8 us; the launch traced here: 37.6 us
  starting transfers between devices  24.2 us (64%)
  Pallas kernels  6.26 us (17%)
  waiting for transfers between devices  5.14 us (14%)
  between operations  0.73 us (2%)
  local copies, waits for them, and re-layouts  0.72 us (2%)
  other arithmetic  0.51 us (1%)
    ppermute x14, starting transfers between devices, swap(): return lax.ppermute(x, ('replica', 'tensor'), pairs)  24.2 us
    ppermute x14, waiting for transfers between devices, swap(): return lax.ppermute(x, ('replica', 'tensor'), pairs)  4.74 us
    pallas_call x4, Pallas kernels, serve(): pl.pallas_call(functools.partial(serve_kernel, capacity, heads), out_shap...  3.3 us
    pallas_call x1, Pallas kernels, shards(): pl.pallas_call(functools.partial(pack_kernel, capacity, turns), out_shape...  2.48 us
  transfers between devices with their start and end apart: 15, of which 6 were waited for; matrix products, arithmetic and copies ran while one was open for 2% of the time, Pallas kernels for 9%

profile of v4, /device:TPU:0, one launch (start us, length us, event | category | flops | bytes accessed | tf_op | source)
XLA Modules:
  0.0 37.6 jit_solution(2883865380055879878)
XLA Ops:
  0.6 2.5 %pack.1 = (bf16[304,128]{1,0:T(8,128)(2,1)S(1)}, bf16[304,128]{1,0:T(8,128)(2,1)S(1)}, bf16[304,128]{1,0:T(8,128)(2,1)S(1)}, bf16[304,128]{1,0:T(8,128)(2,1)S(1)...) custom-call(bf16[32,4096]{1,0:T(8,128)(2,1)} %q_hbm.1, ...), custom_call_target="tpu_custom_call" | custom-call | tf_op jit(solution)/shard_map/pack/pallas_call | solution.py:257
  3.1 6.1 %collective-permute-start.12 = (bf16[304,128]{1,0:T(8,128)(2,1)S(1)}, bf16[304,128]{1,0:T(8,128)(2,1)S(1)}, u32[]{:S(2)}, u32[]{:S(2)}) collective-permute-start(bf16[304,128]{1,0:T(8,128)(2,1)S(1)} %get-tuple-element.40), channel_id=1, source_target_pairs={{0,14},{1,15},{2,12},{3,13},{4,10},{5,11},{6,8},{7,9},{8,6},{9,7},... | collective-permute-start | bytes 233480 | tf_op jit(solution)/shard_map/ppermute | solution.py:309
  9.2 0.2 collective-permute-start.8
  9.4 0.0 collective-permute-start.9
  9.4 5.1 %collective-permute-start.4 = (bf16[304,128]{1,0:T(8,128)(2,1)S(1)}, bf16[304,128]{1,0:T(8,128)(2,1)S(1)}, u32[]{:S(2)}, u32[]{:S(2)}) collective-permute-start(bf16[304,128]{1,0:T(8,128)(2,1)S(1)} %get-tuple-element.32), channel_id=1, source_target_pairs={{0,10},{1,5},{2,8},{3,7},{4,14},{5,1},{6,12},{7,3},{8,2},{9,13},{1... | collective-permute-start | bytes 233480 | tf_op jit(solution)/shard_map/ppermute | solution.py:309
  14.5 0.0 collective-permute-start.5
  14.5 0.0 collective-permute-done.12.blocks_and_answers_0_
  14.5 0.8 %collective-permute-start = (bf16[304,128]{1,0:T(8,128)(2,1)S(1)}, bf16[304,128]{1,0:T(8,128)(2,1)S(1)}, u32[]{:S(2)}, u32[]{:S(2)}) collective-permute-start(bf16[304,128]{1,0:T(8,128)(2,1)S(1)} %get-tuple-element.28), channel_id=1, source_target_pairs={{0,8},{1,3},{2,10},{3,1},{4,12},{5,7},{6,14},{7,5},{8,0},{9,11},{1... | collective-permute-start | bytes 233480 | tf_op jit(solution)/shard_map/ppermute | solution.py:309
  15.3 1.1 %collective-permute-done.8.blocks_and_answers_0_ = bf16[304,128]{1,0:T(8,128)(2,1)S(1)} collective-permute-done((bf16[304,128]{1,0:T(8,128)(2,1)S(1)}, bf16[304,128]{1,0:T(8,128)(2,1)S(1)}, u32[]{:S(2)}, u32[]{:S(2)}) %collective-permute-start.8) | collective-permute-done | bytes 77856 | tf_op jit(solution)/shard_map/ppermute | solution.py:309
  16.4 0.2 collective-permute-start.1
  16.6 0.8 %serve.7 = (bf16[256,128]{1,0:T(8,128)(2,1)S(1)}, bf16[256,128]{1,0:T(8,128)(2,1)S(1)}) custom-call(s32[4,32]{1,0:T(4,128)S(4)} %get-tuple-element.25.table_ref, bf16[128,16,512]{2,1,0:T(8,128)(2,1)S(1)} %get-tuple-element.26.key_ref, bf16[128,16,512]{2,1,0:T(8,128)(2,1)S(1)} %get-tuple-element.27.value_ref, ...), custom_call_target="tpu_custom_call" | custom-call | flops 10000000 | bytes 2000000 | tf_op jit(solution)/shard_map/serve/pallas_call | solution.py:292
  17.5 0.1 collective-permute-done.9.blocks_and_answers_1_
  17.5 3.7 %collective-permute-start.13 = (bf16[256,128]{1,0:T(8,128)(2,1)S(1)}, bf16[256,128]{1,0:T(8,128)(2,1)S(1)}, u32[]{:S(2)}, u32[]{:S(2)}) collective-permute-start(bf16[256,128]{1,0:T(8,128)(2,1)S(1)} %get-tuple-element.42), channel_id=1, source_target_pairs={{0,14},{1,15},{2,12},{3,13},{4,10},{5,11},{6,8},{7,9},{8,6},{9,7},... | collective-permute-start | bytes 196616 | tf_op jit(solution)/shard_map/ppermute | solution.py:309
  21.2 0.8 %serve.6 = (bf16[256,128]{1,0:T(8,128)(2,1)S(1)}, bf16[256,128]{1,0:T(8,128)(2,1)S(1)}) custom-call(s32[4,32]{1,0:T(4,128)S(4)} %get-tuple-element.25.table_ref, bf16[128,16,512]{2,1,0:T(8,128)(2,1)S(1)} %get-tuple-element.26.key_ref, bf16[128,16,512]{2,1,0:T(8,128)(2,1)S(1)} %get-tuple-element.27.value_ref, ...), custom_call_target="tpu_custom_call" | custom-call | flops 10000000 | bytes 2000000 | tf_op jit(solution)/shard_map/serve/pallas_call | solution.py:292
  22.1 0.0 collective-permute-done.4.blocks_and_answers_0_
  22.1 1.4 %collective-permute-start.10 = (bf16[256,128]{1,0:T(8,128)(2,1)S(1)}, bf16[256,128]{1,0:T(8,128)(2,1)S(1)}, u32[]{:S(2)}, u32[]{:S(2)}) collective-permute-start(bf16[256,128]{1,0:T(8,128)(2,1)S(1)} %get-tuple-element.38), channel_id=1, source_target_pairs={{0,12},{1,7},{2,14},{3,5},{4,8},{5,3},{6,10},{7,1},{8,4},{9,15},{1... | collective-permute-start | bytes 196616 | tf_op jit(solution)/shard_map/ppermute | solution.py:309
  23.5 0.0 collective-permute-done.5.blocks_and_answers_1_
  23.5 0.0 collective-permute-start.11
  23.5 0.8 %serve.5 = (bf16[256,128]{1,0:T(8,128)(2,1)S(1)}, bf16[256,128]{1,0:T(8,128)(2,1)S(1)}) custom-call(s32[4,32]{1,0:T(4,128)S(4)} %get-tuple-element.25.table_ref, bf16[128,16,512]{2,1,0:T(8,128)(2,1)S(1)} %get-tuple-element.26.key_ref, bf16[128,16,512]{2,1,0:T(8,128)(2,1)S(1)} %get-tuple-element.27.value_ref, ...), custom_call_target="tpu_custom_call" | custom-call | flops 10000000 | bytes 2000000 | tf_op jit(solution)/shard_map/serve/pallas_call | solution.py:292
  24.3 0.0 collective-permute-done.blocks_and_answers_0_
  24.3 4.0 %collective-permute-start.6 = (bf16[256,128]{1,0:T(8,128)(2,1)S(1)}, bf16[256,128]{1,0:T(8,128)(2,1)S(1)}, u32[]{:S(2)}, u32[]{:S(2)}) collective-permute-start(bf16[256,128]{1,0:T(8,128)(2,1)S(1)} %get-tuple-element.34), channel_id=1, source_target_pairs={{0,10},{1,5},{2,8},{3,7},{4,14},{5,1},{6,12},{7,3},{8,2},{9,13},{1... | collective-permute-start | bytes 196616 | tf_op jit(solution)/shard_map/ppermute | solution.py:309
  28.3 0.0 collective-permute-done.1.blocks_and_answers_1_
  28.4 0.0 copy-start
  28.4 0.0 collective-permute-start.7
  28.4 0.8 %serve.4 = (bf16[256,128]{1,0:T(8,128)(2,1)S(1)}, bf16[256,128]{1,0:T(8,128)(2,1)S(1)}) custom-call(s32[4,32]{1,0:T(4,128)S(4)} %get-tuple-element.25.table_ref, bf16[128,16,512]{2,1,0:T(8,128)(2,1)S(1)} %get-tuple-element.26.key_ref, bf16[128,16,512]{2,1,0:T(8,128)(2,1)S(1)} %get-tuple-element.27.value_ref, ...), custom_call_target="tpu_custom_call" | custom-call | flops 10000000 | bytes 2000000 | tf_op jit(solution)/shard_map/serve/pallas_call | solution.py:292
  29.2 0.0 collective-permute-done.13.rest_6_
  29.2 1.9 %collective-permute-start.2 = (bf16[256,128]{1,0:T(8,128)(2,1)S(1)}, bf16[256,128]{1,0:T(8,128)(2,1)S(1)}, u32[]{:S(2)}, u32[]{:S(2)}) collective-permute-start(bf16[256,128]{1,0:T(8,128)(2,1)S(1)} %get-tuple-element.30), channel_id=1, source_target_pairs={{0,8},{1,3},{2,10},{3,1},{4,12},{5,7},{6,14},{7,5},{8,0},{9,11},{1... | collective-permute-start | bytes 196616 | tf_op jit(solution)/shard_map/ppermute | solution.py:309
  31.2 0.0 collective-permute-done.10.rest_4_
  31.2 0.7 %collective-permute-start.3 = (bf16[256,128]{1,0:T(8,128)(2,1)S(1)}, bf16[256,128]{1,0:T(8,128)(2,1)S(1)}, u32[]{:S(2)}, u32[]{:S(2)}) collective-permute-start(bf16[256,128]{1,0:T(8,128)(2,1)S(1)} %get-tuple-element.31), channel_id=1, source_target_pairs={{0,2},{1,9},{2,0},{3,11},{4,6},{5,13},{6,4},{7,15},{8,10},{9,1},{1... | collective-permute-start | bytes 196616 | tf_op jit(solution)/shard_map/ppermute | solution.py:309
  31.8 0.0 copy-done
  31.9 0.0 collective-permute-done.11.rest_5_
  31.9 0.0 collective-permute-done.6.rest_2_
  31.9 0.7 %collective-permute-done.7.rest_3_ = bf16[256,128]{1,0:T(8,128)(2,1)S(1)} collective-permute-done((bf16[256,128]{1,0:T(8,128)(2,1)S(1)}, bf16[256,128]{1,0:T(8,128)(2,1)S(1)}, u32[]{:S(2)}, u32[]{:S(2)}) %collective-permute-start.7) | collective-permute-done | bytes 65568 | tf_op jit(solution)/shard_map/ppermute | solution.py:309
  32.6 1.8 %collective-permute-done.2.rest_0_ = bf16[256,128]{1,0:T(8,128)(2,1)S(1)} collective-permute-done((bf16[256,128]{1,0:T(8,128)(2,1)S(1)}, bf16[256,128]{1,0:T(8,128)(2,1)S(1)}, u32[]{:S(2)}, u32[]{:S(2)}) %collective-permute-start.2) | collective-permute-done | bytes 65568 | tf_op jit(solution)/shard_map/ppermute | solution.py:309
  34.4 1.0 %collective-permute-done.3.rest_1_ = bf16[256,128]{1,0:T(8,128)(2,1)S(1)} collective-permute-done((bf16[256,128]{1,0:T(8,128)(2,1)S(1)}, bf16[256,128]{1,0:T(8,128)(2,1)S(1)}, u32[]{:S(2)}, u32[]{:S(2)}) %collective-permute-start.3) | collective-permute-done | bytes 65568 | tf_op jit(solution)/shard_map/ppermute | solution.py:309
  35.4 0.5 %unpack.1 = (bf16[32,4096]{1,0:T(8,128)(2,1)S(1)}, f32[1,32]{1,0:T(1,128)S(1)}) custom-call(s32[64]{0:T(128)S(4)} %get-tuple-element.24.row_ref, bf16[1,4096]{1,0:T(2,128)(2,1)S(1)} %reshape.15.probe_ref, bf16[256,128]{1,0:T(8,128)(2,1)S(1)} %collective-permute-done.2.rest_0_, bf16[256,128]{1,0:T(8,128)(2,1)S(1)} %collective-permute-done.3.rest_1_, ...), custom_call_target="tpu_custom_call" | custom-call | tf_op jit(solution)/shard_map/unpack/pallas_call | solution.py:317
  35.9 0.1 collective-permute-start.14
  36.0 0.7 %copy.12 = bf16[32,4096]{1,0:T(8,128)(2,1)} copy(bf16[32,4096]{1,0:T(8,128)(2,1)S(1)} %get-tuple-element.46) | data formatting | bytes 524288
  36.7 0.4 %collective-permute-done.14 = f32[1,32]{1,0:T(1,128)S(1)} collective-permute-done((f32[1,32]{1,0:T(1,128)S(1)}, f32[1,32]{1,0:T(1,128)S(1)}, u32[]{:S(2)}, u32[]{:S(2)}) %collective-permute-start.14) | collective-permute-done | bytes 160 | tf_op jit(solution)/shard_map/ppermute | solution.py:326
  37.1 0.5 %add_bitcast_fusion = f32[32]{0:T(128)} fusion(f32[1,32]{1,0:T(1,128)S(1)} %get-tuple-element.45, f32[1,32]{1,0:T(1,128)S(1)} %collective-permute-done.14), kind=kLoop, calls=%fused_computation | loop fusion | flops 32 | bytes 384 | tf_op jit(solution)/shard_map/squeeze | solution.py:327
  (1 shorter events, 0.0 us)
Async XLA Ops:
  3.1 11.4 %collective-permute-start.12 = (bf16[304,128]{1,0:T(8,128)(2,1)S(1)}, bf16[304,128]{1,0:T(8,128)(2,1)S(1)}, u32[]{:S(2)}, u32[]{:S(2)}) collective-permute-start(bf16[304,128]{1,0:T(8,128)(2,1)S(1)} %get-tuple-element.40), channel_id=1, source_target_pairs={{0,14},{1,15},{2,12},{3,13},{4,10},{5,11},{6,8},{7,9},{8,6},{9,7},... | collective-permute-start | bytes 233480 | tf_op jit(solution)/shard_map/ppermute | solution.py:309
  9.2 7.2 %collective-permute-start.8 = (bf16[304,128]{1,0:T(8,128)(2,1)S(1)}, bf16[304,128]{1,0:T(8,128)(2,1)S(1)}, u32[]{:S(2)}, u32[]{:S(2)}) collective-permute-start(bf16[304,128]{1,0:T(8,128)(2,1)S(1)} %get-tuple-element.36), channel_id=1, source_target_pairs={{0,12},{1,7},{2,14},{3,5},{4,8},{5,3},{6,10},{7,1},{8,4},{9,15},{1... | collective-permute-start | bytes 233480 | tf_op jit(solution)/shard_map/ppermute | solution.py:309
  9.4 8.1 %collective-permute-start.9 = (bf16[304,128]{1,0:T(8,128)(2,1)S(1)}, bf16[304,128]{1,0:T(8,128)(2,1)S(1)}, u32[]{:S(2)}, u32[]{:S(2)}) collective-permute-start(bf16[304,128]{1,0:T(8,128)(2,1)S(1)} %get-tuple-element.37), channel_id=1, source_target_pairs={{0,6},{1,13},{2,4},{3,15},{4,2},{5,9},{6,0},{7,11},{8,14},{9,5},{1... | collective-permute-start | bytes 233480 | tf_op jit(solution)/shard_map/ppermute | solution.py:309
  9.4 12.7 %collective-permute-start.4 = (bf16[304,128]{1,0:T(8,128)(2,1)S(1)}, bf16[304,128]{1,0:T(8,128)(2,1)S(1)}, u32[]{:S(2)}, u32[]{:S(2)}) collective-permute-start(bf16[304,128]{1,0:T(8,128)(2,1)S(1)} %get-tuple-element.32), channel_id=1, source_target_pairs={{0,10},{1,5},{2,8},{3,7},{4,14},{5,1},{6,12},{7,3},{8,2},{9,13},{1... | collective-permute-start | bytes 233480 | tf_op jit(solution)/shard_map/ppermute | solution.py:309
  14.5 9.0 %collective-permute-start.5 = (bf16[304,128]{1,0:T(8,128)(2,1)S(1)}, bf16[304,128]{1,0:T(8,128)(2,1)S(1)}, u32[]{:S(2)}, u32[]{:S(2)}) collective-permute-start(bf16[304,128]{1,0:T(8,128)(2,1)S(1)} %get-tuple-element.33), channel_id=1, source_target_pairs={{0,4},{1,11},{2,6},{3,9},{4,0},{5,15},{6,2},{7,13},{8,12},{9,3},{1... | collective-permute-start | bytes 233480 | tf_op jit(solution)/shard_map/ppermute | solution.py:309
  14.5 9.8 %collective-permute-start = (bf16[304,128]{1,0:T(8,128)(2,1)S(1)}, bf16[304,128]{1,0:T(8,128)(2,1)S(1)}, u32[]{:S(2)}, u32[]{:S(2)}) collective-permute-start(bf16[304,128]{1,0:T(8,128)(2,1)S(1)} %get-tuple-element.28), channel_id=1, source_target_pairs={{0,8},{1,3},{2,10},{3,1},{4,12},{5,7},{6,14},{7,5},{8,0},{9,11},{1... | collective-permute-start | bytes 233480 | tf_op jit(solution)/shard_map/ppermute | solution.py:309
  16.4 12.0 %collective-permute-start.1 = (bf16[304,128]{1,0:T(8,128)(2,1)S(1)}, bf16[304,128]{1,0:T(8,128)(2,1)S(1)}, u32[]{:S(2)}, u32[]{:S(2)}) collective-permute-start(bf16[304,128]{1,0:T(8,128)(2,1)S(1)} %get-tuple-element.29), channel_id=1, source_target_pairs={{0,2},{1,9},{2,0},{3,11},{4,6},{5,13},{6,4},{7,15},{8,10},{9,1},{1... | collective-permute-start | bytes 233480 | tf_op jit(solution)/shard_map/ppermute | solution.py:309
  17.5 11.7 %collective-permute-start.13 = (bf16[256,128]{1,0:T(8,128)(2,1)S(1)}, bf16[256,128]{1,0:T(8,128)(2,1)S(1)}, u32[]{:S(2)}, u32[]{:S(2)}) collective-permute-start(bf16[256,128]{1,0:T(8,128)(2,1)S(1)} %get-tuple-element.42), channel_id=1, source_target_pairs={{0,14},{1,15},{2,12},{3,13},{4,10},{5,11},{6,8},{7,9},{8,6},{9,7},... | collective-permute-start | bytes 196616 | tf_op jit(solution)/shard_map/ppermute | solution.py:309
  22.1 9.1 %collective-permute-start.10 = (bf16[256,128]{1,0:T(8,128)(2,1)S(1)}, bf16[256,128]{1,0:T(8,128)(2,1)S(1)}, u32[]{:S(2)}, u32[]{:S(2)}) collective-permute-start(bf16[256,128]{1,0:T(8,128)(2,1)S(1)} %get-tuple-element.38), channel_id=1, source_target_pairs={{0,12},{1,7},{2,14},{3,5},{4,8},{5,3},{6,10},{7,1},{8,4},{9,15},{1... | collective-permute-start | bytes 196616 | tf_op jit(solution)/shard_map/ppermute | solution.py:309
  23.5 8.4 %collective-permute-start.11 = (bf16[256,128]{1,0:T(8,128)(2,1)S(1)}, bf16[256,128]{1,0:T(8,128)(2,1)S(1)}, u32[]{:S(2)}, u32[]{:S(2)}) collective-permute-start(bf16[256,128]{1,0:T(8,128)(2,1)S(1)} %get-tuple-element.39), channel_id=1, source_target_pairs={{0,6},{1,13},{2,4},{3,15},{4,2},{5,9},{6,0},{7,11},{8,14},{9,5},{1... | collective-permute-start | bytes 196616 | tf_op jit(solution)/shard_map/ppermute | solution.py:309
  24.3 7.5 %collective-permute-start.6 = (bf16[256,128]{1,0:T(8,128)(2,1)S(1)}, bf16[256,128]{1,0:T(8,128)(2,1)S(1)}, u32[]{:S(2)}, u32[]{:S(2)}) collective-permute-start(bf16[256,128]{1,0:T(8,128)(2,1)S(1)} %get-tuple-element.34), channel_id=1, source_target_pairs={{0,10},{1,5},{2,8},{3,7},{4,14},{5,1},{6,12},{7,3},{8,2},{9,13},{1... | collective-permute-start | bytes 196616 | tf_op jit(solution)/shard_map/ppermute | solution.py:309
  28.4 3.5 %copy-start = (bf16[4096]{0:T(1024)(128)(2,1)S(1)}, bf16[4096]{0:T(1024)(128)(2,1)}, u32[]{:S(2)}) copy-start(bf16[4096]{0:T(1024)(128)(2,1)} %param.19) | copy-start | bytes 24580
  28.4 4.3 %collective-permute-start.7 = (bf16[256,128]{1,0:T(8,128)(2,1)S(1)}, bf16[256,128]{1,0:T(8,128)(2,1)S(1)}, u32[]{:S(2)}, u32[]{:S(2)}) collective-permute-start(bf16[256,128]{1,0:T(8,128)(2,1)S(1)} %get-tuple-element.35), channel_id=1, source_target_pairs={{0,4},{1,11},{2,6},{3,9},{4,0},{5,15},{6,2},{7,13},{8,12},{9,3},{1... | collective-permute-start | bytes 196616 | tf_op jit(solution)/shard_map/ppermute | solution.py:309
  29.2 5.2 %collective-permute-start.2 = (bf16[256,128]{1,0:T(8,128)(2,1)S(1)}, bf16[256,128]{1,0:T(8,128)(2,1)S(1)}, u32[]{:S(2)}, u32[]{:S(2)}) collective-permute-start(bf16[256,128]{1,0:T(8,128)(2,1)S(1)} %get-tuple-element.30), channel_id=1, source_target_pairs={{0,8},{1,3},{2,10},{3,1},{4,12},{5,7},{6,14},{7,5},{8,0},{9,11},{1... | collective-permute-start | bytes 196616 | tf_op jit(solution)/shard_map/ppermute | solution.py:309
  31.2 4.3 %collective-permute-start.3 = (bf16[256,128]{1,0:T(8,128)(2,1)S(1)}, bf16[256,128]{1,0:T(8,128)(2,1)S(1)}, u32[]{:S(2)}, u32[]{:S(2)}) collective-permute-start(bf16[256,128]{1,0:T(8,128)(2,1)S(1)} %get-tuple-element.31), channel_id=1, source_target_pairs={{0,2},{1,9},{2,0},{3,11},{4,6},{5,13},{6,4},{7,15},{8,10},{9,1},{1... | collective-permute-start | bytes 196616 | tf_op jit(solution)/shard_map/ppermute | solution.py:309
  35.9 1.2 %collective-permute-start.14 = (f32[1,32]{1,0:T(1,128)S(1)}, f32[1,32]{1,0:T(1,128)S(1)}, u32[]{:S(2)}, u32[]{:S(2)}) collective-permute-start(f32[1,32]{1,0:T(1,128)S(1)} %get-tuple-element.45), channel_id=1, source_target_pairs={{0,1},{1,0},{2,3},{3,2},{4,5},{5,4},{6,7},{7,6},{8,9},{9,8},{10,11... | collective-permute-start | bytes 392 | tf_op jit(solution)/shard_map/ppermute | solution.py:326

commit v5 on v4

--- a/solution.py
+++ b/solution.py
@@ -9,7 +9,6 @@
 
 HEAD_SIZE = 128
 TILE = 16
-TOGETHER = 2
 masked_score = -1e30
 f32, bf16, i32 = jnp.float32, jnp.bfloat16, jnp.int32
 
@@ -28,9 +27,11 @@
 
 def partners_in_turn(replicas):
     near, far = list(range(1, replicas // 2)), list(range(replicas // 2, replicas))
-    pairs = list(zip(far, near))
-    even = [m for pair in pairs for m in pair] + far[len(near) :] + [0]
-    odd = [m for pair in pairs for m in pair[::-1]] + far[len(near) :] + [0]
+    other_far = list(far)
+    for i in range(1, len(far) - 1, 2):
+        other_far[i : i + 2] = other_far[i + 1], other_far[i]
+    even = [m for pair in zip(far, near) for m in pair] + far[len(near) :] + [0]
+    odd = [m for pair in zip(near, other_far) for m in pair] + other_far[len(near) :] + [0]
     return even, odd
 
 
@@ -309,10 +310,11 @@
         return lax.ppermute(x, ("replica", "tensor"), pairs)
 
     arrived = [swap(blocks[turn], turn) for turn in range(replicas - 1)] + [blocks[replicas - 1]]
-    answers = []
-    for turn in range(0, replicas, TOGETHER):
-        for answer in serve(arrived[turn : turn + TOGETHER]):
-            answers.append(swap(answer, len(answers)) if len(answers) < replicas - 1 else answer)
+    answers = [None] * replicas
+    groups = [[0, replicas - 1]] + [[turn, turn + 1] for turn in range(1, replicas - 1, 2)]
+    for group in groups:
+        for turn, answer in zip(group, serve([arrived[turn] for turn in group])):
+            answers[turn] = swap(answer, turn) if turn < replicas - 1 else answer
 
     attended, partial_reward = pl.pallas_call(
         functools.partial(unpack_kernel, capacity, heads, rows),

time: 37.8 us -> 37.6 us (level)
  waiting for transfers between devices: 5.14 us -> 4.51 us
  starting transfers between devices: 24.2 us -> 24.7 us
    ppermute x14, waiting for transfers between devices: 4.74 us -> 4.1 us  [swap(): return lax.ppermute(x, ('replica', 'tensor'), pairs)]
    ppermute x14, starting transfers between devices: 24.2 us -> 24.6 us  [swap(): return lax.ppermute(x, ('replica', 'tensor'), pairs)]
  transfers between devices with their start and end apart: 15 -> 15, of which waited for: 6 -> 4; matrix products, arithmetic and copies ran while one was open for 2% -> 2% of each run, Pallas kernels for 9% -> 9%
where the time goes in v5:
time: 37.6 us; the launch traced here: 37.4 us
  starting transfers between devices  24.7 us (66%)
  Pallas kernels  6.26 us (17%)
  waiting for transfers between devices  4.51 us (12%)
  between operations  0.75 us (2%)
  local copies, waits for them, and re-layouts  0.72 us (2%)
  other arithmetic  0.51 us (1%)
    ppermute x14, starting transfers between devices, swap(): return lax.ppermute(x, ('replica', 'tensor'), pairs)  24.6 us
    ppermute x14, waiting for transfers between devices, swap(): return lax.ppermute(x, ('replica', 'tensor'), pairs)  4.1 us
    pallas_call x4, Pallas kernels, serve(): pl.pallas_call(functools.partial(serve_kernel, capacity, heads), out_shap...  3.3 us
    pallas_call x1, Pallas kernels, shards(): pl.pallas_call(functools.partial(pack_kernel, capacity, turns), out_shape...  2.48 us
  transfers between devices with their start and end apart: 15, of which 4 were waited for; matrix products, arithmetic and copies ran while one was open for 2% of the time, Pallas kernels for 9%

profile of v5, /device:TPU:0, one launch (start us, length us, event | category | flops | bytes accessed | tf_op | source)
XLA Modules:
  0.0 37.4 jit_solution(8210266744577301782)
XLA Ops:
  0.6 2.5 %pack.1 = (bf16[304,128]{1,0:T(8,128)(2,1)S(1)}, bf16[304,128]{1,0:T(8,128)(2,1)S(1)}, bf16[304,128]{1,0:T(8,128)(2,1)S(1)}, bf16[304,128]{1,0:T(8,128)(2,1)S(1)...) custom-call(bf16[32,4096]{1,0:T(8,128)(2,1)} %q_hbm.1, ...), custom_call_target="tpu_custom_call" | custom-call | tf_op jit(solution)/shard_map/pack/pallas_call | solution.py:258
  3.1 4.0 %collective-permute-start.10 = (bf16[304,128]{1,0:T(8,128)(2,1)S(1)}, bf16[304,128]{1,0:T(8,128)(2,1)S(1)}, u32[]{:S(2)}, u32[]{:S(2)}) collective-permute-start(bf16[304,128]{1,0:T(8,128)(2,1)S(1)} %get-tuple-element.39), channel_id=1, source_target_pairs={{0,6},{1,11},{2,4},{3,9},{4,2},{5,15},{6,0},{7,13},{8,14},{9,3},{1... | collective-permute-start | bytes 233480 | tf_op jit(solution)/shard_map/ppermute | solution.py:310
  7.2 2.4 %collective-permute-start.11 = (bf16[304,128]{1,0:T(8,128)(2,1)S(1)}, bf16[304,128]{1,0:T(8,128)(2,1)S(1)}, u32[]{:S(2)}, u32[]{:S(2)}) collective-permute-start(bf16[304,128]{1,0:T(8,128)(2,1)S(1)} %get-tuple-element.40), channel_id=1, source_target_pairs={{0,14},{1,15},{2,12},{3,13},{4,10},{5,11},{6,8},{7,9},{8,6},{9,7},... | collective-permute-start | bytes 233480 | tf_op jit(solution)/shard_map/ppermute | solution.py:310
  9.6 0.7 %collective-permute-start.6 = (bf16[304,128]{1,0:T(8,128)(2,1)S(1)}, bf16[304,128]{1,0:T(8,128)(2,1)S(1)}, u32[]{:S(2)}, u32[]{:S(2)}) collective-permute-start(bf16[304,128]{1,0:T(8,128)(2,1)S(1)} %get-tuple-element.35), channel_id=1, source_target_pairs={{0,4},{1,13},{2,6},{3,15},{4,0},{5,9},{6,2},{7,11},{8,12},{9,5},{1... | collective-permute-start | bytes 233480 | tf_op jit(solution)/shard_map/ppermute | solution.py:310
  10.3 1.0 %collective-permute-start.7 = (bf16[304,128]{1,0:T(8,128)(2,1)S(1)}, bf16[304,128]{1,0:T(8,128)(2,1)S(1)}, u32[]{:S(2)}, u32[]{:S(2)}) collective-permute-start(bf16[304,128]{1,0:T(8,128)(2,1)S(1)} %get-tuple-element.36), channel_id=1, source_target_pairs={{0,12},{1,7},{2,14},{3,5},{4,8},{5,3},{6,10},{7,1},{8,4},{9,15},{1... | collective-permute-start | bytes 233480 | tf_op jit(solution)/shard_map/ppermute | solution.py:310
  11.2 1.2 %collective-permute-start.2 = (bf16[304,128]{1,0:T(8,128)(2,1)S(1)}, bf16[304,128]{1,0:T(8,128)(2,1)S(1)}, u32[]{:S(2)}, u32[]{:S(2)}) collective-permute-start(bf16[304,128]{1,0:T(8,128)(2,1)S(1)} %get-tuple-element.31), channel_id=1, source_target_pairs={{0,2},{1,9},{2,0},{3,11},{4,6},{5,13},{6,4},{7,15},{8,10},{9,1},{1... | collective-permute-start | bytes 233480 | tf_op jit(solution)/shard_map/ppermute | solution.py:310
  12.5 0.0 collective-permute-done.10.blocks_and_answers_0_
  12.5 2.1 %collective-permute-start.3 = (bf16[304,128]{1,0:T(8,128)(2,1)S(1)}, bf16[304,128]{1,0:T(8,128)(2,1)S(1)}, u32[]{:S(2)}, u32[]{:S(2)}) collective-permute-start(bf16[304,128]{1,0:T(8,128)(2,1)S(1)} %get-tuple-element.32), channel_id=1, source_target_pairs={{0,10},{1,5},{2,8},{3,7},{4,14},{5,1},{6,12},{7,3},{8,2},{9,13},{1... | collective-permute-start | bytes 233480 | tf_op jit(solution)/shard_map/ppermute | solution.py:310
  14.5 0.7 %collective-permute-done.11.blocks_and_answers_1_ = bf16[304,128]{1,0:T(8,128)(2,1)S(1)} collective-permute-done((bf16[304,128]{1,0:T(8,128)(2,1)S(1)}, bf16[304,128]{1,0:T(8,128)(2,1)S(1)}, u32[]{:S(2)}, u32[]{:S(2)}) %collective-permute-start.11) | collective-permute-done | bytes 77856 | tf_op jit(solution)/shard_map/ppermute | solution.py:310
  15.2 2.7 %collective-permute-start = (bf16[304,128]{1,0:T(8,128)(2,1)S(1)}, bf16[304,128]{1,0:T(8,128)(2,1)S(1)}, u32[]{:S(2)}, u32[]{:S(2)}) collective-permute-start(bf16[304,128]{1,0:T(8,128)(2,1)S(1)} %get-tuple-element.28), channel_id=1, source_target_pairs={{0,8},{1,3},{2,10},{3,1},{4,12},{5,7},{6,14},{7,5},{8,0},{9,11},{1... | collective-permute-start | bytes 233480 | tf_op jit(solution)/shard_map/ppermute | solution.py:310
  17.9 0.8 %serve.7 = (bf16[256,128]{1,0:T(8,128)(2,1)S(1)}, bf16[256,128]{1,0:T(8,128)(2,1)S(1)}) custom-call(s32[4,32]{1,0:T(4,128)S(4)} %get-tuple-element.25.table_ref, bf16[128,16,512]{2,1,0:T(8,128)(2,1)S(1)} %get-tuple-element.26.key_ref, bf16[128,16,512]{2,1,0:T(8,128)(2,1)S(1)} %get-tuple-element.27.value_ref, ...), custom_call_target="tpu_custom_call" | custom-call | flops 10000000 | bytes 2000000 | tf_op jit(solution)/shard_map/serve/pallas_call | solution.py:293
  18.7 0.0 collective-permute-done.6.blocks_and_answers_0_
  18.7 0.2 collective-permute-start.12
  18.9 0.0 collective-permute-done.7.blocks_and_answers_1_
  18.9 2.5 %collective-permute-start.13 = (bf16[256,128]{1,0:T(8,128)(2,1)S(1)}, bf16[256,128]{1,0:T(8,128)(2,1)S(1)}, u32[]{:S(2)}, u32[]{:S(2)}) collective-permute-start(bf16[256,128]{1,0:T(8,128)(2,1)S(1)} %get-tuple-element.42), channel_id=1, source_target_pairs={{0,14},{1,15},{2,12},{3,13},{4,10},{5,11},{6,8},{7,9},{8,6},{9,7},... | collective-permute-start | bytes 196616 | tf_op jit(solution)/shard_map/ppermute | solution.py:310
  21.4 0.8 %serve.6 = (bf16[256,128]{1,0:T(8,128)(2,1)S(1)}, bf16[256,128]{1,0:T(8,128)(2,1)S(1)}) custom-call(s32[4,32]{1,0:T(4,128)S(4)} %get-tuple-element.25.table_ref, bf16[128,16,512]{2,1,0:T(8,128)(2,1)S(1)} %get-tuple-element.26.key_ref, bf16[128,16,512]{2,1,0:T(8,128)(2,1)S(1)} %get-tuple-element.27.value_ref, ...), custom_call_target="tpu_custom_call" | custom-call | flops 10000000 | bytes 2000000 | tf_op jit(solution)/shard_map/serve/pallas_call | solution.py:293
  22.2 0.0 collective-permute-done.2.blocks_and_answers_0_
  22.2 2.0 %collective-permute-start.8 = (bf16[256,128]{1,0:T(8,128)(2,1)S(1)}, bf16[256,128]{1,0:T(8,128)(2,1)S(1)}, u32[]{:S(2)}, u32[]{:S(2)}) collective-permute-start(bf16[256,128]{1,0:T(8,128)(2,1)S(1)} %get-tuple-element.37), channel_id=1, source_target_pairs={{0,4},{1,13},{2,6},{3,15},{4,0},{5,9},{6,2},{7,11},{8,12},{9,5},{1... | collective-permute-start | bytes 196616 | tf_op jit(solution)/shard_map/ppermute | solution.py:310
  24.2 0.0 collective-permute-done.3.blocks_and_answers_1_
  24.2 1.4 %collective-permute-start.9 = (bf16[256,128]{1,0:T(8,128)(2,1)S(1)}, bf16[256,128]{1,0:T(8,128)(2,1)S(1)}, u32[]{:S(2)}, u32[]{:S(2)}) collective-permute-start(bf16[256,128]{1,0:T(8,128)(2,1)S(1)} %get-tuple-element.38), channel_id=1, source_target_pairs={{0,12},{1,7},{2,14},{3,5},{4,8},{5,3},{6,10},{7,1},{8,4},{9,15},{1... | collective-permute-start | bytes 196616 | tf_op jit(solution)/shard_map/ppermute | solution.py:310
  25.6 0.8 %serve.5 = (bf16[256,128]{1,0:T(8,128)(2,1)S(1)}, bf16[256,128]{1,0:T(8,128)(2,1)S(1)}) custom-call(s32[4,32]{1,0:T(4,128)S(4)} %get-tuple-element.25.table_ref, bf16[128,16,512]{2,1,0:T(8,128)(2,1)S(1)} %get-tuple-element.26.key_ref, bf16[128,16,512]{2,1,0:T(8,128)(2,1)S(1)} %get-tuple-element.27.value_ref, ...), custom_call_target="tpu_custom_call" | custom-call | flops 10000000 | bytes 2000000 | tf_op jit(solution)/shard_map/serve/pallas_call | solution.py:293
  26.4 0.0 collective-permute-done.blocks_and_answers_0_
  26.4 1.6 %collective-permute-start.4 = (bf16[256,128]{1,0:T(8,128)(2,1)S(1)}, bf16[256,128]{1,0:T(8,128)(2,1)S(1)}, u32[]{:S(2)}, u32[]{:S(2)}) collective-permute-start(bf16[256,128]{1,0:T(8,128)(2,1)S(1)} %get-tuple-element.33), channel_id=1, source_target_pairs={{0,2},{1,9},{2,0},{3,11},{4,6},{5,13},{6,4},{7,15},{8,10},{9,1},{1... | collective-permute-start | bytes 196616 | tf_op jit(solution)/shard_map/ppermute | solution.py:310
  28.0 0.0 copy-start
  28.0 0.8 %serve.4 = (bf16[256,128]{1,0:T(8,128)(2,1)S(1)}, bf16[256,128]{1,0:T(8,128)(2,1)S(1)}) custom-call(s32[4,32]{1,0:T(4,128)S(4)} %get-tuple-element.25.table_ref, bf16[128,16,512]{2,1,0:T(8,128)(2,1)S(1)} %get-tuple-element.26.key_ref, bf16[128,16,512]{2,1,0:T(8,128)(2,1)S(1)} %get-tuple-element.27.value_ref, ...), custom_call_target="tpu_custom_call" | custom-call | flops 10000000 | bytes 2000000 | tf_op jit(solution)/shard_map/serve/pallas_call | solution.py:293
  28.9 0.0 collective-permute-done.12.rest_5_
  28.9 0.2 collective-permute-start.5
  29.1 0.0 collective-permute-done.13.rest_6_
  29.1 2.7 %collective-permute-start.1 = (bf16[256,128]{1,0:T(8,128)(2,1)S(1)}, bf16[256,128]{1,0:T(8,128)(2,1)S(1)}, u32[]{:S(2)}, u32[]{:S(2)}) collective-permute-start(bf16[256,128]{1,0:T(8,128)(2,1)S(1)} %get-tuple-element.30), channel_id=1, source_target_pairs={{0,8},{1,3},{2,10},{3,1},{4,12},{5,7},{6,14},{7,5},{8,0},{9,11},{1... | collective-permute-start | bytes 196616 | tf_op jit(solution)/shard_map/ppermute | solution.py:310
  31.8 0.0 copy-done
  31.8 0.0 collective-permute-done.8.rest_3_
  31.8 0.0 collective-permute-done.9.rest_4_
  31.8 0.0 collective-permute-done.4.rest_1_
  31.8 3.2 %collective-permute-done.5.rest_2_ = bf16[256,128]{1,0:T(8,128)(2,1)S(1)} collective-permute-done((bf16[256,128]{1,0:T(8,128)(2,1)S(1)}, bf16[256,128]{1,0:T(8,128)(2,1)S(1)}, u32[]{:S(2)}, u32[]{:S(2)}) %collective-permute-start.5) | collective-permute-done | bytes 65568 | tf_op jit(solution)/shard_map/ppermute | solution.py:310
  35.0 0.2 collective-permute-done.1.rest_0_
  35.2 0.5 %unpack.1 = (bf16[32,4096]{1,0:T(8,128)(2,1)S(1)}, f32[1,32]{1,0:T(1,128)S(1)}) custom-call(s32[64]{0:T(128)S(4)} %get-tuple-element.24.row_ref, bf16[1,4096]{1,0:T(2,128)(2,1)S(1)} %reshape.15.probe_ref, bf16[256,128]{1,0:T(8,128)(2,1)S(1)} %collective-permute-done.1.rest_0_, bf16[256,128]{1,0:T(8,128)(2,1)S(1)} %collective-permute-done.4.rest_1_, ...), custom_call_target="tpu_custom_call" | custom-call | tf_op jit(solution)/shard_map/unpack/pallas_call | solution.py:319
  35.7 0.1 collective-permute-start.14
  35.8 0.7 %copy.12 = bf16[32,4096]{1,0:T(8,128)(2,1)} copy(bf16[32,4096]{1,0:T(8,128)(2,1)S(1)} %get-tuple-element.46) | data formatting | bytes 524288
  36.5 0.4 %collective-permute-done.14 = f32[1,32]{1,0:T(1,128)S(1)} collective-permute-done((f32[1,32]{1,0:T(1,128)S(1)}, f32[1,32]{1,0:T(1,128)S(1)}, u32[]{:S(2)}, u32[]{:S(2)}) %collective-permute-start.14) | collective-permute-done | bytes 160 | tf_op jit(solution)/shard_map/ppermute | solution.py:328
  36.9 0.5 %add_bitcast_fusion = f32[32]{0:T(128)} fusion(f32[1,32]{1,0:T(1,128)S(1)} %get-tuple-element.45, f32[1,32]{1,0:T(1,128)S(1)} %collective-permute-done.14), kind=kLoop, calls=%fused_computation | loop fusion | flops 32 | bytes 384 | tf_op jit(solution)/shard_map/squeeze | solution.py:329
  (1 shorter events, 0.0 us)
Async XLA Ops:
  3.1 9.3 %collective-permute-start.10 = (bf16[304,128]{1,0:T(8,128)(2,1)S(1)}, bf16[304,128]{1,0:T(8,128)(2,1)S(1)}, u32[]{:S(2)}, u32[]{:S(2)}) collective-permute-start(bf16[304,128]{1,0:T(8,128)(2,1)S(1)} %get-tuple-element.39), channel_id=1, source_target_pairs={{0,6},{1,11},{2,4},{3,9},{4,2},{5,15},{6,0},{7,13},{8,14},{9,3},{1... | collective-permute-start | bytes 233480 | tf_op jit(solution)/shard_map/ppermute | solution.py:310
  7.2 8.0 %collective-permute-start.11 = (bf16[304,128]{1,0:T(8,128)(2,1)S(1)}, bf16[304,128]{1,0:T(8,128)(2,1)S(1)}, u32[]{:S(2)}, u32[]{:S(2)}) collective-permute-start(bf16[304,128]{1,0:T(8,128)(2,1)S(1)} %get-tuple-element.40), channel_id=1, source_target_pairs={{0,14},{1,15},{2,12},{3,13},{4,10},{5,11},{6,8},{7,9},{8,6},{9,7},... | collective-permute-start | bytes 233480 | tf_op jit(solution)/shard_map/ppermute | solution.py:310
  9.6 9.1 %collective-permute-start.6 = (bf16[304,128]{1,0:T(8,128)(2,1)S(1)}, bf16[304,128]{1,0:T(8,128)(2,1)S(1)}, u32[]{:S(2)}, u32[]{:S(2)}) collective-permute-start(bf16[304,128]{1,0:T(8,128)(2,1)S(1)} %get-tuple-element.35), channel_id=1, source_target_pairs={{0,4},{1,13},{2,6},{3,15},{4,0},{5,9},{6,2},{7,11},{8,12},{9,5},{1... | collective-permute-start | bytes 233480 | tf_op jit(solution)/shard_map/ppermute | solution.py:310
  10.3 8.6 %collective-permute-start.7 = (bf16[304,128]{1,0:T(8,128)(2,1)S(1)}, bf16[304,128]{1,0:T(8,128)(2,1)S(1)}, u32[]{:S(2)}, u32[]{:S(2)}) collective-permute-start(bf16[304,128]{1,0:T(8,128)(2,1)S(1)} %get-tuple-element.36), channel_id=1, source_target_pairs={{0,12},{1,7},{2,14},{3,5},{4,8},{5,3},{6,10},{7,1},{8,4},{9,15},{1... | collective-permute-start | bytes 233480 | tf_op jit(solution)/shard_map/ppermute | solution.py:310
  11.2 11.0 %collective-permute-start.2 = (bf16[304,128]{1,0:T(8,128)(2,1)S(1)}, bf16[304,128]{1,0:T(8,128)(2,1)S(1)}, u32[]{:S(2)}, u32[]{:S(2)}) collective-permute-start(bf16[304,128]{1,0:T(8,128)(2,1)S(1)} %get-tuple-element.31), channel_id=1, source_target_pairs={{0,2},{1,9},{2,0},{3,11},{4,6},{5,13},{6,4},{7,15},{8,10},{9,1},{1... | collective-permute-start | bytes 233480 | tf_op jit(solution)/shard_map/ppermute | solution.py:310
  12.5 11.7 %collective-permute-start.3 = (bf16[304,128]{1,0:T(8,128)(2,1)S(1)}, bf16[304,128]{1,0:T(8,128)(2,1)S(1)}, u32[]{:S(2)}, u32[]{:S(2)}) collective-permute-start(bf16[304,128]{1,0:T(8,128)(2,1)S(1)} %get-tuple-element.32), channel_id=1, source_target_pairs={{0,10},{1,5},{2,8},{3,7},{4,14},{5,1},{6,12},{7,3},{8,2},{9,13},{1... | collective-permute-start | bytes 233480 | tf_op jit(solution)/shard_map/ppermute | solution.py:310
  15.2 11.2 %collective-permute-start = (bf16[304,128]{1,0:T(8,128)(2,1)S(1)}, bf16[304,128]{1,0:T(8,128)(2,1)S(1)}, u32[]{:S(2)}, u32[]{:S(2)}) collective-permute-start(bf16[304,128]{1,0:T(8,128)(2,1)S(1)} %get-tuple-element.28), channel_id=1, source_target_pairs={{0,8},{1,3},{2,10},{3,1},{4,12},{5,7},{6,14},{7,5},{8,0},{9,11},{1... | collective-permute-start | bytes 233480 | tf_op jit(solution)/shard_map/ppermute | solution.py:310
  18.7 10.2 %collective-permute-start.12 = (bf16[256,128]{1,0:T(8,128)(2,1)S(1)}, bf16[256,128]{1,0:T(8,128)(2,1)S(1)}, u32[]{:S(2)}, u32[]{:S(2)}) collective-permute-start(bf16[256,128]{1,0:T(8,128)(2,1)S(1)} %get-tuple-element.41), channel_id=1, source_target_pairs={{0,6},{1,11},{2,4},{3,9},{4,2},{5,15},{6,0},{7,13},{8,14},{9,3},{1... | collective-permute-start | bytes 196616 | tf_op jit(solution)/shard_map/ppermute | solution.py:310
  18.9 10.2 %collective-permute-start.13 = (bf16[256,128]{1,0:T(8,128)(2,1)S(1)}, bf16[256,128]{1,0:T(8,128)(2,1)S(1)}, u32[]{:S(2)}, u32[]{:S(2)}) collective-permute-start(bf16[256,128]{1,0:T(8,128)(2,1)S(1)} %get-tuple-element.42), channel_id=1, source_target_pairs={{0,14},{1,15},{2,12},{3,13},{4,10},{5,11},{6,8},{7,9},{8,6},{9,7},... | collective-permute-start | bytes 196616 | tf_op jit(solution)/shard_map/ppermute | solution.py:310
  22.2 9.5 %collective-permute-start.8 = (bf16[256,128]{1,0:T(8,128)(2,1)S(1)}, bf16[256,128]{1,0:T(8,128)(2,1)S(1)}, u32[]{:S(2)}, u32[]{:S(2)}) collective-permute-start(bf16[256,128]{1,0:T(8,128)(2,1)S(1)} %get-tuple-element.37), channel_id=1, source_target_pairs={{0,4},{1,13},{2,6},{3,15},{4,0},{5,9},{6,2},{7,11},{8,12},{9,5},{1... | collective-permute-start | bytes 196616 | tf_op jit(solution)/shard_map/ppermute | solution.py:310
  24.2 7.6 %collective-permute-start.9 = (bf16[256,128]{1,0:T(8,128)(2,1)S(1)}, bf16[256,128]{1,0:T(8,128)(2,1)S(1)}, u32[]{:S(2)}, u32[]{:S(2)}) collective-permute-start(bf16[256,128]{1,0:T(8,128)(2,1)S(1)} %get-tuple-element.38), channel_id=1, source_target_pairs={{0,12},{1,7},{2,14},{3,5},{4,8},{5,3},{6,10},{7,1},{8,4},{9,15},{1... | collective-permute-start | bytes 196616 | tf_op jit(solution)/shard_map/ppermute | solution.py:310
  26.4 5.4 %collective-permute-start.4 = (bf16[256,128]{1,0:T(8,128)(2,1)S(1)}, bf16[256,128]{1,0:T(8,128)(2,1)S(1)}, u32[]{:S(2)}, u32[]{:S(2)}) collective-permute-start(bf16[256,128]{1,0:T(8,128)(2,1)S(1)} %get-tuple-element.33), channel_id=1, source_target_pairs={{0,2},{1,9},{2,0},{3,11},{4,6},{5,13},{6,4},{7,15},{8,10},{9,1},{1... | collective-permute-start | bytes 196616 | tf_op jit(solution)/shard_map/ppermute | solution.py:310
  28.0 3.7 %copy-start = (bf16[4096]{0:T(1024)(128)(2,1)S(1)}, bf16[4096]{0:T(1024)(128)(2,1)}, u32[]{:S(2)}) copy-start(bf16[4096]{0:T(1024)(128)(2,1)} %param.19) | copy-start | bytes 24580
  28.9 6.1 %collective-permute-start.5 = (bf16[256,128]{1,0:T(8,128)(2,1)S(1)}, bf16[256,128]{1,0:T(8,128)(2,1)S(1)}, u32[]{:S(2)}, u32[]{:S(2)}) collective-permute-start(bf16[256,128]{1,0:T(8,128)(2,1)S(1)} %get-tuple-element.34), channel_id=1, source_target_pairs={{0,10},{1,5},{2,8},{3,7},{4,14},{5,1},{6,12},{7,3},{8,2},{9,13},{1... | collective-permute-start | bytes 196616 | tf_op jit(solution)/shard_map/ppermute | solution.py:310
  29.1 6.1 %collective-permute-start.1 = (bf16[256,128]{1,0:T(8,128)(2,1)S(1)}, bf16[256,128]{1,0:T(8,128)(2,1)S(1)}, u32[]{:S(2)}, u32[]{:S(2)}) collective-permute-start(bf16[256,128]{1,0:T(8,128)(2,1)S(1)} %get-tuple-element.30), channel_id=1, source_target_pairs={{0,8},{1,3},{2,10},{3,1},{4,12},{5,7},{6,14},{7,5},{8,0},{9,11},{1... | collective-permute-start | bytes 196616 | tf_op jit(solution)/shard_map/ppermute | solution.py:310
  35.7 1.2 %collective-permute-start.14 = (f32[1,32]{1,0:T(1,128)S(1)}, f32[1,32]{1,0:T(1,128)S(1)}, u32[]{:S(2)}, u32[]{:S(2)}) collective-permute-start(f32[1,32]{1,0:T(1,128)S(1)} %get-tuple-element.45), channel_id=1, source_target_pairs={{0,1},{1,0},{2,3},{3,2},{4,5},{5,4},{6,7},{7,6},{8,9},{9,8},{10,11... | collective-permute-start | bytes 392 | tf_op jit(solution)/shard_map/ppermute | solution.py:328

commit v6 on v5

--- a/solution.py
+++ b/solution.py
@@ -198,14 +198,19 @@
         answers[n][slot * heads : (slot + 1) * heads, :] = (numerator / denominators[i]).astype(bf16)
 
 
-def unpack_kernel(capacity, heads, rows, row_ref, probe_ref, *rest):
-    answers, (out_ref, reward_ref, gathered) = rest[:-3], rest[-3:]
-    for partner, answer in enumerate(answers):
+def gather_kernel(capacity, heads, turns, row_ref, *rest):
+    answers, gathered = rest[: len(turns)], rest[-1]
+    for turn, answer in zip(turns, answers):
         for slot in range(capacity):
-            row = row_ref[partner * capacity + slot]
+            row = row_ref[turn * capacity + slot]
             gathered[pl.ds(pl.multiple_of(row * heads, heads), heads), :] = answer[
                 slot * heads : (slot + 1) * heads, :
             ].astype(f32)
+
+
+def unpack_kernel(capacity, heads, rows, turns, row_ref, probe_ref, *rest):
+    answers, (_, out_ref, reward_ref, gathered) = rest[: len(turns)], rest[len(turns) :]
+    gather_kernel(capacity, heads, turns, row_ref, *answers, gathered)
     total = jnp.zeros((rows, HEAD_SIZE), f32)
     for head in range(heads):
         part = gathered[pl.ds(head, rows, stride=heads), :]
@@ -316,15 +321,31 @@
         for turn, answer in zip(group, serve([arrived[turn] for turn in group])):
             answers[turn] = swap(answer, turn) if turn < replicas - 1 else answer
 
-    attended, partial_reward = pl.pallas_call(
-        functools.partial(unpack_kernel, capacity, heads, rows),
-        out_shape=[pltpu.VMEM((rows, heads * HEAD_SIZE), bf16), pltpu.VMEM((1, rows), f32)],
-        in_specs=[smem] + [vmem] * (replicas + 1),
-        out_specs=[vmem] * 2,
-        scratch_shapes=[pltpu.VMEM(((rows + 1) * heads, HEAD_SIZE), f32)],
+    gathered = pltpu.VMEM(((rows + 1) * heads, HEAD_SIZE), f32)
+    last = [0, 1]
+    early = [turn for turn in range(replicas) if turn not in last]
+    rows_of_early = pl.pallas_call(
+        functools.partial(gather_kernel, capacity, heads, early),
+        out_shape=gathered,
+        in_specs=[smem] + [vmem] * len(early),
+        out_specs=vmem,
+        compiler_params=params,
+        name="gather",
+    )(slot_rows, *[in_vmem(answers[turn]) for turn in early])
+    attended, partial_reward, _ = pl.pallas_call(
+        functools.partial(unpack_kernel, capacity, heads, rows, last),
+        out_shape=[pltpu.VMEM((rows, heads * HEAD_SIZE), bf16), pltpu.VMEM((1, rows), f32), gathered],
+        in_specs=[smem] + [vmem] * (len(last) + 2),
+        out_specs=[vmem] * 3,
+        input_output_aliases={len(last) + 2: 2},
         compiler_params=params,
         name="unpack",
-    )(slot_rows, in_vmem(reward_probe.reshape(1, -1)), *[in_vmem(x) for x in answers])
+    )(
+        slot_rows,
+        in_vmem(reward_probe.reshape(1, -1)),
+        *[in_vmem(answers[turn]) for turn in last],
+        in_vmem(rows_of_early),
+    )
     other_half = lax.ppermute(partial_reward, "tensor", [(0, 1), (1, 0)])
     return attended, (partial_reward + other_half)[0]
 

time: 37.6 us -> 36.9 us (0.981)
  waiting for transfers between devices: 4.51 us -> 3.84 us
    ppermute x14, waiting for transfers between devices: 4.1 us -> 3.44 us  [swap(): return lax.ppermute(x, ('replica', 'tensor'), pairs)]
  transfers between devices with their start and end apart: 15 -> 15, of which waited for: 4 -> 5; matrix products, arithmetic and copies ran while one was open for 2% -> 2% of each run, Pallas kernels for 9% -> 9%
where the time goes in v6:
time: 36.9 us; the launch traced here: 36.7 us
  starting transfers between devices  24.7 us (67%)
  Pallas kernels  6.26 us (17%)
  waiting for transfers between devices  3.84 us (10%)
  between operations  0.74 us (2%)
  local copies, waits for them, and re-layouts  0.72 us (2%)
  other arithmetic  0.51 us (1%)
    ppermute x14, starting transfers between devices, swap(): return lax.ppermute(x, ('replica', 'tensor'), pairs)  24.6 us
    ppermute x14, waiting for transfers between devices, swap(): return lax.ppermute(x, ('replica', 'tensor'), pairs)  3.44 us
    pallas_call x4, Pallas kernels, serve(): pl.pallas_call(functools.partial(serve_kernel, capacity, heads), out_shap...  3.3 us
    pallas_call x1, Pallas kernels, shards(): pl.pallas_call(functools.partial(pack_kernel, capacity, turns), out_shape...  2.48 us
  transfers between devices with their start and end apart: 15, of which 5 were waited for; matrix products, arithmetic and copies ran while one was open for 2% of the time, Pallas kernels for 9%

profile of v6, /device:TPU:0, one launch (start us, length us, event | category | flops | bytes accessed | tf_op | source)
XLA Modules:
  0.0 36.7 jit_solution(2316875063391939889)
XLA Ops:
  0.6 2.5 %pack.1 = (bf16[304,128]{1,0:T(8,128)(2,1)S(1)}, bf16[304,128]{1,0:T(8,128)(2,1)S(1)}, bf16[304,128]{1,0:T(8,128)(2,1)S(1)}, bf16[304,128]{1,0:T(8,128)(2,1)S(1)...) custom-call(bf16[32,4096]{1,0:T(8,128)(2,1)} %q_hbm.1, ...), custom_call_target="tpu_custom_call" | custom-call | tf_op jit(solution)/shard_map/pack/pallas_call | solution.py:263
  3.1 4.0 %collective-permute-start.10 = (bf16[304,128]{1,0:T(8,128)(2,1)S(1)}, bf16[304,128]{1,0:T(8,128)(2,1)S(1)}, u32[]{:S(2)}, u32[]{:S(2)}) collective-permute-start(bf16[304,128]{1,0:T(8,128)(2,1)S(1)} %get-tuple-element.39), channel_id=1, source_target_pairs={{0,6},{1,11},{2,4},{3,9},{4,2},{5,15},{6,0},{7,13},{8,14},{9,3},{1... | collective-permute-start | bytes 233480 | tf_op jit(solution)/shard_map/ppermute | solution.py:315
  7.2 2.4 %collective-permute-start.11 = (bf16[304,128]{1,0:T(8,128)(2,1)S(1)}, bf16[304,128]{1,0:T(8,128)(2,1)S(1)}, u32[]{:S(2)}, u32[]{:S(2)}) collective-permute-start(bf16[304,128]{1,0:T(8,128)(2,1)S(1)} %get-tuple-element.40), channel_id=1, source_target_pairs={{0,14},{1,15},{2,12},{3,13},{4,10},{5,11},{6,8},{7,9},{8,6},{9,7},... | collective-permute-start | bytes 233480 | tf_op jit(solution)/shard_map/ppermute | solution.py:315
  9.6 0.7 %collective-permute-start.6 = (bf16[304,128]{1,0:T(8,128)(2,1)S(1)}, bf16[304,128]{1,0:T(8,128)(2,1)S(1)}, u32[]{:S(2)}, u32[]{:S(2)}) collective-permute-start(bf16[304,128]{1,0:T(8,128)(2,1)S(1)} %get-tuple-element.35), channel_id=1, source_target_pairs={{0,4},{1,13},{2,6},{3,15},{4,0},{5,9},{6,2},{7,11},{8,12},{9,5},{1... | collective-permute-start | bytes 233480 | tf_op jit(solution)/shard_map/ppermute | solution.py:315
  10.3 1.0 %collective-permute-start.7 = (bf16[304,128]{1,0:T(8,128)(2,1)S(1)}, bf16[304,128]{1,0:T(8,128)(2,1)S(1)}, u32[]{:S(2)}, u32[]{:S(2)}) collective-permute-start(bf16[304,128]{1,0:T(8,128)(2,1)S(1)} %get-tuple-element.36), channel_id=1, source_target_pairs={{0,12},{1,7},{2,14},{3,5},{4,8},{5,3},{6,10},{7,1},{8,4},{9,15},{1... | collective-permute-start | bytes 233480 | tf_op jit(solution)/shard_map/ppermute | solution.py:315
  11.2 1.2 %collective-permute-start.2 = (bf16[304,128]{1,0:T(8,128)(2,1)S(1)}, bf16[304,128]{1,0:T(8,128)(2,1)S(1)}, u32[]{:S(2)}, u32[]{:S(2)}) collective-permute-start(bf16[304,128]{1,0:T(8,128)(2,1)S(1)} %get-tuple-element.31), channel_id=1, source_target_pairs={{0,2},{1,9},{2,0},{3,11},{4,6},{5,13},{6,4},{7,15},{8,10},{9,1},{1... | collective-permute-start | bytes 233480 | tf_op jit(solution)/shard_map/ppermute | solution.py:315
  12.5 0.0 collective-permute-done.10.blocks_and_answers_0_
  12.5 2.1 %collective-permute-start.3 = (bf16[304,128]{1,0:T(8,128)(2,1)S(1)}, bf16[304,128]{1,0:T(8,128)(2,1)S(1)}, u32[]{:S(2)}, u32[]{:S(2)}) collective-permute-start(bf16[304,128]{1,0:T(8,128)(2,1)S(1)} %get-tuple-element.32), channel_id=1, source_target_pairs={{0,10},{1,5},{2,8},{3,7},{4,14},{5,1},{6,12},{7,3},{8,2},{9,13},{1... | collective-permute-start | bytes 233480 | tf_op jit(solution)/shard_map/ppermute | solution.py:315
  14.5 0.7 %collective-permute-done.11.blocks_and_answers_1_ = bf16[304,128]{1,0:T(8,128)(2,1)S(1)} collective-permute-done((bf16[304,128]{1,0:T(8,128)(2,1)S(1)}, bf16[304,128]{1,0:T(8,128)(2,1)S(1)}, u32[]{:S(2)}, u32[]{:S(2)}) %collective-permute-start.11) | collective-permute-done | bytes 77856 | tf_op jit(solution)/shard_map/ppermute | solution.py:315
  15.2 2.7 %collective-permute-start = (bf16[304,128]{1,0:T(8,128)(2,1)S(1)}, bf16[304,128]{1,0:T(8,128)(2,1)S(1)}, u32[]{:S(2)}, u32[]{:S(2)}) collective-permute-start(bf16[304,128]{1,0:T(8,128)(2,1)S(1)} %get-tuple-element.28), channel_id=1, source_target_pairs={{0,8},{1,3},{2,10},{3,1},{4,12},{5,7},{6,14},{7,5},{8,0},{9,11},{1... | collective-permute-start | bytes 233480 | tf_op jit(solution)/shard_map/ppermute | solution.py:315
  17.9 0.8 %serve.7 = (bf16[256,128]{1,0:T(8,128)(2,1)S(1)}, bf16[256,128]{1,0:T(8,128)(2,1)S(1)}) custom-call(s32[4,32]{1,0:T(4,128)S(4)} %get-tuple-element.25.table_ref, bf16[128,16,512]{2,1,0:T(8,128)(2,1)S(1)} %get-tuple-element.26.key_ref, bf16[128,16,512]{2,1,0:T(8,128)(2,1)S(1)} %get-tuple-element.27.value_ref, ...), custom_call_target="tpu_custom_call" | custom-call | flops 10000000 | bytes 2000000 | tf_op jit(solution)/shard_map/serve/pallas_call | solution.py:298
  18.7 0.0 collective-permute-done.6.blocks_and_answers_0_
  18.7 0.2 collective-permute-start.12
  18.9 0.0 collective-permute-done.7.blocks_and_answers_1_
  18.9 2.5 %collective-permute-start.13 = (bf16[256,128]{1,0:T(8,128)(2,1)S(1)}, bf16[256,128]{1,0:T(8,128)(2,1)S(1)}, u32[]{:S(2)}, u32[]{:S(2)}) collective-permute-start(bf16[256,128]{1,0:T(8,128)(2,1)S(1)} %get-tuple-element.42), channel_id=1, source_target_pairs={{0,14},{1,15},{2,12},{3,13},{4,10},{5,11},{6,8},{7,9},{8,6},{9,7},... | collective-permute-start | bytes 196616 | tf_op jit(solution)/shard_map/ppermute | solution.py:315
  21.4 0.8 %serve.6 = (bf16[256,128]{1,0:T(8,128)(2,1)S(1)}, bf16[256,128]{1,0:T(8,128)(2,1)S(1)}) custom-call(s32[4,32]{1,0:T(4,128)S(4)} %get-tuple-element.25.table_ref, bf16[128,16,512]{2,1,0:T(8,128)(2,1)S(1)} %get-tuple-element.26.key_ref, bf16[128,16,512]{2,1,0:T(8,128)(2,1)S(1)} %get-tuple-element.27.value_ref, ...), custom_call_target="tpu_custom_call" | custom-call | flops 10000000 | bytes 2000000 | tf_op jit(solution)/shard_map/serve/pallas_call | solution.py:298
  22.2 0.0 collective-permute-done.2.blocks_and_answers_0_
  22.2 2.0 %collective-permute-start.8 = (bf16[256,128]{1,0:T(8,128)(2,1)S(1)}, bf16[256,128]{1,0:T(8,128)(2,1)S(1)}, u32[]{:S(2)}, u32[]{:S(2)}) collective-permute-start(bf16[256,128]{1,0:T(8,128)(2,1)S(1)} %get-tuple-element.37), channel_id=1, source_target_pairs={{0,4},{1,13},{2,6},{3,15},{4,0},{5,9},{6,2},{7,11},{8,12},{9,5},{1... | collective-permute-start | bytes 196616 | tf_op jit(solution)/shard_map/ppermute | solution.py:315
  24.2 0.0 collective-permute-done.3.blocks_and_answers_1_
  24.2 1.4 %collective-permute-start.9 = (bf16[256,128]{1,0:T(8,128)(2,1)S(1)}, bf16[256,128]{1,0:T(8,128)(2,1)S(1)}, u32[]{:S(2)}, u32[]{:S(2)}) collective-permute-start(bf16[256,128]{1,0:T(8,128)(2,1)S(1)} %get-tuple-element.38), channel_id=1, source_target_pairs={{0,12},{1,7},{2,14},{3,5},{4,8},{5,3},{6,10},{7,1},{8,4},{9,15},{1... | collective-permute-start | bytes 196616 | tf_op jit(solution)/shard_map/ppermute | solution.py:315
  25.6 0.8 %serve.5 = (bf16[256,128]{1,0:T(8,128)(2,1)S(1)}, bf16[256,128]{1,0:T(8,128)(2,1)S(1)}) custom-call(s32[4,32]{1,0:T(4,128)S(4)} %get-tuple-element.25.table_ref, bf16[128,16,512]{2,1,0:T(8,128)(2,1)S(1)} %get-tuple-element.26.key_ref, bf16[128,16,512]{2,1,0:T(8,128)(2,1)S(1)} %get-tuple-element.27.value_ref, ...), custom_call_target="tpu_custom_call" | custom-call | flops 10000000 | bytes 2000000 | tf_op jit(solution)/shard_map/serve/pallas_call | solution.py:298
  26.4 0.0 collective-permute-done.blocks_and_answers_0_
  26.4 1.2 %collective-permute-start.5 = (bf16[256,128]{1,0:T(8,128)(2,1)S(1)}, bf16[256,128]{1,0:T(8,128)(2,1)S(1)}, u32[]{:S(2)}, u32[]{:S(2)}) collective-permute-start(bf16[256,128]{1,0:T(8,128)(2,1)S(1)} %get-tuple-element.34), channel_id=1, source_target_pairs={{0,10},{1,5},{2,8},{3,7},{4,14},{5,1},{6,12},{7,3},{8,2},{9,13},{1... | collective-permute-start | bytes 196616 | tf_op jit(solution)/shard_map/ppermute | solution.py:315
  27.6 0.0 copy-start
  27.6 0.8 %serve.4 = (bf16[256,128]{1,0:T(8,128)(2,1)S(1)}, bf16[256,128]{1,0:T(8,128)(2,1)S(1)}) custom-call(s32[4,32]{1,0:T(4,128)S(4)} %get-tuple-element.25.table_ref, bf16[128,16,512]{2,1,0:T(8,128)(2,1)S(1)} %get-tuple-element.26.key_ref, bf16[128,16,512]{2,1,0:T(8,128)(2,1)S(1)} %get-tuple-element.27.value_ref, ...), custom_call_target="tpu_custom_call" | custom-call | flops 10000000 | bytes 2000000 | tf_op jit(solution)/shard_map/serve/pallas_call | solution.py:298
  28.4 0.0 collective-permute-done.12.rest_3_
  28.4 0.7 %collective-permute-start.4 = (bf16[256,128]{1,0:T(8,128)(2,1)S(1)}, bf16[256,128]{1,0:T(8,128)(2,1)S(1)}, u32[]{:S(2)}, u32[]{:S(2)}) collective-permute-start(bf16[256,128]{1,0:T(8,128)(2,1)S(1)} %get-tuple-element.33), channel_id=1, source_target_pairs={{0,2},{1,9},{2,0},{3,11},{4,6},{5,13},{6,4},{7,15},{8,10},{9,1},{1... | collective-permute-start | bytes 196616 | tf_op jit(solution)/shard_map/ppermute | solution.py:315
  29.1 0.0 collective-permute-done.13.rest_4_
  29.1 2.7 %collective-permute-start.1 = (bf16[256,128]{1,0:T(8,128)(2,1)S(1)}, bf16[256,128]{1,0:T(8,128)(2,1)S(1)}, u32[]{:S(2)}, u32[]{:S(2)}) collective-permute-start(bf16[256,128]{1,0:T(8,128)(2,1)S(1)} %get-tuple-element.30), channel_id=1, source_target_pairs={{0,8},{1,3},{2,10},{3,1},{4,12},{5,7},{6,14},{7,5},{8,0},{9,11},{1... | collective-permute-start | bytes 196616 | tf_op jit(solution)/shard_map/ppermute | solution.py:315
  31.8 0.0 copy-done
  31.8 0.0 collective-permute-done.8.rest_1_
  31.8 0.0 collective-permute-done.9.rest_2_
  31.8 1.3 %collective-permute-done.5.rest_0_ = bf16[256,128]{1,0:T(8,128)(2,1)S(1)} collective-permute-done((bf16[256,128]{1,0:T(8,128)(2,1)S(1)}, bf16[256,128]{1,0:T(8,128)(2,1)S(1)}, u32[]{:S(2)}, u32[]{:S(2)}) %collective-permute-start.5) | collective-permute-done | bytes 65568 | tf_op jit(solution)/shard_map/ppermute | solution.py:315
  33.1 0.1 gather.1.rest_2_
  33.2 0.8 %collective-permute-done.4.rest_1_ = bf16[256,128]{1,0:T(8,128)(2,1)S(1)} collective-permute-done((bf16[256,128]{1,0:T(8,128)(2,1)S(1)}, bf16[256,128]{1,0:T(8,128)(2,1)S(1)}, u32[]{:S(2)}, u32[]{:S(2)}) %collective-permute-start.4) | collective-permute-done | bytes 65568 | tf_op jit(solution)/shard_map/ppermute | solution.py:315
  34.0 0.6 %collective-permute-done.1.rest_0_ = bf16[256,128]{1,0:T(8,128)(2,1)S(1)} collective-permute-done((bf16[256,128]{1,0:T(8,128)(2,1)S(1)}, bf16[256,128]{1,0:T(8,128)(2,1)S(1)}, u32[]{:S(2)}, u32[]{:S(2)}) %collective-permute-start.1) | collective-permute-done | bytes 65568 | tf_op jit(solution)/shard_map/ppermute | solution.py:315
  34.6 0.4 %unpack.1 = (bf16[32,4096]{1,0:T(8,128)(2,1)S(1)}, f32[1,32]{1,0:T(1,128)S(1)}, f32[1056,128]{1,0:T(8,128)S(1)}) custom-call(s32[64]{0:T(128)S(4)} %get-tuple-element.24.row_ref, bf16[1,4096]{1,0:T(2,128)(2,1)S(1)} %reshape.15.probe_ref, bf16[256,128]{1,0:T(8,128)(2,1)S(1)} %collective-permute-done.1.rest_0_, ...), custom_call_target="tpu_custom_call", output_to_operand_aliasing={{2}: (4, {})} | custom-call | tf_op jit(solution)/shard_map/unpack/pallas_call | solution.py:335
  35.0 0.1 collective-permute-start.14
  35.1 0.7 %copy.14 = bf16[32,4096]{1,0:T(8,128)(2,1)} copy(bf16[32,4096]{1,0:T(8,128)(2,1)S(1)} %get-tuple-element.46) | data formatting | bytes 524288
  35.8 0.4 %collective-permute-done.14 = f32[1,32]{1,0:T(1,128)S(1)} collective-permute-done((f32[1,32]{1,0:T(1,128)S(1)}, f32[1,32]{1,0:T(1,128)S(1)}, u32[]{:S(2)}, u32[]{:S(2)}) %collective-permute-start.14) | collective-permute-done | bytes 160 | tf_op jit(solution)/shard_map/ppermute | solution.py:349
  36.2 0.5 %add_bitcast_fusion = f32[32]{0:T(128)} fusion(f32[1,32]{1,0:T(1,128)S(1)} %get-tuple-element.45, f32[1,32]{1,0:T(1,128)S(1)} %collective-permute-done.14), kind=kLoop, calls=%fused_computation | loop fusion | flops 32 | bytes 384 | tf_op jit(solution)/shard_map/squeeze | solution.py:350
  (1 shorter events, 0.0 us)
Async XLA Ops:
  3.1 9.3 %collective-permute-start.10 = (bf16[304,128]{1,0:T(8,128)(2,1)S(1)}, bf16[304,128]{1,0:T(8,128)(2,1)S(1)}, u32[]{:S(2)}, u32[]{:S(2)}) collective-permute-start(bf16[304,128]{1,0:T(8,128)(2,1)S(1)} %get-tuple-element.39), channel_id=1, source_target_pairs={{0,6},{1,11},{2,4},{3,9},{4,2},{5,15},{6,0},{7,13},{8,14},{9,3},{1... | collective-permute-start | bytes 233480 | tf_op jit(solution)/shard_map/ppermute | solution.py:315
  7.2 8.0 %collective-permute-start.11 = (bf16[304,128]{1,0:T(8,128)(2,1)S(1)}, bf16[304,128]{1,0:T(8,128)(2,1)S(1)}, u32[]{:S(2)}, u32[]{:S(2)}) collective-permute-start(bf16[304,128]{1,0:T(8,128)(2,1)S(1)} %get-tuple-element.40), channel_id=1, source_target_pairs={{0,14},{1,15},{2,12},{3,13},{4,10},{5,11},{6,8},{7,9},{8,6},{9,7},... | collective-permute-start | bytes 233480 | tf_op jit(solution)/shard_map/ppermute | solution.py:315
  9.6 9.1 %collective-permute-start.6 = (bf16[304,128]{1,0:T(8,128)(2,1)S(1)}, bf16[304,128]{1,0:T(8,128)(2,1)S(1)}, u32[]{:S(2)}, u32[]{:S(2)}) collective-permute-start(bf16[304,128]{1,0:T(8,128)(2,1)S(1)} %get-tuple-element.35), channel_id=1, source_target_pairs={{0,4},{1,13},{2,6},{3,15},{4,0},{5,9},{6,2},{7,11},{8,12},{9,5},{1... | collective-permute-start | bytes 233480 | tf_op jit(solution)/shard_map/ppermute | solution.py:315
  10.3 8.6 %collective-permute-start.7 = (bf16[304,128]{1,0:T(8,128)(2,1)S(1)}, bf16[304,128]{1,0:T(8,128)(2,1)S(1)}, u32[]{:S(2)}, u32[]{:S(2)}) collective-permute-start(bf16[304,128]{1,0:T(8,128)(2,1)S(1)} %get-tuple-element.36), channel_id=1, source_target_pairs={{0,12},{1,7},{2,14},{3,5},{4,8},{5,3},{6,10},{7,1},{8,4},{9,15},{1... | collective-permute-start | bytes 233480 | tf_op jit(solution)/shard_map/ppermute | solution.py:315
  11.2 11.0 %collective-permute-start.2 = (bf16[304,128]{1,0:T(8,128)(2,1)S(1)}, bf16[304,128]{1,0:T(8,128)(2,1)S(1)}, u32[]{:S(2)}, u32[]{:S(2)}) collective-permute-start(bf16[304,128]{1,0:T(8,128)(2,1)S(1)} %get-tuple-element.31), channel_id=1, source_target_pairs={{0,2},{1,9},{2,0},{3,11},{4,6},{5,13},{6,4},{7,15},{8,10},{9,1},{1... | collective-permute-start | bytes 233480 | tf_op jit(solution)/shard_map/ppermute | solution.py:315
  12.5 11.7 %collective-permute-start.3 = (bf16[304,128]{1,0:T(8,128)(2,1)S(1)}, bf16[304,128]{1,0:T(8,128)(2,1)S(1)}, u32[]{:S(2)}, u32[]{:S(2)}) collective-permute-start(bf16[304,128]{1,0:T(8,128)(2,1)S(1)} %get-tuple-element.32), channel_id=1, source_target_pairs={{0,10},{1,5},{2,8},{3,7},{4,14},{5,1},{6,12},{7,3},{8,2},{9,13},{1... | collective-permute-start | bytes 233480 | tf_op jit(solution)/shard_map/ppermute | solution.py:315
  15.2 11.2 %collective-permute-start = (bf16[304,128]{1,0:T(8,128)(2,1)S(1)}, bf16[304,128]{1,0:T(8,128)(2,1)S(1)}, u32[]{:S(2)}, u32[]{:S(2)}) collective-permute-start(bf16[304,128]{1,0:T(8,128)(2,1)S(1)} %get-tuple-element.28), channel_id=1, source_target_pairs={{0,8},{1,3},{2,10},{3,1},{4,12},{5,7},{6,14},{7,5},{8,0},{9,11},{1... | collective-permute-start | bytes 233480 | tf_op jit(solution)/shard_map/ppermute | solution.py:315
  18.7 9.7 %collective-permute-start.12 = (bf16[256,128]{1,0:T(8,128)(2,1)S(1)}, bf16[256,128]{1,0:T(8,128)(2,1)S(1)}, u32[]{:S(2)}, u32[]{:S(2)}) collective-permute-start(bf16[256,128]{1,0:T(8,128)(2,1)S(1)} %get-tuple-element.41), channel_id=1, source_target_pairs={{0,6},{1,11},{2,4},{3,9},{4,2},{5,15},{6,0},{7,13},{8,14},{9,3},{1... | collective-permute-start | bytes 196616 | tf_op jit(solution)/shard_map/ppermute | solution.py:315
  18.9 10.2 %collective-permute-start.13 = (bf16[256,128]{1,0:T(8,128)(2,1)S(1)}, bf16[256,128]{1,0:T(8,128)(2,1)S(1)}, u32[]{:S(2)}, u32[]{:S(2)}) collective-permute-start(bf16[256,128]{1,0:T(8,128)(2,1)S(1)} %get-tuple-element.42), channel_id=1, source_target_pairs={{0,14},{1,15},{2,12},{3,13},{4,10},{5,11},{6,8},{7,9},{8,6},{9,7},... | collective-permute-start | bytes 196616 | tf_op jit(solution)/shard_map/ppermute | solution.py:315
  22.2 9.5 %collective-permute-start.8 = (bf16[256,128]{1,0:T(8,128)(2,1)S(1)}, bf16[256,128]{1,0:T(8,128)(2,1)S(1)}, u32[]{:S(2)}, u32[]{:S(2)}) collective-permute-start(bf16[256,128]{1,0:T(8,128)(2,1)S(1)} %get-tuple-element.37), channel_id=1, source_target_pairs={{0,4},{1,13},{2,6},{3,15},{4,0},{5,9},{6,2},{7,11},{8,12},{9,5},{1... | collective-permute-start | bytes 196616 | tf_op jit(solution)/shard_map/ppermute | solution.py:315
  24.2 7.6 %collective-permute-start.9 = (bf16[256,128]{1,0:T(8,128)(2,1)S(1)}, bf16[256,128]{1,0:T(8,128)(2,1)S(1)}, u32[]{:S(2)}, u32[]{:S(2)}) collective-permute-start(bf16[256,128]{1,0:T(8,128)(2,1)S(1)} %get-tuple-element.38), channel_id=1, source_target_pairs={{0,12},{1,7},{2,14},{3,5},{4,8},{5,3},{6,10},{7,1},{8,4},{9,15},{1... | collective-permute-start | bytes 196616 | tf_op jit(solution)/shard_map/ppermute | solution.py:315
  26.4 6.7 %collective-permute-start.5 = (bf16[256,128]{1,0:T(8,128)(2,1)S(1)}, bf16[256,128]{1,0:T(8,128)(2,1)S(1)}, u32[]{:S(2)}, u32[]{:S(2)}) collective-permute-start(bf16[256,128]{1,0:T(8,128)(2,1)S(1)} %get-tuple-element.34), channel_id=1, source_target_pairs={{0,10},{1,5},{2,8},{3,7},{4,14},{5,1},{6,12},{7,3},{8,2},{9,13},{1... | collective-permute-start | bytes 196616 | tf_op jit(solution)/shard_map/ppermute | solution.py:315
  27.6 4.2 %copy-start = (bf16[4096]{0:T(1024)(128)(2,1)S(1)}, bf16[4096]{0:T(1024)(128)(2,1)}, u32[]{:S(2)}) copy-start(bf16[4096]{0:T(1024)(128)(2,1)} %param.19) | copy-start | bytes 24580
  28.4 5.6 %collective-permute-start.4 = (bf16[256,128]{1,0:T(8,128)(2,1)S(1)}, bf16[256,128]{1,0:T(8,128)(2,1)S(1)}, u32[]{:S(2)}, u32[]{:S(2)}) collective-permute-start(bf16[256,128]{1,0:T(8,128)(2,1)S(1)} %get-tuple-element.33), channel_id=1, source_target_pairs={{0,2},{1,9},{2,0},{3,11},{4,6},{5,13},{6,4},{7,15},{8,10},{9,1},{1... | collective-permute-start | bytes 196616 | tf_op jit(solution)/shard_map/ppermute | solution.py:315
  29.1 5.5 %collective-permute-start.1 = (bf16[256,128]{1,0:T(8,128)(2,1)S(1)}, bf16[256,128]{1,0:T(8,128)(2,1)S(1)}, u32[]{:S(2)}, u32[]{:S(2)}) collective-permute-start(bf16[256,128]{1,0:T(8,128)(2,1)S(1)} %get-tuple-element.30), channel_id=1, source_target_pairs={{0,8},{1,3},{2,10},{3,1},{4,12},{5,7},{6,14},{7,5},{8,0},{9,11},{1... | collective-permute-start | bytes 196616 | tf_op jit(solution)/shard_map/ppermute | solution.py:315
  35.0 1.2 %collective-permute-start.14 = (f32[1,32]{1,0:T(1,128)S(1)}, f32[1,32]{1,0:T(1,128)S(1)}, u32[]{:S(2)}, u32[]{:S(2)}) collective-permute-start(f32[1,32]{1,0:T(1,128)S(1)} %get-tuple-element.45), channel_id=1, source_target_pairs={{0,1},{1,0},{2,3},{3,2},{4,5},{5,4},{6,7},{7,6},{8,9},{9,8},{10,11... | collective-permute-start | bytes 392 | tf_op jit(solution)/shard_map/ppermute | solution.py:349
